TPU v7x, 32 devices: a whole 2x2x4 slice. The times are simulated.
32 devices in a mesh: groups: 2 (over y), mz: 4 (over z), pix: 4 (over x, core).
Axes of the slice: x: 2, y: 2, z: 4, core: 2. Of those that a mesh axis runs over, the one named last changes fastest.
Arguments:
- spectra: bfloat16 [1024, 262144], P(('groups', 'pix'), 'mz'), parts along dimension 0
- kernel: bfloat16 [129], replicated, may hold values from 0.0009994507 to 0.029907227
- probes: bfloat16 [262144, 128], P('mz'), may hold values from -0.01171875 to 0.01171875
Outputs:
- basis: bfloat16 [1024, 128], P(('groups', 'pix')), parts along dimension 0
- projected: bfloat16 [256, 262144], P(('groups', 'pix'), 'mz'), parts along dimension 0
There are 2 independent parts, one for each index of `groups`. A program takes and returns all parts, laid end to end along the dimension named above; an argument that names none is the same for every part. Nothing has to cross between parts.
All inputs are finite; a program needn't handle non-finite values.
Results may differ from a plain program's by a relative error of at most 0.019.
Values may be sent and summed in bfloat16 or wider, within the bound.
No kernel may reach another device: no remote copies, remote signals or barrier semaphores. Data moves between devices by JAX's collectives and lax.ppermute only.
A program may use at most 192 MiB of HBM per device.

v0:
```python
import functools
import math

import jax
import jax.numpy as jnp
from jax import lax
from jax.experimental import pallas as pl
from jax.experimental.pallas import tpu as pltpu
from jax.sharding import PartitionSpec as P

F32 = jnp.float32
BF16 = jnp.bfloat16
HIGHEST = lax.Precision.HIGHEST
TILE = 128
WIDTH = 256
REACH = 64
VMEM = pl.BlockSpec(memory_space=pltpu.VMEM)


def params(limit=56):
    return pltpu.CompilerParams(vmem_limit_bytes=limit * 2**20)


def partner(x, axis, shift):
    count = lax.axis_size(axis)
    return lax.ppermute(x, axis, [(i, i ^ shift) for i in range(count)])


def spread(x, axis):
    count = lax.axis_size(axis)
    if count & (count - 1):
        return [lax.psum(x, axis)]
    shift = count // 2
    while shift >= 4:
        x = x + partner(x, axis, shift)
        shift //= 2
    return [x] + [partner(x, axis, s) for s in range(1, min(count, 4))]


def pairwise(parts):
    while len(parts) > 1:
        parts = [a + b for a, b in zip(parts[::2], parts[1::2])]
    return parts[0]


def band_of(taps):
    wide = jnp.broadcast_to(taps, (WIDTH, 2 * WIDTH))
    return pltpu.roll(wide, 0, 1, stride=1, stride_axis=0).T.astype(BF16)


def clean(before, block, after, band):
    ext = jnp.concatenate([before, block, after], axis=1)
    rows, bins = block.shape
    starts = range(0, bins, WIDTH)
    lhs = jnp.concatenate([ext[:, a : a + 2 * WIDTH] for a in starts], axis=0)
    base = jnp.dot(lhs, band, preferred_element_type=F32)
    mid = jnp.concatenate([block[:, a : a + WIDTH] for a in starts], axis=0)
    out = (mid.astype(F32) - base).astype(BF16)
    return jnp.concatenate([out[i * rows : (i + 1) * rows] for i in range(bins // WIDTH)], axis=1)


def sketch_kernel(steps, taps, block, prev, after, low, high, probes, sketch, band):
    i = pl.program_id(0)

    @pl.when(i == 0)
    def _():
        band[...] = band_of(taps[...])
        sketch[...] = jnp.zeros_like(sketch)

    cleaned = clean(
        jnp.where(i == 0, low[...], prev[...]),
        block[...],
        jnp.where(i == steps - 1, high[...], after[...]),
        band[...],
    )
    sketch[...] += jnp.dot(cleaned, probes[...], preferred_element_type=F32)


ANY = pl.BlockSpec(memory_space=pl.ANY)


def whole(shape):
    return pl.BlockSpec(shape, lambda i: (0, 0))


def block_specs(rows, size, first, last):
    per = size // TILE
    return [
        pl.BlockSpec((rows, size), lambda i: (0, first + i)),
        pl.BlockSpec((rows, TILE), lambda i: (0, jnp.maximum((first + i) * per - 1, 0))),
        pl.BlockSpec((rows, TILE), lambda i: (0, jnp.minimum((first + i + 1) * per, last))),
    ]


def sketch_of(taps, spectra, low, high, probes):
    rows, bins = spectra.shape
    size = math.gcd(bins, 8192)
    steps = bins // size
    columns = probes.shape[1]
    return pl.pallas_call(
        functools.partial(sketch_kernel, steps),
        grid=(steps,),
        in_specs=[whole(taps.shape)]
        + block_specs(rows, size, 0, bins // TILE - 1)
        + [whole(low.shape), whole(high.shape)]
        + [pl.BlockSpec((size, columns), lambda i: (i, 0))],
        out_specs=[whole((rows, columns)), whole((2 * WIDTH, WIDTH))],
        out_shape=[
            jax.ShapeDtypeStruct((rows, columns), F32),
            jax.ShapeDtypeStruct((2 * WIDTH, WIDTH), BF16),
        ],
        compiler_params=params(),
    )(taps, spectra, spectra, spectra, low, high, probes)


def gram_kernel(*refs):
    parts, sketch, gram = refs[:-2], refs[-2], refs[-1]
    total = pairwise([part[...] for part in parts])
    sketch[...] = total
    gram[...] = lax.dot_general(
        total, total, (((0,), (0,)), ((), ())), precision=HIGHEST, preferred_element_type=F32
    )


def gram_of(parts):
    shape = parts[0].shape
    return pl.pallas_call(
        gram_kernel,
        in_specs=[VMEM] * len(parts),
        out_specs=[VMEM] * 2,
        out_shape=[
            jax.ShapeDtypeStruct(shape, F32),
            jax.ShapeDtypeStruct((shape[1], shape[1]), F32),
        ],
        compiler_params=params(32),
    )(*parts)


def inverse_factor(gram):
    size = gram.shape[0]
    groups = range(size // 8)
    rows = [gram[8 * g : 8 * g + 8] for g in groups]
    lane = lax.broadcasted_iota(jnp.int32, (8, size), 1)
    sub = lax.broadcasted_iota(jnp.int32, (8, size), 0)

    def row_of(x, k):
        return jnp.broadcast_to(x[k : k + 1], (8, size))

    result = []
    for g in groups:
        inside = (lane >= 8 * g) & (lane < 8 * g + 8)
        below = groups[g:]
        cols = {
            h: [
                jnp.broadcast_to(rows[h][:, 8 * g + k : 8 * g + k + 1], (8, size))
                for k in range(8)
            ]
            for h in below
        }
        for h in below:
            unit = jnp.where(lane - 8 * g == sub, 1.0, 0.0) if h == g else 0.0
            rows[h] = jnp.where(inside, unit, rows[h])
        pivots = jnp.ones((8, size), F32)
        for k in range(8):
            pivot = row_of(cols[g][k], k)
            scale = 1.0 / pivot
            pivots = jnp.where(sub == k, pivot, pivots)
            line = row_of(rows[g], k) * scale
            heads = {m: row_of(cols[g][m], k) * scale for m in range(k + 1, 8)}
            for h in below:
                c = cols[h][k]
                if h == g:
                    c = jnp.where(sub > k, c, 0.0)
                rows[h] = rows[h] - c * line
                for m in range(k + 1, 8):
                    cols[h][m] = cols[h][m] - c * heads[m]
        result.append(jnp.where(lane < 8 * g + 8, rows[g] * lax.rsqrt(pivots), 0.0))
    return jnp.concatenate(result, axis=0)


def basis_kernel(pixels, chips, *refs):
    parts, sketch, basis, turned = refs[:-3], refs[-3], refs[-2], refs[-1]
    gram = pairwise([part[...] for part in parts]) / float(pixels)
    inverse = inverse_factor(gram)
    size = gram.shape[0]
    across = lax.dot_general(
        inverse, sketch[...], (((1,), (1,)), ((), ())), precision=HIGHEST,
        preferred_element_type=F32,
    )
    basis[...] = across.T.astype(BF16)
    share = size // (2 * chips)
    me = lax.axis_index("pix")
    to = lax.broadcasted_iota(jnp.int32, (size, size), 0)
    source = lax.broadcasted_iota(jnp.int32, (size, size), 1)
    block = to // share
    other = block // chips
    chip = lax.rem(lax.rem(block, chips) + me // 2, chips)
    core = jnp.where(other == 1, 1 - lax.rem(me, 2), lax.rem(me, 2))
    wanted = (2 * chip + core) * share + lax.rem(to, share)
    pick = jnp.where(wanted == source, 1.0, 0.0).astype(BF16)
    turned[...] = jnp.dot(pick, across.astype(BF16), preferred_element_type=F32).astype(BF16)


def basis_of(parts, sketch, pixels, chips):
    rows, size = sketch.shape
    return pl.pallas_call(
        functools.partial(basis_kernel, pixels, chips),
        in_specs=[VMEM] * (len(parts) + 1),
        out_specs=[VMEM] * 2,
        out_shape=[
            jax.ShapeDtypeStruct((rows, size), BF16),
            jax.ShapeDtypeStruct((size, rows), BF16),
        ],
        compiler_params=params(32),
    )(*parts, sketch)


def project_kernel(first, last, factor, *refs):
    turned, band, block, prev, after, low, high = refs[:7]
    keep, give = refs[-2:]
    i = first + pl.program_id(0)
    cleaned = clean(
        jnp.where(i == 0, low[...], prev[...]),
        block[...],
        jnp.where(i == last, high[...], after[...]),
        band[...],
    )
    part = jnp.dot(turned[...], cleaned, preferred_element_type=F32) * factor
    half = keep.shape[0]
    keep[...] = part[:half].astype(BF16)
    give[...] = part[half:].astype(BF16)


def project(turned, band, spectra, low, high, start, count, factor, wait):
    rows, bins = spectra.shape
    size = math.gcd(math.gcd(start, count), 4096)
    first = start // size
    half = turned.shape[0] // 2
    out = pl.BlockSpec((half, size), lambda i: (0, i))
    shape = jax.ShapeDtypeStruct((half, count), BF16)
    return pl.pallas_call(
        functools.partial(project_kernel, first, bins // size - 1, factor),
        grid=(count // size,),
        in_specs=[whole(turned.shape), whole(band.shape)]
        + block_specs(rows, size, first, bins // TILE - 1)
        + [whole(low.shape), whole(high.shape)]
        + [ANY] * len(wait),
        out_specs=[out, out],
        out_shape=[shape, shape],
        compiler_params=params(50),
    )(turned, band, spectra, spectra, spectra, low, high, *wait)


def merge_kernel(share, chips, keep, got, *refs):
    outs = refs[-chips:]
    total = (keep[...].astype(F32) + got[...].astype(F32)).astype(BF16)
    for k, out in enumerate(outs):
        out[...] = total[k * share : (k + 1) * share]


def merge(keep, got, chips, wait):
    half, count = keep.shape
    share = half // chips
    size = math.gcd(count, 8192)
    return pl.pallas_call(
        functools.partial(merge_kernel, share, chips),
        grid=(count // size,),
        in_specs=[pl.BlockSpec((half, size), lambda i: (0, i))] * 2 + [ANY] * len(wait),
        out_specs=[pl.BlockSpec((share, size), lambda i: (0, i))] * chips,
        out_shape=[jax.ShapeDtypeStruct((share, count), BF16)] * chips,
        compiler_params=params(32),
    )(keep, got, *wait)


def finish_kernel(count, *refs):
    parts, out, done = refs[:count], refs[-2], refs[-1]
    done[...] = jnp.zeros_like(done)
    total = parts[0][...].astype(F32)
    for part in parts[1:]:
        total = total + part[...].astype(F32)
    out[...] = total.astype(BF16)


def finish(out, parts, start, bins, wait):
    share, count = parts[0].shape
    size = math.gcd(math.gcd(count, start), 8192)
    first = start // size
    place = pl.BlockSpec((share, size), lambda i: (0, first + i))
    extra = [] if out is None else [out]
    return pl.pallas_call(
        functools.partial(finish_kernel, len(parts)),
        grid=(count // size,),
        in_specs=[pl.BlockSpec((share, size), lambda i: (0, i))] * len(parts)
        + [ANY] * (len(extra) + len(wait)),
        out_specs=[place, whole((8, TILE))],
        out_shape=[
            jax.ShapeDtypeStruct((share, bins), BF16),
            jax.ShapeDtypeStruct((8, TILE), F32),
        ],
        input_output_aliases={len(parts): 0} if extra else {},
        compiler_params=params(32),
    )(*parts, *extra, *wait)


def chunks_of(bins):
    sizes = []
    left = bins
    for size in (2048, 6144):
        if left > size:
            sizes.append(size)
            left -= size
    while left > 0:
        size = min(8192, left)
        sizes.append(size)
        left -= size
    return sizes


def per_device(spectra, kernel, probes):
    rows, bins = spectra.shape
    pix = lax.axis_size("pix")
    depth = lax.axis_size("mz")
    chips = pix // 2
    pixels = rows * pix
    factor = 1.0 / math.sqrt(float(pixels))

    up = [(i, i + 1) for i in range(depth - 1)]
    down = [(i + 1, i) for i in range(depth - 1)]
    low = lax.ppermute(spectra[:, bins - TILE :], "mz", up)
    high = lax.ppermute(spectra[:, :TILE], "mz", down)
    taps = jnp.pad(kernel.astype(F32), (REACH, 2 * WIDTH - REACH - kernel.shape[0]))[None]

    partial_sketch, band = sketch_of(taps, spectra, low, high, probes)
    sketch, partial_gram = gram_of(spread(partial_sketch, "mz"))
    basis, turned = basis_of(spread(partial_gram, "pix"), sketch, pixels, chips)

    counts = chunks_of(bins)
    starts = [sum(counts[:k]) for k in range(len(counts))]
    routes = [
        [
            (2 * chip + core, 2 * ((chip + k) % chips) + core)
            for chip in range(chips)
            for core in range(2)
        ]
        for k in range(chips)
    ]

    def project_at(k, wait):
        return project(turned, band, spectra, low, high, starts[k], counts[k], factor, wait)

    out, sent = None, []
    ready = project_at(0, [])
    for k in range(len(counts)):
        keep, give = ready
        got = partner(give, "pix", 1)
        recent = [give]
        if k + 1 < len(counts):
            ready = project_at(k + 1, recent + [parts[0] for parts in sent[-1:]])
            recent = [ready[1]]
        if k >= 2:
            out, done = finish(out, sent[k - 2], starts[k - 2], bins, recent)
            recent = [done]
        mine = merge(keep, got, chips, recent)
        sent.append(
            [mine[0]] + [lax.ppermute(mine[m], "pix", routes[m]) for m in range(1, chips)]
        )
    for k in range(max(len(counts) - 2, 0), len(counts)):
        out, done = finish(out, sent[k], starts[k], bins, [])
    return (basis, out)


def solution(mesh):
    in_specs = (P(("groups", "pix"), "mz"), P(), P("mz", None))
    out_specs = (P(("groups", "pix"), None), P(("groups", "pix"), "mz"))
    return jax.shard_map(
        per_device, mesh=mesh, in_specs=in_specs, out_specs=out_specs, check_vma=False
    )
```

profile of v0, /device:TPU:0, one launch (start us, length us, event | category | flops | bytes accessed | tf_op | source)
XLA Modules:
  0.0 193.6 jit_solution(12968483176029219441)
XLA Ops:
  0.6 0.8 fusion
  1.4 1.3 collective-permute-start.1
  2.7 5.6 %collective-permute-start = (bf16[128,128]{1,0:T(8,128)(2,1)S(1)}, bf16[128,128]{1,0:T(8,128)(2,1)S(1)}, u32[]{:S(2)}, u32[]{:S(2)}) collective-permute-start(bf16[128,128]{1,0:T(8,128)(2,1)S(1)} %get-tuple-element.119), channel_id=1, source_target_pairs={{0,4},{4,8},{8,12},{1,5},{5,9},{9,13},{2,6},{6,10},{10,14},{3,7},{... | collective-permute-start | bytes 98312 | tf_op jit(solution)/shard_map/ppermute | solution.py:329
  8.3 1.3 pad_convert_fusion
  9.6 0.3 collective-permute-done.low.refs_5_
  9.8 0.3 copy-done.1
  10.2 0.3 copy-done.3
  10.5 19.7 %shard_map.50 = (f32[128,128]{1,0:T(8,128)}, bf16[512,256]{1,0:T(8,128)(2,1)}) custom-call(f32[1,512]{1,0:T(1,128)} %bitcast.1, bf16[128,65536]{1,0:T(8,128)(2,1)} %refs_4_.17, bf16[128,65536]{1,0:T(8,128)(2,1)} %refs_4_.17, bf16[128,65536]{1,0:T(8,128)(2,1)} %refs_4_.17, bf16[128,128]{1,0:T(8,128)(2,1)} %copy-done.3, bf16[128,128]{1,0:T(8,128)(2,1)} %copy-done.1, ...), custom_call_target="tpu_custom_call" | custom-call | tf_op jit(solution)/shard_map/pallas_call | solution.py:100
  30.1 4.8 %collective-permute-start.4 = (f32[128,128]{1,0:T(8,128)}, f32[128,128]{1,0:T(8,128)S(1)}, u32[]{:S(2)}, u32[]{:S(2)}) collective-permute-start(f32[128,128]{1,0:T(8,128)} %get-tuple-element.60.refs_0_), channel_id=1, source_target_pairs={{0,12},{4,8},{8,4},{12,0},{1,13},{5,9},{9,5},{13,1},{2,14},{6,10},... | collective-permute-start | bytes 196616 | tf_op jit(solution)/shard_map/ppermute | solution.py:26
  34.9 0.6 collective-permute-start.2
  35.6 1.8 collective-permute-done.4.refs_3_
  37.4 2.9 %collective-permute-done.3.refs_2_ = f32[128,128]{1,0:T(8,128)S(1)} collective-permute-done((f32[128,128]{1,0:T(8,128)}, f32[128,128]{1,0:T(8,128)S(1)}, u32[]{:S(2)}, u32[]{:S(2)}) %collective-permute-start.3) | collective-permute-done | bytes 65568 | tf_op jit(solution)/shard_map/ppermute | solution.py:26
  40.3 0.8 copy-done.5
  41.1 0.3 shard_map.51
  41.5 1.6 collective-permute-start.6
  43.0 0.3 collective-permute-start.5
  43.3 2.5 %collective-permute-done.7.refs_3_ = f32[128,128]{1,0:T(8,128)S(1)} collective-permute-done((f32[128,128]{1,0:T(8,128)S(1)}, f32[128,128]{1,0:T(8,128)S(1)}, u32[]{:S(2)}, u32[]{:S(2)}) %collective-permute-start.7) | collective-permute-done | bytes 65568 | tf_op jit(solution)/shard_map/ppermute | solution.py:26
  45.8 1.4 collective-permute-done.6.refs_2_
  47.3 5.0 %shard_map.52 = (bf16[128,128]{1,0:T(8,128)(2,1)}, bf16[128,128]{1,0:T(8,128)(2,1)S(1)}) custom-call(f32[128,128]{1,0:T(8,128)S(1)} %get-tuple-element.61.refs_0_, f32[128,128]{1,0:T(8,128)S(1)} %collective-permute-done.5.refs_1_, f32[128,128]{1,0:T(8,128)S(1)} %collective-permute-done.6.refs_2_, f32[128,128]{1,0:T(8,128)S(1)} %collective-permute-done.7.refs_3_, ...), custom_call_target="tpu_custom_call" | custom-call | tf_op jit(solution)/shard_map/pallas_call | solution.py:206
  52.3 0.9 copy-done
  53.2 0.8 copy-done.2
  54.0 0.8 copy-done.4
  54.7 1.8 shard_map.53
  56.7 3.7 %shard_map.54 = (bf16[64,6144]{1,0:T(8,128)(2,1)S(1)}, bf16[64,6144]{1,0:T(8,128)(2,1)S(1)}) custom-call(bf16[128,128]{1,0:T(8,128)(2,1)S(1)} %get-tuple-element.64.refs_0_, bf16[512,256]{1,0:T(8,128)(2,1)S(1)} %copy-done, bf16[128,65536]{1,0:T(8,128)(2,1)} %refs_4_.17, bf16[128,65536]{1,0:T(8,128)(2,1)} %refs_4_.17, bf16[128,65536]{1,0:T(8,128)(2,1)} %refs_4_.17, ...), custom_call_target="tpu_custom_call" | custom-call | tf_op jit(solution)/shard_map/pallas_call | solution.py:241
  60.4 3.7 %shard_map.56 = (bf16[64,8192]{1,0:T(8,128)(2,1)S(1)}, bf16[64,8192]{1,0:T(8,128)(2,1)S(1)}) custom-call(bf16[128,128]{1,0:T(8,128)(2,1)S(1)} %get-tuple-element.64.refs_0_, bf16[512,256]{1,0:T(8,128)(2,1)S(1)} %copy-done, bf16[128,65536]{1,0:T(8,128)(2,1)} %refs_4_.17, bf16[128,65536]{1,0:T(8,128)(2,1)} %refs_4_.17, bf16[128,65536]{1,0:T(8,128)(2,1)} %refs_4_.17, ...), custom_call_target="tpu_custom_call" | custom-call | tf_op jit(solution)/shard_map/pallas_call | solution.py:241
  64.2 0.5 collective-permute-start.10
  64.7 0.8 collective-permute-start.11
  65.5 2.6 %collective-permute-done.9.got = bf16[64,6144]{1,0:T(8,128)(2,1)S(1)} collective-permute-done((bf16[64,6144]{1,0:T(8,128)(2,1)S(1)}, bf16[64,6144]{1,0:T(8,128)(2,1)S(1)}, u32[]{:S(2)}, u32[]{:S(2)}) %collective-permute-start.9) | collective-permute-done | bytes 786464 | tf_op jit(solution)/shard_map/ppermute | solution.py:26
  68.1 0.4 shard_map.57
  68.5 3.7 %shard_map.58 = (bf16[64,8192]{1,0:T(8,128)(2,1)S(1)}, bf16[64,8192]{1,0:T(8,128)(2,1)S(1)}) custom-call(bf16[128,128]{1,0:T(8,128)(2,1)S(1)} %get-tuple-element.64.refs_0_, bf16[512,256]{1,0:T(8,128)(2,1)S(1)} %copy-done, bf16[128,65536]{1,0:T(8,128)(2,1)} %refs_4_.17, bf16[128,65536]{1,0:T(8,128)(2,1)} %refs_4_.17, bf16[128,65536]{1,0:T(8,128)(2,1)} %refs_4_.17, ...), custom_call_target="tpu_custom_call" | custom-call | tf_op jit(solution)/shard_map/pallas_call | solution.py:241
  72.2 0.4 collective-permute-start.12
  72.6 0.7 shard_map.59
  73.3 0.2 shard_map.60
  73.6 3.7 %shard_map.61 = (bf16[64,8192]{1,0:T(8,128)(2,1)S(1)}, bf16[64,8192]{1,0:T(8,128)(2,1)S(1)}) custom-call(bf16[128,128]{1,0:T(8,128)(2,1)S(1)} %get-tuple-element.64.refs_0_, bf16[512,256]{1,0:T(8,128)(2,1)S(1)} %copy-done, bf16[128,65536]{1,0:T(8,128)(2,1)} %refs_4_.17, bf16[128,65536]{1,0:T(8,128)(2,1)} %refs_4_.17, bf16[128,65536]{1,0:T(8,128)(2,1)} %refs_4_.17, ...), custom_call_target="tpu_custom_call" | custom-call | tf_op jit(solution)/shard_map/pallas_call | solution.py:241
  77.5 0.7 collective-permute-start.15
  78.2 1.3 collective-permute-start.13
  79.5 20.6 %collective-permute-done.13.refs_1_ = bf16[32,6144]{1,0:T(8,128)(2,1)S(1)} collective-permute-done((bf16[32,6144]{1,0:T(8,128)(2,1)S(1)}, bf16[32,6144]{1,0:T(8,128)(2,1)S(1)}, u32[]{:S(2)}, u32[]{:S(2)}) %collective-permute-start.13) | collective-permute-done | bytes 393248 | tf_op jit(solution)/shard_map/ppermute | solution.py:365
  100.1 1.4 shard_map.62
  101.6 0.2 shard_map.63
  101.8 3.7 %shard_map.64 = (bf16[64,8192]{1,0:T(8,128)(2,1)S(1)}, bf16[64,8192]{1,0:T(8,128)(2,1)S(1)}) custom-call(bf16[128,128]{1,0:T(8,128)(2,1)S(1)} %get-tuple-element.64.refs_0_, bf16[512,256]{1,0:T(8,128)(2,1)S(1)} %copy-done, bf16[128,65536]{1,0:T(8,128)(2,1)} %refs_4_.17, bf16[128,65536]{1,0:T(8,128)(2,1)} %refs_4_.17, bf16[128,65536]{1,0:T(8,128)(2,1)} %refs_4_.17, ...), custom_call_target="tpu_custom_call" | custom-call | tf_op jit(solution)/shard_map/pallas_call | solution.py:241
  105.6 0.9 shard_map.65
  106.5 0.2 shard_map.66
  106.8 3.7 %shard_map.67 = (bf16[64,8192]{1,0:T(8,128)(2,1)S(1)}, bf16[64,8192]{1,0:T(8,128)(2,1)S(1)}) custom-call(bf16[128,128]{1,0:T(8,128)(2,1)S(1)} %get-tuple-element.64.refs_0_, bf16[512,256]{1,0:T(8,128)(2,1)S(1)} %copy-done, bf16[128,65536]{1,0:T(8,128)(2,1)} %refs_4_.17, bf16[128,65536]{1,0:T(8,128)(2,1)} %refs_4_.17, bf16[128,65536]{1,0:T(8,128)(2,1)} %refs_4_.17, ...), custom_call_target="tpu_custom_call" | custom-call | tf_op jit(solution)/shard_map/pallas_call | solution.py:241
  110.5 0.6 collective-permute-start.18
  111.0 0.7 collective-permute-start.17
  111.7 1.3 collective-permute-start.19
  113.1 12.8 %collective-permute-done.17.refs_1_ = bf16[32,8192]{1,0:T(8,128)(2,1)S(1)} collective-permute-done((bf16[32,8192]{1,0:T(8,128)(2,1)S(1)}, bf16[32,8192]{1,0:T(8,128)(2,1)S(1)}, u32[]{:S(2)}, u32[]{:S(2)}) %collective-permute-start.17) | collective-permute-done | bytes 524320 | tf_op jit(solution)/shard_map/ppermute | solution.py:365
  125.8 0.9 shard_map.68
  127.0 3.7 %shard_map.70 = (bf16[64,8192]{1,0:T(8,128)(2,1)S(1)}, bf16[64,8192]{1,0:T(8,128)(2,1)S(1)}) custom-call(bf16[128,128]{1,0:T(8,128)(2,1)S(1)} %get-tuple-element.64.refs_0_, bf16[512,256]{1,0:T(8,128)(2,1)S(1)} %copy-done, bf16[128,65536]{1,0:T(8,128)(2,1)} %refs_4_.17, bf16[128,65536]{1,0:T(8,128)(2,1)} %refs_4_.17, bf16[128,65536]{1,0:T(8,128)(2,1)} %refs_4_.17, ...), custom_call_target="tpu_custom_call" | custom-call | tf_op jit(solution)/shard_map/pallas_call | solution.py:241
  130.8 5.4 %collective-permute-done.19.refs_1_ = bf16[32,8192]{1,0:T(8,128)(2,1)S(1)} collective-permute-done((bf16[32,8192]{1,0:T(8,128)(2,1)S(1)}, bf16[32,8192]{1,0:T(8,128)(2,1)S(1)}, u32[]{:S(2)}, u32[]{:S(2)}) %collective-permute-start.19) | collective-permute-done | bytes 524320 | tf_op jit(solution)/shard_map/ppermute | solution.py:365
  136.2 0.9 shard_map.71
  137.3 3.7 %shard_map.73 = (bf16[64,8192]{1,0:T(8,128)(2,1)S(1)}, bf16[64,8192]{1,0:T(8,128)(2,1)S(1)}) custom-call(bf16[128,128]{1,0:T(8,128)(2,1)S(1)} %get-tuple-element.64.refs_0_, bf16[512,256]{1,0:T(8,128)(2,1)S(1)} %copy-done, bf16[128,65536]{1,0:T(8,128)(2,1)} %refs_4_.17, bf16[128,65536]{1,0:T(8,128)(2,1)} %refs_4_.17, bf16[128,65536]{1,0:T(8,128)(2,1)} %refs_4_.17, ...), custom_call_target="tpu_custom_call" | custom-call | tf_op jit(solution)/shard_map/pallas_call | solution.py:241
  141.1 0.7 collective-permute-start.22
  141.9 1.3 collective-permute-start.21
  143.2 12.7 %collective-permute-done.22.refs_1_ = bf16[32,8192]{1,0:T(8,128)(2,1)S(1)} collective-permute-done((bf16[32,8192]{1,0:T(8,128)(2,1)S(1)}, bf16[32,8192]{1,0:T(8,128)(2,1)S(1)}, u32[]{:S(2)}, u32[]{:S(2)}) %collective-permute-start.22) | collective-permute-done | bytes 524320 | tf_op jit(solution)/shard_map/ppermute | solution.py:365
  155.9 0.9 shard_map.74
  156.8 9.9 %collective-permute-done.21.refs_1_ = bf16[32,8192]{1,0:T(8,128)(2,1)S(1)} collective-permute-done((bf16[32,8192]{1,0:T(8,128)(2,1)S(1)}, bf16[32,8192]{1,0:T(8,128)(2,1)S(1)}, u32[]{:S(2)}, u32[]{:S(2)}) %collective-permute-start.21) | collective-permute-done | bytes 524320 | tf_op jit(solution)/shard_map/ppermute | solution.py:365
  166.7 0.9 shard_map.75
  167.9 0.7 collective-permute-start.25
  168.9 1.4 collective-permute-start.23
  170.3 12.5 %collective-permute-done.25.refs_1_ = bf16[32,8192]{1,0:T(8,128)(2,1)S(1)} collective-permute-done((bf16[32,8192]{1,0:T(8,128)(2,1)S(1)}, bf16[32,8192]{1,0:T(8,128)(2,1)S(1)}, u32[]{:S(2)}, u32[]{:S(2)}) %collective-permute-start.25) | collective-permute-done | bytes 524320 | tf_op jit(solution)/shard_map/ppermute | solution.py:365
  182.8 0.9 shard_map.78
  183.7 8.9 %collective-permute-done.23.refs_1_ = bf16[32,8192]{1,0:T(8,128)(2,1)S(1)} collective-permute-done((bf16[32,8192]{1,0:T(8,128)(2,1)S(1)}, bf16[32,8192]{1,0:T(8,128)(2,1)S(1)}, u32[]{:S(2)}, u32[]{:S(2)}) %collective-permute-start.23) | collective-permute-done | bytes 524320 | tf_op jit(solution)/shard_map/ppermute | solution.py:365
  192.7 0.9 shard_map.79
  (32 shorter events, 1.8 us)
Async XLA Ops:
  1.4 8.2 %collective-permute-start.1 = (bf16[128,128]{1,0:T(8,128)(2,1)S(1)}, bf16[128,128]{1,0:T(8,128)(2,1)S(1)}, u32[]{:S(2)}, u32[]{:S(2)}) collective-permute-start(bf16[128,128]{1,0:T(8,128)(2,1)S(1)} %get-tuple-element.118), channel_id=1, source_target_pairs={{4,0},{8,4},{12,8},{5,1},{9,5},{13,9},{6,2},{10,6},{14,10},{7,3},{... | collective-permute-start | bytes 98312 | tf_op jit(solution)/shard_map/ppermute | solution.py:330
  2.7 7.1 %collective-permute-start = (bf16[128,128]{1,0:T(8,128)(2,1)S(1)}, bf16[128,128]{1,0:T(8,128)(2,1)S(1)}, u32[]{:S(2)}, u32[]{:S(2)}) collective-permute-start(bf16[128,128]{1,0:T(8,128)(2,1)S(1)} %get-tuple-element.119), channel_id=1, source_target_pairs={{0,4},{4,8},{8,12},{1,5},{5,9},{9,13},{2,6},{6,10},{10,14},{3,7},{... | collective-permute-start | bytes 98312 | tf_op jit(solution)/shard_map/ppermute | solution.py:329
  9.6 0.6 copy-start.1
  9.8 0.6 copy-start.3
  30.1 7.2 %collective-permute-start.4 = (f32[128,128]{1,0:T(8,128)}, f32[128,128]{1,0:T(8,128)S(1)}, u32[]{:S(2)}, u32[]{:S(2)}) collective-permute-start(f32[128,128]{1,0:T(8,128)} %get-tuple-element.60.refs_0_), channel_id=1, source_target_pairs={{0,12},{4,8},{8,4},{12,0},{1,13},{5,9},{9,5},{13,1},{2,14},{6,10},... | collective-permute-start | bytes 196616 | tf_op jit(solution)/shard_map/ppermute | solution.py:26
  34.9 5.4 %collective-permute-start.3 = (f32[128,128]{1,0:T(8,128)}, f32[128,128]{1,0:T(8,128)S(1)}, u32[]{:S(2)}, u32[]{:S(2)}) collective-permute-start(f32[128,128]{1,0:T(8,128)} %get-tuple-element.60.refs_0_), channel_id=1, source_target_pairs={{0,8},{4,12},{8,0},{12,4},{1,9},{5,13},{9,1},{13,5},{2,10},{6,14},... | collective-permute-start | bytes 196616 | tf_op jit(solution)/shard_map/ppermute | solution.py:26
  34.9 5.4 %collective-permute-start.2 = (f32[128,128]{1,0:T(8,128)}, f32[128,128]{1,0:T(8,128)S(1)}, u32[]{:S(2)}, u32[]{:S(2)}) collective-permute-start(f32[128,128]{1,0:T(8,128)} %get-tuple-element.60.refs_0_), channel_id=1, source_target_pairs={{0,4},{4,0},{8,12},{12,8},{1,5},{5,1},{9,13},{13,9},{2,6},{6,2},{1... | collective-permute-start | bytes 196616 | tf_op jit(solution)/shard_map/ppermute | solution.py:26
  40.3 0.8 copy-start.5
  41.4 4.4 %collective-permute-start.7 = (f32[128,128]{1,0:T(8,128)S(1)}, f32[128,128]{1,0:T(8,128)S(1)}, u32[]{:S(2)}, u32[]{:S(2)}) collective-permute-start(f32[128,128]{1,0:T(8,128)S(1)} %get-tuple-element.61.refs_0_), channel_id=1, source_target_pairs={{0,3},{1,2},{2,1},{3,0},{4,7},{5,6},{6,5},{7,4},{8,11},{9,10},{10,... | collective-permute-start | bytes 196616 | tf_op jit(solution)/shard_map/ppermute | solution.py:26
  41.5 5.8 %collective-permute-start.6 = (f32[128,128]{1,0:T(8,128)S(1)}, f32[128,128]{1,0:T(8,128)S(1)}, u32[]{:S(2)}, u32[]{:S(2)}) collective-permute-start(f32[128,128]{1,0:T(8,128)S(1)} %get-tuple-element.61.refs_0_), channel_id=1, source_target_pairs={{0,2},{1,3},{2,0},{3,1},{4,6},{5,7},{6,4},{7,5},{8,10},{9,11},{10,... | collective-permute-start | bytes 196616 | tf_op jit(solution)/shard_map/ppermute | solution.py:26
  43.0 4.2 %collective-permute-start.5 = (f32[128,128]{1,0:T(8,128)S(1)}, f32[128,128]{1,0:T(8,128)S(1)}, u32[]{:S(2)}, u32[]{:S(2)}) collective-permute-start(f32[128,128]{1,0:T(8,128)S(1)} %get-tuple-element.61.refs_0_), channel_id=1, source_target_pairs={{0,1},{1,0},{2,3},{3,2},{4,5},{5,4},{6,7},{7,6},{8,9},{9,8},{10,11... | collective-permute-start | bytes 196616 | tf_op jit(solution)/shard_map/ppermute | solution.py:26
  52.2 0.9 copy-start
  53.2 0.8 copy-start.2
  54.0 0.8 copy-start.4
  56.6 3.8 %collective-permute-start.8 = (bf16[64,2048]{1,0:T(8,128)(2,1)S(1)}, bf16[64,2048]{1,0:T(8,128)(2,1)S(1)}, u32[]{:S(2)}, u32[]{:S(2)}) collective-permute-start(bf16[64,2048]{1,0:T(8,128)(2,1)S(1)} %get-tuple-element.66.refs_7_), channel_id=1, source_target_pairs={{0,1},{1,0},{2,3},{3,2},{4,5},{5,4},{6,7},{7,6},{8,9},{9,8},{10,11... | collective-permute-start | bytes 786440 | tf_op jit(solution)/shard_map/ppermute | solution.py:26
  64.2 9.2 %collective-permute-start.10 = (bf16[64,8192]{1,0:T(8,128)(2,1)S(1)}, bf16[64,8192]{1,0:T(8,128)(2,1)S(1)}, u32[]{:S(2)}, u32[]{:S(2)}) collective-permute-start(bf16[64,8192]{1,0:T(8,128)(2,1)S(1)} %get-tuple-element.70.refs_0_.refs_7_), channel_id=1, source_target_pairs={{0,1},{1,0},{2,3},{3,2},{4,5},{5,4},{6,7},{7,6},{8,9},{9,8},{10,11... | collective-permute-start | bytes 3145736 | tf_op jit(solution)/shard_map/ppermute | solution.py:26
  64.7 3.4 %collective-permute-start.9 = (bf16[64,6144]{1,0:T(8,128)(2,1)S(1)}, bf16[64,6144]{1,0:T(8,128)(2,1)S(1)}, u32[]{:S(2)}, u32[]{:S(2)}) collective-permute-start(bf16[64,6144]{1,0:T(8,128)(2,1)S(1)} %get-tuple-element.67.refs_0_.refs_7_), channel_id=1, source_target_pairs={{0,1},{1,0},{2,3},{3,2},{4,5},{5,4},{6,7},{7,6},{8,9},{9,8},{10,11... | collective-permute-start | bytes 2359304 | tf_op jit(solution)/shard_map/ppermute | solution.py:26
  64.7 7.9 %collective-permute-start.11 = (bf16[32,2048]{1,0:T(8,128)(2,1)S(1)}, bf16[32,2048]{1,0:T(8,128)(2,1)S(1)}, u32[]{:S(2)}, u32[]{:S(2)}) collective-permute-start(bf16[32,2048]{1,0:T(8,128)(2,1)S(1)} %get-tuple-element.75), channel_id=1, source_target_pairs={{0,2},{1,3},{2,0},{3,1},{4,6},{5,7},{6,4},{7,5},{8,10},{9,11},{10,... | collective-permute-start | bytes 393224 | tf_op jit(solution)/shard_map/ppermute | solution.py:365
  72.2 29.4 %collective-permute-start.12 = (bf16[64,8192]{1,0:T(8,128)(2,1)S(1)}, bf16[64,8192]{1,0:T(8,128)(2,1)S(1)}, u32[]{:S(2)}, u32[]{:S(2)}) collective-permute-start(bf16[64,8192]{1,0:T(8,128)(2,1)S(1)} %get-tuple-element.73.refs_2_.refs_7_), channel_id=1, source_target_pairs={{0,1},{1,0},{2,3},{3,2},{4,5},{5,4},{6,7},{7,6},{8,9},{9,8},{10,11... | collective-permute-start | bytes 3145736 | tf_op jit(solution)/shard_map/ppermute | solution.py:26
  77.3 29.2 %collective-permute-start.14 = (bf16[64,8192]{1,0:T(8,128)(2,1)S(1)}, bf16[64,8192]{1,0:T(8,128)(2,1)S(1)}, u32[]{:S(2)}, u32[]{:S(2)}) collective-permute-start(bf16[64,8192]{1,0:T(8,128)(2,1)S(1)} %get-tuple-element.78.refs_3_.refs_7_), channel_id=1, source_target_pairs={{0,1},{1,0},{2,3},{3,2},{4,5},{5,4},{6,7},{7,6},{8,9},{9,8},{10,11... | collective-permute-start | bytes 3145736 | tf_op jit(solution)/shard_map/ppermute | solution.py:26
  77.5 28.1 %collective-permute-start.15 = (bf16[32,8192]{1,0:T(8,128)(2,1)S(1)}, bf16[32,8192]{1,0:T(8,128)(2,1)S(1)}, u32[]{:S(2)}, u32[]{:S(2)}) collective-permute-start(bf16[32,8192]{1,0:T(8,128)(2,1)S(1)} %get-tuple-element.86), channel_id=1, source_target_pairs={{0,2},{1,3},{2,0},{3,1},{4,6},{5,7},{6,4},{7,5},{8,10},{9,11},{10,... | collective-permute-start | bytes 1572872 | tf_op jit(solution)/shard_map/ppermute | solution.py:365
  78.2 21.9 %collective-permute-start.13 = (bf16[32,6144]{1,0:T(8,128)(2,1)S(1)}, bf16[32,6144]{1,0:T(8,128)(2,1)S(1)}, u32[]{:S(2)}, u32[]{:S(2)}) collective-permute-start(bf16[32,6144]{1,0:T(8,128)(2,1)S(1)} %get-tuple-element.80), channel_id=1, source_target_pairs={{0,2},{1,3},{2,0},{3,1},{4,6},{5,7},{6,4},{7,5},{8,10},{9,11},{10,... | collective-permute-start | bytes 1179656 | tf_op jit(solution)/shard_map/ppermute | solution.py:365
  105.5 21.2 %collective-permute-start.16 = (bf16[64,8192]{1,0:T(8,128)(2,1)S(1)}, bf16[64,8192]{1,0:T(8,128)(2,1)S(1)}, u32[]{:S(2)}, u32[]{:S(2)}) collective-permute-start(bf16[64,8192]{1,0:T(8,128)(2,1)S(1)} %get-tuple-element.84.refs_3_.refs_7_), channel_id=1, source_target_pairs={{0,1},{1,0},{2,3},{3,2},{4,5},{5,4},{6,7},{7,6},{8,9},{9,8},{10,11... | collective-permute-start | bytes 3145736 | tf_op jit(solution)/shard_map/ppermute | solution.py:26
  110.5 26.6 %collective-permute-start.18 = (bf16[64,8192]{1,0:T(8,128)(2,1)S(1)}, bf16[64,8192]{1,0:T(8,128)(2,1)S(1)}, u32[]{:S(2)}, u32[]{:S(2)}) collective-permute-start(bf16[64,8192]{1,0:T(8,128)(2,1)S(1)} %get-tuple-element.90.refs_3_.refs_7_), channel_id=1, source_target_pairs={{0,1},{1,0},{2,3},{3,2},{4,5},{5,4},{6,7},{7,6},{8,9},{9,8},{10,11... | collective-permute-start | bytes 3145736 | tf_op jit(solution)/shard_map/ppermute | solution.py:26
  111.0 14.8 %collective-permute-start.17 = (bf16[32,8192]{1,0:T(8,128)(2,1)S(1)}, bf16[32,8192]{1,0:T(8,128)(2,1)S(1)}, u32[]{:S(2)}, u32[]{:S(2)}) collective-permute-start(bf16[32,8192]{1,0:T(8,128)(2,1)S(1)} %get-tuple-element.92), channel_id=1, source_target_pairs={{0,2},{1,3},{2,0},{3,1},{4,6},{5,7},{6,4},{7,5},{8,10},{9,11},{10,... | collective-permute-start | bytes 1572872 | tf_op jit(solution)/shard_map/ppermute | solution.py:365
  111.7 24.5 %collective-permute-start.19 = (bf16[32,8192]{1,0:T(8,128)(2,1)S(1)}, bf16[32,8192]{1,0:T(8,128)(2,1)S(1)}, u32[]{:S(2)}, u32[]{:S(2)}) collective-permute-start(bf16[32,8192]{1,0:T(8,128)(2,1)S(1)} %get-tuple-element.98), channel_id=1, source_target_pairs={{0,2},{1,3},{2,0},{3,1},{4,6},{5,7},{6,4},{7,5},{8,10},{9,11},{10,... | collective-permute-start | bytes 1572872 | tf_op jit(solution)/shard_map/ppermute | solution.py:365
  130.7 36.9 %collective-permute-start.24 = (bf16[64,8192]{1,0:T(8,128)(2,1)S(1)}, bf16[64,8192]{1,0:T(8,128)(2,1)S(1)}, u32[]{:S(2)}, u32[]{:S(2)}) collective-permute-start(bf16[64,8192]{1,0:T(8,128)(2,1)S(1)} %get-tuple-element.96.refs_3_.refs_7_), channel_id=1, source_target_pairs={{0,1},{1,0},{2,3},{3,2},{4,5},{5,4},{6,7},{7,6},{8,9},{9,8},{10,11... | collective-permute-start | bytes 3145736 | tf_op jit(solution)/shard_map/ppermute | solution.py:26
  141.1 27.6 %collective-permute-start.20 = (bf16[64,8192]{1,0:T(8,128)(2,1)S(1)}, bf16[64,8192]{1,0:T(8,128)(2,1)S(1)}, u32[]{:S(2)}, u32[]{:S(2)}) collective-permute-start(bf16[64,8192]{1,0:T(8,128)(2,1)S(1)} %get-tuple-element.103.refs_3_), channel_id=1, source_target_pairs={{0,1},{1,0},{2,3},{3,2},{4,5},{5,4},{6,7},{7,6},{8,9},{9,8},{10,11... | collective-permute-start | bytes 3145736 | tf_op jit(solution)/shard_map/ppermute | solution.py:26
  141.1 14.8 %collective-permute-start.22 = (bf16[32,8192]{1,0:T(8,128)(2,1)S(1)}, bf16[32,8192]{1,0:T(8,128)(2,1)S(1)}, u32[]{:S(2)}, u32[]{:S(2)}) collective-permute-start(bf16[32,8192]{1,0:T(8,128)(2,1)S(1)} %get-tuple-element.105), channel_id=1, source_target_pairs={{0,2},{1,3},{2,0},{3,1},{4,6},{5,7},{6,4},{7,5},{8,10},{9,11},{10,... | collective-permute-start | bytes 1572872 | tf_op jit(solution)/shard_map/ppermute | solution.py:365
  141.9 24.8 %collective-permute-start.21 = (bf16[32,8192]{1,0:T(8,128)(2,1)S(1)}, bf16[32,8192]{1,0:T(8,128)(2,1)S(1)}, u32[]{:S(2)}, u32[]{:S(2)}) collective-permute-start(bf16[32,8192]{1,0:T(8,128)(2,1)S(1)} %get-tuple-element.104), channel_id=1, source_target_pairs={{0,2},{1,3},{2,0},{3,1},{4,6},{5,7},{6,4},{7,5},{8,10},{9,11},{10,... | collective-permute-start | bytes 1572872 | tf_op jit(solution)/shard_map/ppermute | solution.py:365
  167.9 14.9 %collective-permute-start.25 = (bf16[32,8192]{1,0:T(8,128)(2,1)S(1)}, bf16[32,8192]{1,0:T(8,128)(2,1)S(1)}, u32[]{:S(2)}, u32[]{:S(2)}) collective-permute-start(bf16[32,8192]{1,0:T(8,128)(2,1)S(1)} %get-tuple-element.114), channel_id=1, source_target_pairs={{0,2},{1,3},{2,0},{3,1},{4,6},{5,7},{6,4},{7,5},{8,10},{9,11},{10,... | collective-permute-start | bytes 1572872 | tf_op jit(solution)/shard_map/ppermute | solution.py:365
  168.9 23.8 %collective-permute-start.23 = (bf16[32,8192]{1,0:T(8,128)(2,1)S(1)}, bf16[32,8192]{1,0:T(8,128)(2,1)S(1)}, u32[]{:S(2)}, u32[]{:S(2)}) collective-permute-start(bf16[32,8192]{1,0:T(8,128)(2,1)S(1)} %get-tuple-element.110), channel_id=1, source_target_pairs={{0,2},{1,3},{2,0},{3,1},{4,6},{5,7},{6,4},{7,5},{8,10},{9,11},{10,... | collective-permute-start | bytes 1572872 | tf_op jit(solution)/shard_map/ppermute | solution.py:365
where the time goes:
time: 194 us
  waiting for transfers between devices  94.3 us (49%)
  Pallas kernels  67 us (35%)
  starting transfers between devices  25.4 us (13%)
  local copies, waits for them, and re-layouts  4.71 us (2%)
    ppermute x9, waiting for transfers between devices, per_device(): lax.ppermute(mine[m], 'pix', routes[m])  82.8 us
    pallas_call x9, Pallas kernels, project(): pl.pallas_call(functools.partial(project_kernel, first, bins // size - 1,...  31.4 us
    pallas_call x1, Pallas kernels, sketch_of(): pl.pallas_call(functools.partial(sketch_kernel, steps), grid=(steps,), in...  19.7 us
    ppermute x15, waiting for transfers between devices, partner(): return lax.ppermute(x, axis, [(i, i ^ shift) for i in range(count)])  11.3 us
    ppermute x15, starting transfers between devices, partner(): return lax.ppermute(x, axis, [(i, i ^ shift) for i in range(count)])  9.45 us
    ppermute x9, starting transfers between devices, per_device(): lax.ppermute(mine[m], 'pix', routes[m])  9.08 us
    pallas_call x9, Pallas kernels, finish(): pl.pallas_call(functools.partial(finish_kernel, len(parts)), grid=(count...  8.55 us
    ppermute x1, starting transfers between devices, per_device(): low = lax.ppermute(spectra[:, bins - TILE:], 'mz', up)  5.56 us
  transfers between devices with their start and end apart: 26, of which 13 were waited for; matrix products, arithmetic and copies ran while one was open for 1% of the time, Pallas kernels for 18%

commit v1 on v0

v1 whole, which is shorter than its diff:
```python
import functools
import math

import jax
import jax.numpy as jnp
from jax import lax
from jax.experimental import pallas as pl
from jax.experimental.pallas import tpu as pltpu
from jax.sharding import PartitionSpec as P

F32 = jnp.float32
BF16 = jnp.bfloat16
HIGHEST = lax.Precision.HIGHEST
TILE = 128
WIDTH = 256
REACH = 64
CHUNK = 8192
VMEM = pl.BlockSpec(memory_space=pltpu.VMEM)


COST = pl.CostEstimate(flops=1, bytes_accessed=1, transcendentals=0)


def params(limit=56):
    return pltpu.CompilerParams(vmem_limit_bytes=limit * 2**20)


def partner(x, axis, shift):
    count = lax.axis_size(axis)
    return lax.ppermute(x, axis, [(i, i ^ shift) for i in range(count)])


def gather(x, axis):
    count = lax.axis_size(axis)
    if count & (count - 1):
        every = lax.all_gather(x, axis)
        return [every[k] for k in range(count)]
    return [x] + [partner(x, axis, shift) for shift in range(1, count)]


def spread(x, axis):
    count = lax.axis_size(axis)
    if count & (count - 1):
        return [lax.psum(x, axis)]
    shift = count // 2
    while shift >= 4:
        x = x + partner(x, axis, shift)
        shift //= 2
    return [x] + [partner(x, axis, s) for s in range(1, min(count, 4))]


def pairwise(parts):
    while len(parts) > 1:
        odd = [parts[-1]] if len(parts) % 2 else []
        parts = [a + b for a, b in zip(parts[::2], parts[1::2])] + odd
    return parts[0]


def band_of(taps):
    wide = jnp.broadcast_to(taps, (WIDTH, 2 * WIDTH))
    return pltpu.roll(wide, 0, 1, stride=1, stride_axis=0).T.astype(BF16)


def clean(before, block, after, band):
    ext = jnp.concatenate([before, block, after], axis=1)
    rows, bins = block.shape
    starts = range(0, bins, WIDTH)
    lhs = jnp.concatenate([ext[:, a : a + 2 * WIDTH] for a in starts], axis=0)
    base = jnp.dot(lhs, band, preferred_element_type=F32)
    mid = jnp.concatenate([block[:, a : a + WIDTH] for a in starts], axis=0)
    out = (mid.astype(F32) - base).astype(BF16)
    return jnp.concatenate([out[i * rows : (i + 1) * rows] for i in range(bins // WIDTH)], axis=1)


def sketch_kernel(steps, taps, block, prev, after, low, high, probes, sketch, band, edges):
    i = pl.program_id(0)

    @pl.when(i == 0)
    def _():
        band[...] = band_of(taps[...])
        sketch[...] = jnp.zeros_like(sketch)

    cleaned = clean(
        jnp.where(i == 0, low[...], prev[...]),
        block[...],
        jnp.where(i == steps - 1, high[...], after[...]),
        band[...],
    )
    sketch[...] += jnp.dot(cleaned, probes[...], preferred_element_type=F32)

    @pl.when((i == 0) | (i == steps - 1))
    def _():
        edges[...] = cleaned


ANY = pl.BlockSpec(memory_space=pl.ANY)


def whole(shape):
    return pl.BlockSpec(shape, lambda i: (0, 0))


def block_specs(rows, size, first, last):
    per = size // TILE
    return [
        pl.BlockSpec((rows, size), lambda i: (0, first + i)),
        pl.BlockSpec((rows, TILE), lambda i: (0, jnp.maximum((first + i) * per - 1, 0))),
        pl.BlockSpec((rows, TILE), lambda i: (0, jnp.minimum((first + i + 1) * per, last))),
    ]


def sketch_of(taps, spectra, low, high, probes, size):
    rows, bins = spectra.shape
    steps = bins // size
    columns = probes.shape[1]
    return pl.pallas_call(
        functools.partial(sketch_kernel, steps),
        grid=(steps,),
        in_specs=[whole(taps.shape)]
        + block_specs(rows, size, 0, bins // TILE - 1)
        + [whole(low.shape), whole(high.shape)]
        + [pl.BlockSpec((size, columns), lambda i: (i, 0))],
        out_specs=[
            whole((rows, columns)),
            whole((2 * WIDTH, WIDTH)),
            pl.BlockSpec((rows, size), lambda i: (0, (i + 1) // steps)),
        ],
        out_shape=[
            jax.ShapeDtypeStruct((rows, columns), F32),
            jax.ShapeDtypeStruct((2 * WIDTH, WIDTH), BF16),
            jax.ShapeDtypeStruct((rows, 2 * size), BF16),
        ],
        cost_estimate=COST,
        compiler_params=params(48),
    )(taps, spectra, spectra, spectra, low, high, probes)


def total_kernel(*refs):
    refs[-1][...] = pairwise([part[...] for part in refs[:-1]])


def total_of(parts):
    return pl.pallas_call(
        total_kernel,
        in_specs=[VMEM] * len(parts),
        out_specs=VMEM,
        out_shape=jax.ShapeDtypeStruct(parts[0].shape, F32),
        cost_estimate=COST,
        compiler_params=params(32),
    )(*parts)


def inverse_factor(gram):
    size = gram.shape[0]
    groups = range(size // 8)
    rows = [gram[8 * g : 8 * g + 8] for g in groups]
    lane = lax.broadcasted_iota(jnp.int32, (8, size), 1)
    sub = lax.broadcasted_iota(jnp.int32, (8, size), 0)

    def row_of(x, k):
        return jnp.broadcast_to(x[k : k + 1], (8, size))

    result = []
    for g in groups:
        inside = (lane >= 8 * g) & (lane < 8 * g + 8)
        below = groups[g:]
        cols = {
            h: [
                jnp.broadcast_to(rows[h][:, 8 * g + k : 8 * g + k + 1], (8, size))
                for k in range(8)
            ]
            for h in below
        }
        for h in below:
            unit = jnp.where(lane - 8 * g == sub, 1.0, 0.0) if h == g else 0.0
            rows[h] = jnp.where(inside, unit, rows[h])
        pivots = jnp.ones((8, size), F32)
        for k in range(8):
            pivot = row_of(cols[g][k], k)
            scale = 1.0 / pivot
            pivots = jnp.where(sub == k, pivot, pivots)
            line = row_of(rows[g], k) * scale
            heads = {m: row_of(cols[g][m], k) * scale for m in range(k + 1, 8)}
            for h in below:
                c = cols[h][k]
                if h == g:
                    c = jnp.where(sub > k, c, 0.0)
                rows[h] = rows[h] - c * line
                for m in range(k + 1, 8):
                    cols[h][m] = cols[h][m] - c * heads[m]
        result.append(jnp.where(lane < 8 * g + 8, rows[g] * lax.rsqrt(pivots), 0.0))
    return jnp.concatenate(result, axis=0)


def basis_kernel(chips, *refs):
    sketches, (basis, turned) = [ref[...] for ref in refs[:-2]], refs[-2:]
    rows, size = sketches[0].shape
    grams = [
        lax.dot_general(
            one, one, (((0,), (0,)), ((), ())), precision=HIGHEST, preferred_element_type=F32
        )
        for one in sketches
    ]
    inverse = inverse_factor(pairwise(grams) / float(rows * len(sketches)))
    used = jnp.concatenate(sketches[: turned.shape[1] // rows], axis=0)
    across = lax.dot_general(
        inverse, used, (((1,), (1,)), ((), ())), precision=HIGHEST, preferred_element_type=F32
    )
    basis[...] = across[:, :rows].T.astype(BF16)
    share = size // (2 * chips)
    me = lax.axis_index("pix")
    shape = (size // 2, size)
    to = lax.broadcasted_iota(jnp.int32, shape, 0)
    source = lax.broadcasted_iota(jnp.int32, shape, 1)
    chip = lax.rem(to // share + me // 2, chips)
    wanted = (2 * chip + lax.rem(me, 2)) * share + lax.rem(to, share)
    pick = jnp.where(wanted == source, 1.0, 0.0).astype(BF16)
    turned[...] = jnp.dot(pick, across.astype(BF16), preferred_element_type=F32).astype(BF16)


def basis_of(sketches, chips, used):
    rows, size = sketches[0].shape
    return pl.pallas_call(
        functools.partial(basis_kernel, chips),
        in_specs=[VMEM] * len(sketches),
        out_specs=[VMEM] * 2,
        out_shape=[
            jax.ShapeDtypeStruct((rows, size), BF16),
            jax.ShapeDtypeStruct((size // 2, used * rows), BF16),
        ],
        cost_estimate=COST,
        compiler_params=params(32),
    )(*sketches)


def put_parts(turned, cleaned, factor, outs):
    used = cleaned.shape[0]
    part = jnp.dot(turned[:, :used], cleaned, preferred_element_type=F32) * factor
    share = outs[0].shape[0]
    for k, out in enumerate(outs):
        out[...] = part[k * share : (k + 1) * share].astype(BF16)


def project_ready_kernel(factor, chips, turned, own, near, *refs):
    outs, done = refs[-1 - chips : -1], refs[-1]
    done[...] = jnp.zeros_like(done)
    put_parts(turned, jnp.concatenate([own[...], near[...]], axis=0), factor, outs)


def project_ready(turned, own, near, start, count, factor, chips, wait):
    rows = own.shape[0]
    size = math.gcd(math.gcd(start, count), 4096)
    share = turned.shape[0] // chips
    return pl.pallas_call(
        functools.partial(project_ready_kernel, factor, chips),
        grid=(count // size,),
        in_specs=[whole(turned.shape)]
        + [pl.BlockSpec((rows, size), lambda i: (0, start // size + i))] * 2
        + [ANY] * len(wait),
        out_specs=[pl.BlockSpec((share, size), lambda i: (0, i))] * chips
        + [whole((8, TILE))],
        out_shape=[jax.ShapeDtypeStruct((share, count), BF16)] * chips
        + [jax.ShapeDtypeStruct((8, TILE), F32)],
        cost_estimate=COST,
        compiler_params=params(60),
    )(turned, own, near, *wait)


def project_kernel(factor, chips, passed, turned, band, *refs):
    blocks = refs[:6]
    outs, done = refs[len(refs) - passed - 1 - chips :][:chips], refs[-1 - passed]
    done[...] = jnp.zeros_like(done)
    put_parts(turned, clean_all(blocks, band[...]), factor, outs)


def clean_all(blocks, band):
    return jnp.concatenate(
        [
            clean(blocks[n + 1][...], blocks[n][...], blocks[n + 2][...], band)
            for n in range(0, len(blocks), 3)
        ],
        axis=0,
    )


def project(turned, band, spectra, near, start, count, factor, chips, wait, passed):
    rows, bins = spectra.shape
    size = math.gcd(math.gcd(start, count), 4096)
    share = turned.shape[0] // chips
    return pl.pallas_call(
        functools.partial(project_kernel, factor, chips, len(passed)),
        grid=(count // size,),
        in_specs=[whole(turned.shape), whole(band.shape)]
        + block_specs(rows, size, start // size, bins // TILE - 1) * 2
        + [ANY] * (len(wait) + len(passed)),
        out_specs=[pl.BlockSpec((share, size), lambda i: (0, i))] * chips
        + [whole((8, TILE))]
        + [ANY] * len(passed),
        out_shape=[jax.ShapeDtypeStruct((share, count), BF16)] * chips
        + [jax.ShapeDtypeStruct((8, TILE), F32)]
        + [jax.ShapeDtypeStruct(one.shape, one.dtype) for one in passed],
        input_output_aliases={8 + len(wait) + n: chips + 1 + n for n in range(len(passed))},
        cost_estimate=COST,
        compiler_params=params(50),
    )(turned, band, spectra, spectra, spectra, near, near, near, *wait, *passed)


def project_whole_kernel(factor, turned, band, *refs):
    blocks, out, done = refs[:12], refs[-2], refs[-1]
    done[...] = jnp.zeros_like(done)
    put_parts(turned[: out.shape[0]], clean_all(blocks, band[...]), factor, [out])


def project_whole(out, turned, band, spectra, near, far, start, factor, wait):
    rows, bins = spectra.shape
    count = far[0].shape[1] - 2 * TILE
    size = math.gcd(math.gcd(start, count), 4096)
    first = start // size
    steps, per = count // size, size // TILE
    far_specs = [
        pl.BlockSpec((rows, size), lambda i: (0, i)),
        pl.BlockSpec((rows, TILE), lambda i: (0, jnp.where(i == 0, steps * per, i * per - 1))),
        pl.BlockSpec(
            (rows, TILE),
            lambda i: (0, jnp.where(i == steps - 1, steps * per + 1, (i + 1) * per)),
        ),
    ]
    share = out.shape[0]
    return pl.pallas_call(
        functools.partial(project_whole_kernel, factor),
        grid=(steps,),
        in_specs=[whole(turned.shape), whole(band.shape)]
        + block_specs(rows, size, first, bins // TILE - 1) * 2
        + far_specs * 2
        + [ANY] * (1 + len(wait)),
        out_specs=[pl.BlockSpec((share, size), lambda i: (0, first + i)), whole((8, TILE))],
        out_shape=[
            jax.ShapeDtypeStruct(out.shape, BF16),
            jax.ShapeDtypeStruct((8, TILE), F32),
        ],
        input_output_aliases={14: 0},
        cost_estimate=COST,
        compiler_params=params(50),
    )(turned, band, *[spectra] * 3, *[near] * 3, *[far[0]] * 3, *[far[1]] * 3, out, *wait)


def finish_kernel(count, *refs):
    parts, out, done = refs[:count], refs[-2], refs[-1]
    done[...] = jnp.zeros_like(done)
    total = parts[0][...].astype(F32)
    for part in parts[1:]:
        total = total + part[...].astype(F32)
    out[...] = total.astype(BF16)


def finish(out, parts, start, bins, wait):
    share, count = parts[0].shape
    size = math.gcd(math.gcd(count, start), 8192)
    first = start // size
    place = pl.BlockSpec((share, size), lambda i: (0, first + i))
    extra = [] if out is None else [out]
    return pl.pallas_call(
        functools.partial(finish_kernel, len(parts)),
        grid=(count // size,),
        in_specs=[pl.BlockSpec((share, size), lambda i: (0, i))] * len(parts)
        + [ANY] * (len(extra) + len(wait)),
        out_specs=[place, whole((8, TILE))],
        out_shape=[
            jax.ShapeDtypeStruct((share, bins), BF16),
            jax.ShapeDtypeStruct((8, TILE), F32),
        ],
        input_output_aliases={len(parts): 0} if extra else {},
        cost_estimate=COST,
        compiler_params=params(32),
    )(*parts, *extra, *wait)


def chunks_of(bins, size, early):
    chunks = [(a, size) for a in range(0, bins, size) if a != early]
    start, _ = chunks.pop()
    return chunks + [(start, size // 2), (start + size // 2, size // 2)]


def per_device(spectra, kernel, probes):
    rows, bins = spectra.shape
    pix = lax.axis_size("pix")
    depth = lax.axis_size("mz")
    chips = pix // 2
    factor = 1.0 / math.sqrt(float(rows * pix))

    up = [(i, i + 1) for i in range(depth - 1)]
    down = [(i + 1, i) for i in range(depth - 1)]
    low = lax.ppermute(spectra[:, bins - TILE :], "mz", up)
    high = lax.ppermute(spectra[:, :TILE], "mz", down)
    taps = jnp.pad(kernel.astype(F32), (REACH, 2 * WIDTH - REACH - kernel.shape[0]))[None]

    near = partner(spectra, "pix", 1)
    size = math.gcd(bins, CHUNK)
    early = None
    far = None
    if early is not None:
        end = early + size
        far = partner(
            jnp.concatenate(
                [
                    spectra[:, early:end],
                    spectra[:, early - TILE : early],
                    spectra[:, end : end + TILE],
                ],
                axis=1,
            ),
            "pix",
            2,
        )
    partial_sketch, band, edges = sketch_of(taps, spectra, low, high, probes, size)
    near_edges = partner(edges, "pix", 1)
    sketch = total_of(spread(partial_sketch, "mz"))
    basis, turned = basis_of(gather(sketch, "pix"), chips, 2 if far is None else 4)

    routes = [
        [
            (2 * chip + core, 2 * ((chip + k) % chips) + core)
            for chip in range(chips)
            for core in range(2)
        ]
        for k in range(chips)
    ]

    out, sent, recent = None, [], []
    chunks = chunks_of(bins, size, early)
    for k, (start, count) in enumerate(chunks):
        inner = 0 < start < bins - size
        if inner:
            passed = [] if far is None or len(sent) != 1 else [far]
            *mine, done = project(
                turned, band, spectra, near, start, count, factor, chips, recent, passed
            )
            if passed:
                mine, done, far = mine[:-1], mine[-1], done
        else:
            at = start if start < size else start - bins + 2 * size
            *mine, done = project_ready(
                turned, edges, near_edges, at, count, factor, chips, recent
            )
        recent = [done]
        sent.append(
            [mine[0]] + [lax.ppermute(mine[m], "pix", routes[m]) for m in range(1, chips)]
        )
        if k == len(chunks) - 1 and far is not None:
            out, done = project_whole(
                out, turned, band, spectra, near, [far, partner(far, "pix", 1)], early, factor,
                recent,
            )
            recent = [done]
        if k >= 1:
            out, done = finish(out, sent[k - 1], chunks[k - 1][0], bins, recent)
            recent = [done]
    out, done = finish(out, sent[-1], chunks[-1][0], bins, recent)
    return (basis, out)


def solution(mesh):
    in_specs = (P(("groups", "pix"), "mz"), P(), P("mz", None))
    out_specs = (P(("groups", "pix"), None), P(("groups", "pix"), "mz"))
    return jax.shard_map(
        per_device, mesh=mesh, in_specs=in_specs, out_specs=out_specs, check_vma=False
    )
```

time: 194 us -> 155 us (0.80)
  waiting for transfers between devices: 94.3 us -> 45.9 us
  Pallas kernels: 67 us -> 72.3 us
  local copies, waits for them, and re-layouts: 4.71 us -> 8.57 us
    ppermute x9, waiting for transfers between devices: 82.8 us -> 35.7 us  [per_device(): lax.ppermute(mine[m], 'pix', routes[m])]
    pallas_call x20 -> x11, Pallas kernels: 38.8 us -> 44.6 us  [the longest x6 29.6 us: project(): pl.pallas_call(functools.partial(project_kernel, factor, chips, len(passe...]
    unnamed x12 -> x24, local copies, waits for them, and re-layouts: 3.92 us -> 7.79 us
    ppermute x9, starting transfers between devices: 9.08 us -> 12.6 us  [per_device(): lax.ppermute(mine[m], 'pix', routes[m])]
    ppermute x15 -> x8, waiting for transfers between devices: 11.3 us -> 9.32 us  [partner(): return lax.ppermute(x, axis, [(i, i ^ shift) for i in range(count)])]
    ppermute x15 -> x8, starting transfers between devices: 9.45 us -> 7.81 us  [partner(): return lax.ppermute(x, axis, [(i, i ^ shift) for i in range(count)])]
  transfers between devices with their start and end apart: 26 -> 19, of which waited for: 13 -> 13; matrix products, arithmetic and copies ran while one was open for 1% -> 1% of each run, Pallas kernels for 18% -> 46%
where the time goes in v1:
time: 155 us
  Pallas kernels  72.3 us (47%)
  waiting for transfers between devices  45.9 us (30%)
  starting transfers between devices  26.8 us (17%)
  local copies, waits for them, and re-layouts  8.57 us (6%)
    ppermute x9, waiting for transfers between devices, per_device(): lax.ppermute(mine[m], 'pix', routes[m])  35.7 us
    pallas_call x6, Pallas kernels, project(): pl.pallas_call(functools.partial(project_kernel, factor, chips, len(passe...  29.6 us
    pallas_call x1, Pallas kernels, sketch_of(): pl.pallas_call(functools.partial(sketch_kernel, steps), grid=(steps,), in...  19.7 us
    ppermute x9, starting transfers between devices, per_device(): lax.ppermute(mine[m], 'pix', routes[m])  12.6 us
    pallas_call x3, Pallas kernels, project_ready(): pl.pallas_call(functools.partial(project_ready_kernel, factor, chips), gr...  9.45 us
    ppermute x8, waiting for transfers between devices, partner(): return lax.ppermute(x, axis, [(i, i ^ shift) for i in range(count)])  9.32 us
    pallas_call x9, Pallas kernels, finish(): pl.pallas_call(functools.partial(finish_kernel, len(parts)), grid=(count...  7.96 us
    ppermute x8, starting transfers between devices, partner(): return lax.ppermute(x, axis, [(i, i ^ shift) for i in range(count)])  7.81 us
  transfers between devices with their start and end apart: 19, of which 13 were waited for; matrix products, arithmetic and copies ran while one was open for 1% of the time, Pallas kernels for 46%

profile of v1, /device:TPU:0, one launch (start us, length us, event | category | flops | bytes accessed | tf_op | source)
XLA Modules:
  0.0 155.0 jit_solution(13331333834798118286)
XLA Ops:
  0.6 0.5 collective-permute-start.9
  1.1 0.8 fusion
  1.9 1.3 collective-permute-start.1
  3.2 5.1 %collective-permute-start = (bf16[128,128]{1,0:T(8,128)(2,1)S(1)}, bf16[128,128]{1,0:T(8,128)(2,1)S(1)}, u32[]{:S(2)}, u32[]{:S(2)}) collective-permute-start(bf16[128,128]{1,0:T(8,128)(2,1)S(1)} %get-tuple-element.101), channel_id=1, source_target_pairs={{0,4},{4,8},{8,12},{1,5},{5,9},{9,13},{2,6},{6,10},{10,14},{3,7},{... | collective-permute-start | bytes 98312 | tf_op jit(solution)/shard_map/ppermute | solution.py:393
  8.3 0.7 pad_convert_fusion
  9.1 0.0 collective-permute-done.1.high
  9.1 0.8 collective-permute-done.low
  9.9 19.7 %shard_map.50 = (f32[128,128]{1,0:T(8,128)S(1)}, bf16[512,256]{1,0:T(8,128)(2,1)S(1)}, bf16[128,16384]{1,0:T(8,128)(2,1)S(1)}) custom-call(f32[1,512]{1,0:T(1,128)S(1)} %bitcast.1, bf16[128,65536]{1,0:T(8,128)(2,1)} %refs_2_.11, bf16[128,65536]{1,0:T(8,128)(2,1)} %refs_2_.11, bf16[128,65536]{1,0:T(8,128)(2,1)} %refs_2_.11, ...), custom_call_target="tpu_custom_call" | custom-call | flops 1 | bytes 1 | tf_op jit(solution)/shard_map/pallas_call | solution.py:116
  29.7 2.0 %copy-done = bf16[128,16384]{1,0:T(8,128)(2,1)} copy-done((bf16[128,16384]{1,0:T(8,128)(2,1)}, bf16[128,16384]{1,0:T(8,128)(2,1)S(1)}, u32[]{:S(2)}) %copy-start) | copy-done | bytes 4194328
  31.6 4.8 %collective-permute-start.4 = (f32[128,128]{1,0:T(8,128)S(1)}, f32[128,128]{1,0:T(8,128)S(1)}, u32[]{:S(2)}, u32[]{:S(2)}) collective-permute-start(f32[128,128]{1,0:T(8,128)S(1)} %get-tuple-element.51.refs_0_), channel_id=1, source_target_pairs={{0,12},{4,8},{8,4},{12,0},{1,13},{5,9},{9,5},{13,1},{2,14},{6,10},... | collective-permute-start | bytes 196616 | tf_op jit(solution)/shard_map/ppermute | solution.py:30
  36.4 0.6 collective-permute-start.2
  37.0 2.4 %collective-permute-done.4.refs_3_ = f32[128,128]{1,0:T(8,128)S(1)} collective-permute-done((f32[128,128]{1,0:T(8,128)S(1)}, f32[128,128]{1,0:T(8,128)S(1)}, u32[]{:S(2)}, u32[]{:S(2)}) %collective-permute-start.4) | collective-permute-done | bytes 65568 | tf_op jit(solution)/shard_map/ppermute | solution.py:30
  39.3 3.0 %collective-permute-done.3.refs_2_ = f32[128,128]{1,0:T(8,128)S(1)} collective-permute-done((f32[128,128]{1,0:T(8,128)S(1)}, f32[128,128]{1,0:T(8,128)S(1)}, u32[]{:S(2)}, u32[]{:S(2)}) %collective-permute-start.3) | collective-permute-done | bytes 65568 | tf_op jit(solution)/shard_map/ppermute | solution.py:30
  42.4 1.1 collective-permute-start.7
  43.4 0.7 collective-permute-start.6
  44.2 0.1 collective-permute-start.5
  44.3 2.3 %collective-permute-done.7.refs_3_ = f32[128,128]{1,0:T(8,128)S(1)} collective-permute-done((f32[128,128]{1,0:T(8,128)S(1)}, f32[128,128]{1,0:T(8,128)S(1)}, u32[]{:S(2)}, u32[]{:S(2)}) %collective-permute-start.7) | collective-permute-done | bytes 65568 | tf_op jit(solution)/shard_map/ppermute | solution.py:30
  46.6 1.6 %collective-permute-done.6.refs_2_ = f32[128,128]{1,0:T(8,128)S(1)} collective-permute-done((f32[128,128]{1,0:T(8,128)S(1)}, f32[128,128]{1,0:T(8,128)S(1)}, u32[]{:S(2)}, u32[]{:S(2)}) %collective-permute-start.6) | collective-permute-done | bytes 65568 | tf_op jit(solution)/shard_map/ppermute | solution.py:30
  48.2 0.0 collective-permute-done.5.refs_1_
  48.2 5.5 %shard_map.52 = (bf16[128,128]{1,0:T(8,128)(2,1)}, bf16[64,256]{1,0:T(8,128)(2,1)S(1)}) custom-call(f32[128,128]{1,0:T(8,128)S(1)} %shard_map.51.refs_0_, f32[128,128]{1,0:T(8,128)S(1)} %collective-permute-done.5.refs_1_, f32[128,128]{1,0:T(8,128)S(1)} %collective-permute-done.6.refs_2_, f32[128,128]{1,0:T(8,128)S(1)} %collective-permute-done.7.refs_3_), custom_call_target="tpu_custom_call" | custom-call | flops 1 | bytes 1 | tf_op jit(solution)/shard_map/pallas_call | solution.py:223
  53.8 0.6 copy-done.1
  54.4 2.0 %copy-done.11 = bf16[128,16384]{1,0:T(8,128)(2,1)} copy-done((bf16[128,16384]{1,0:T(8,128)(2,1)}, bf16[128,16384]{1,0:T(8,128)(2,1)S(1)}, u32[]{:S(2)}) %copy-start.11) | copy-done | bytes 4194328
  56.4 3.7 %shard_map.53 = (bf16[32,8192]{1,0:T(8,128)(2,1)}, bf16[32,8192]{1,0:T(8,128)(2,1)}, f32[8,128]{1,0:T(8,128)}) custom-call(bf16[64,256]{1,0:T(8,128)(2,1)} %copy-done.1, bf16[128,16384]{1,0:T(8,128)(2,1)} %copy-done, bf16[128,16384]{1,0:T(8,128)(2,1)} %copy-done.11), custom_call_target="tpu_custom_call" | custom-call | flops 1 | bytes 1 | tf_op jit(solution)/shard_map/pallas_call | solution.py:254
  60.1 1.5 collective-permute-start.10
  61.6 0.0 collective-permute-done.9.refs_3_.refs_4_.refs_5_
  61.6 0.7 copy-done.6
  62.3 5.0 %shard_map.54 = (bf16[32,8192]{1,0:T(8,128)(2,1)S(1)}, bf16[32,8192]{1,0:T(8,128)(2,1)S(1)}, f32[8,128]{1,0:T(8,128)S(1)}) custom-call(bf16[64,256]{1,0:T(8,128)(2,1)S(1)} %copy-done.2, bf16[512,256]{1,0:T(8,128)(2,1)S(1)} %get-tuple-element.55.band, bf16[128,65536]{1,0:T(8,128)(2,1)} %refs_2_.11, bf16[128,65536]{1,0:T(8,128)(2,1)} %refs_2_.11, ...), custom_call_target="tpu_custom_call" | custom-call | flops 1 | bytes 1 | tf_op jit(solution)/shard_map/pallas_call | solution.py:290
  67.3 0.6 collective-permute-start.12
  67.9 7.2 %collective-permute-done.10.refs_1_ = bf16[32,8192]{1,0:T(8,128)(2,1)S(1)} collective-permute-done((bf16[32,8192]{1,0:T(8,128)(2,1)}, bf16[32,8192]{1,0:T(8,128)(2,1)S(1)}, u32[]{:S(2)}, u32[]{:S(2)}) %collective-permute-start.10) | collective-permute-done | bytes 524320 | tf_op jit(solution)/shard_map/ppermute | solution.py:447
  75.1 0.9 shard_map.55
  76.1 4.9 %shard_map.56 = (bf16[32,8192]{1,0:T(8,128)(2,1)S(1)}, bf16[32,8192]{1,0:T(8,128)(2,1)S(1)}, f32[8,128]{1,0:T(8,128)S(1)}) custom-call(bf16[64,256]{1,0:T(8,128)(2,1)S(1)} %copy-done.2, bf16[512,256]{1,0:T(8,128)(2,1)S(1)} %get-tuple-element.55.band, bf16[128,65536]{1,0:T(8,128)(2,1)} %refs_2_.11, bf16[128,65536]{1,0:T(8,128)(2,1)} %refs_2_.11, ...), custom_call_target="tpu_custom_call" | custom-call | flops 1 | bytes 1 | tf_op jit(solution)/shard_map/pallas_call | solution.py:290
  81.0 1.5 collective-permute-start.11
  82.5 3.9 %collective-permute-done.12.refs_1_ = bf16[32,8192]{1,0:T(8,128)(2,1)S(1)} collective-permute-done((bf16[32,8192]{1,0:T(8,128)(2,1)S(1)}, bf16[32,8192]{1,0:T(8,128)(2,1)S(1)}, u32[]{:S(2)}, u32[]{:S(2)}) %collective-permute-start.12) | collective-permute-done | bytes 524320 | tf_op jit(solution)/shard_map/ppermute | solution.py:447
  86.4 0.9 shard_map.57
  87.3 4.9 %shard_map.58 = (bf16[32,8192]{1,0:T(8,128)(2,1)S(1)}, bf16[32,8192]{1,0:T(8,128)(2,1)S(1)}, f32[8,128]{1,0:T(8,128)S(1)}) custom-call(bf16[64,256]{1,0:T(8,128)(2,1)S(1)} %copy-done.2, bf16[512,256]{1,0:T(8,128)(2,1)S(1)} %get-tuple-element.55.band, bf16[128,65536]{1,0:T(8,128)(2,1)} %refs_2_.11, bf16[128,65536]{1,0:T(8,128)(2,1)} %refs_2_.11, ...), custom_call_target="tpu_custom_call" | custom-call | flops 1 | bytes 1 | tf_op jit(solution)/shard_map/pallas_call | solution.py:290
  92.2 1.5 collective-permute-start.14
  93.8 3.9 %collective-permute-done.11.refs_1_ = bf16[32,8192]{1,0:T(8,128)(2,1)S(1)} collective-permute-done((bf16[32,8192]{1,0:T(8,128)(2,1)S(1)}, bf16[32,8192]{1,0:T(8,128)(2,1)S(1)}, u32[]{:S(2)}, u32[]{:S(2)}) %collective-permute-start.11) | collective-permute-done | bytes 524320 | tf_op jit(solution)/shard_map/ppermute | solution.py:447
  97.6 0.9 shard_map.59
  98.5 4.9 %shard_map.60 = (bf16[32,8192]{1,0:T(8,128)(2,1)S(1)}, bf16[32,8192]{1,0:T(8,128)(2,1)S(1)}, f32[8,128]{1,0:T(8,128)S(1)}) custom-call(bf16[64,256]{1,0:T(8,128)(2,1)S(1)} %copy-done.2, bf16[512,256]{1,0:T(8,128)(2,1)S(1)} %get-tuple-element.55.band, bf16[128,65536]{1,0:T(8,128)(2,1)} %refs_2_.11, bf16[128,65536]{1,0:T(8,128)(2,1)} %refs_2_.11, ...), custom_call_target="tpu_custom_call" | custom-call | flops 1 | bytes 1 | tf_op jit(solution)/shard_map/pallas_call | solution.py:290
  103.5 1.5 collective-permute-start.13
  105.0 3.9 %collective-permute-done.14.refs_1_ = bf16[32,8192]{1,0:T(8,128)(2,1)S(1)} collective-permute-done((bf16[32,8192]{1,0:T(8,128)(2,1)S(1)}, bf16[32,8192]{1,0:T(8,128)(2,1)S(1)}, u32[]{:S(2)}, u32[]{:S(2)}) %collective-permute-start.14) | collective-permute-done | bytes 524320 | tf_op jit(solution)/shard_map/ppermute | solution.py:447
  108.9 0.9 shard_map.61
  109.8 4.9 %shard_map.62 = (bf16[32,8192]{1,0:T(8,128)(2,1)S(1)}, bf16[32,8192]{1,0:T(8,128)(2,1)S(1)}, f32[8,128]{1,0:T(8,128)S(1)}) custom-call(bf16[64,256]{1,0:T(8,128)(2,1)S(1)} %copy-done.2, bf16[512,256]{1,0:T(8,128)(2,1)S(1)} %get-tuple-element.55.band, bf16[128,65536]{1,0:T(8,128)(2,1)} %refs_2_.11, bf16[128,65536]{1,0:T(8,128)(2,1)} %refs_2_.11, ...), custom_call_target="tpu_custom_call" | custom-call | flops 1 | bytes 1 | tf_op jit(solution)/shard_map/pallas_call | solution.py:290
  114.7 1.5 collective-permute-start.16
  116.2 3.9 %collective-permute-done.13.refs_1_ = bf16[32,8192]{1,0:T(8,128)(2,1)S(1)} collective-permute-done((bf16[32,8192]{1,0:T(8,128)(2,1)S(1)}, bf16[32,8192]{1,0:T(8,128)(2,1)S(1)}, u32[]{:S(2)}, u32[]{:S(2)}) %collective-permute-start.13) | collective-permute-done | bytes 524320 | tf_op jit(solution)/shard_map/ppermute | solution.py:447
  120.1 0.9 shard_map.63
  121.0 4.9 %shard_map.64 = (bf16[32,8192]{1,0:T(8,128)(2,1)S(1)}, bf16[32,8192]{1,0:T(8,128)(2,1)S(1)}, f32[8,128]{1,0:T(8,128)S(1)}) custom-call(bf16[64,256]{1,0:T(8,128)(2,1)S(1)} %copy-done.2, bf16[512,256]{1,0:T(8,128)(2,1)S(1)} %get-tuple-element.55.band, bf16[128,65536]{1,0:T(8,128)(2,1)} %refs_2_.11, bf16[128,65536]{1,0:T(8,128)(2,1)} %refs_2_.11, ...), custom_call_target="tpu_custom_call" | custom-call | flops 1 | bytes 1 | tf_op jit(solution)/shard_map/pallas_call | solution.py:290
  126.0 1.5 collective-permute-start.15
  127.5 3.9 %collective-permute-done.16.refs_1_ = bf16[32,8192]{1,0:T(8,128)(2,1)S(1)} collective-permute-done((bf16[32,8192]{1,0:T(8,128)(2,1)S(1)}, bf16[32,8192]{1,0:T(8,128)(2,1)S(1)}, u32[]{:S(2)}, u32[]{:S(2)}) %collective-permute-start.16) | collective-permute-done | bytes 524320 | tf_op jit(solution)/shard_map/ppermute | solution.py:447
  131.3 0.9 shard_map.65
  132.2 0.6 copy-done.8
  132.8 2.8 %shard_map.66 = (bf16[32,4096]{1,0:T(8,128)(2,1)}, bf16[32,4096]{1,0:T(8,128)(2,1)}, f32[8,128]{1,0:T(8,128)}) custom-call(bf16[64,256]{1,0:T(8,128)(2,1)} %copy-done.1, bf16[128,16384]{1,0:T(8,128)(2,1)} %copy-done, bf16[128,16384]{1,0:T(8,128)(2,1)} %copy-done.11, f32[8,128]{1,0:T(8,128)} %copy-done.8), custom_call_target="tpu_custom_call" | custom-call | flops 1 | bytes 1 | tf_op jit(solution)/shard_map/pallas_call | solution.py:254
  135.7 1.4 collective-permute-start.18
  137.1 5.5 %collective-permute-done.15.refs_1_ = bf16[32,8192]{1,0:T(8,128)(2,1)S(1)} collective-permute-done((bf16[32,8192]{1,0:T(8,128)(2,1)S(1)}, bf16[32,8192]{1,0:T(8,128)(2,1)S(1)}, u32[]{:S(2)}, u32[]{:S(2)}) %collective-permute-start.15) | collective-permute-done | bytes 524320 | tf_op jit(solution)/shard_map/ppermute | solution.py:447
  142.6 0.7 copy-done.10
  143.2 0.9 shard_map.67
  144.1 0.6 copy-done.7
  144.7 2.9 %shard_map.68 = (bf16[32,4096]{1,0:T(8,128)(2,1)}, bf16[32,4096]{1,0:T(8,128)(2,1)}, f32[8,128]{1,0:T(8,128)}) custom-call(bf16[64,256]{1,0:T(8,128)(2,1)} %copy-done.1, bf16[128,16384]{1,0:T(8,128)(2,1)} %copy-done, bf16[128,16384]{1,0:T(8,128)(2,1)} %copy-done.11, f32[8,128]{1,0:T(8,128)} %copy-done.7), custom_call_target="tpu_custom_call" | custom-call | flops 1 | bytes 1 | tf_op jit(solution)/shard_map/pallas_call | solution.py:254
  147.6 1.4 collective-permute-start.17
  149.1 0.0 collective-permute-done.18.refs_1_
  149.1 0.7 copy-done.9
  149.8 0.8 shard_map.69
  150.5 3.7 %collective-permute-done.17.refs_1_ = bf16[32,4096]{1,0:T(8,128)(2,1)S(1)} collective-permute-done((bf16[32,4096]{1,0:T(8,128)(2,1)}, bf16[32,4096]{1,0:T(8,128)(2,1)S(1)}, u32[]{:S(2)}, u32[]{:S(2)}) %collective-permute-start.17) | collective-permute-done | bytes 262176 | tf_op jit(solution)/shard_map/ppermute | solution.py:447
  154.2 0.8 shard_map.70
  (21 shorter events, 0.1 us)
Async XLA Ops:
  0.6 61.0 %collective-permute-start.9 = (bf16[128,65536]{1,0:T(8,128)(2,1)}, bf16[128,65536]{1,0:T(8,128)(2,1)}, u32[]{:S(2)}, u32[]{:S(2)}) collective-permute-start(bf16[128,65536]{1,0:T(8,128)(2,1)} %refs_2_.11), channel_id=1, source_target_pairs={{0,1},{1,0},{2,3},{3,2},{4,5},{5,4},{6,7},{7,6},{8,9},{9,8},{10,11... | collective-permute-start | bytes 50331656 | tf_op jit(solution)/shard_map/ppermute | solution.py:30
  1.9 7.2 %collective-permute-start.1 = (bf16[128,128]{1,0:T(8,128)(2,1)S(1)}, bf16[128,128]{1,0:T(8,128)(2,1)S(1)}, u32[]{:S(2)}, u32[]{:S(2)}) collective-permute-start(bf16[128,128]{1,0:T(8,128)(2,1)S(1)} %get-tuple-element.100), channel_id=1, source_target_pairs={{4,0},{8,4},{12,8},{5,1},{9,5},{13,9},{6,2},{10,6},{14,10},{7,3},{... | collective-permute-start | bytes 98312 | tf_op jit(solution)/shard_map/ppermute | solution.py:394
  3.2 6.7 %collective-permute-start = (bf16[128,128]{1,0:T(8,128)(2,1)S(1)}, bf16[128,128]{1,0:T(8,128)(2,1)S(1)}, u32[]{:S(2)}, u32[]{:S(2)}) collective-permute-start(bf16[128,128]{1,0:T(8,128)(2,1)S(1)} %get-tuple-element.101), channel_id=1, source_target_pairs={{0,4},{4,8},{8,12},{1,5},{5,9},{9,13},{2,6},{6,10},{10,14},{3,7},{... | collective-permute-start | bytes 98312 | tf_op jit(solution)/shard_map/ppermute | solution.py:393
  29.7 2.0 %copy-start = (bf16[128,16384]{1,0:T(8,128)(2,1)}, bf16[128,16384]{1,0:T(8,128)(2,1)S(1)}, u32[]{:S(2)}) copy-start(bf16[128,16384]{1,0:T(8,128)(2,1)S(1)} %get-tuple-element.54.own) | copy-start | bytes 12582916
  31.6 22.8 %collective-permute-start.8 = (bf16[128,16384]{1,0:T(8,128)(2,1)S(1)}, bf16[128,16384]{1,0:T(8,128)(2,1)S(1)}, u32[]{:S(2)}, u32[]{:S(2)}) collective-permute-start(bf16[128,16384]{1,0:T(8,128)(2,1)S(1)} %get-tuple-element.54.own), channel_id=1, source_target_pairs={{0,1},{1,0},{2,3},{3,2},{4,5},{5,4},{6,7},{7,6},{8,9},{9,8},{10,11... | collective-permute-start | bytes 12582920 | tf_op jit(solution)/shard_map/ppermute | solution.py:30
  31.6 7.7 %collective-permute-start.4 = (f32[128,128]{1,0:T(8,128)S(1)}, f32[128,128]{1,0:T(8,128)S(1)}, u32[]{:S(2)}, u32[]{:S(2)}) collective-permute-start(f32[128,128]{1,0:T(8,128)S(1)} %get-tuple-element.51.refs_0_), channel_id=1, source_target_pairs={{0,12},{4,8},{8,4},{12,0},{1,13},{5,9},{9,5},{13,1},{2,14},{6,10},... | collective-permute-start | bytes 196616 | tf_op jit(solution)/shard_map/ppermute | solution.py:30
  36.4 6.0 %collective-permute-start.3 = (f32[128,128]{1,0:T(8,128)S(1)}, f32[128,128]{1,0:T(8,128)S(1)}, u32[]{:S(2)}, u32[]{:S(2)}) collective-permute-start(f32[128,128]{1,0:T(8,128)S(1)} %get-tuple-element.51.refs_0_), channel_id=1, source_target_pairs={{0,8},{4,12},{8,0},{12,4},{1,9},{5,13},{9,1},{13,5},{2,10},{6,14},... | collective-permute-start | bytes 196616 | tf_op jit(solution)/shard_map/ppermute | solution.py:30
  36.4 6.0 %collective-permute-start.2 = (f32[128,128]{1,0:T(8,128)S(1)}, f32[128,128]{1,0:T(8,128)S(1)}, u32[]{:S(2)}, u32[]{:S(2)}) collective-permute-start(f32[128,128]{1,0:T(8,128)S(1)} %get-tuple-element.51.refs_0_), channel_id=1, source_target_pairs={{0,4},{4,0},{8,12},{12,8},{1,5},{5,1},{9,13},{13,9},{2,6},{6,2},{1... | collective-permute-start | bytes 196616 | tf_op jit(solution)/shard_map/ppermute | solution.py:30
  42.4 4.2 %collective-permute-start.7 = (f32[128,128]{1,0:T(8,128)S(1)}, f32[128,128]{1,0:T(8,128)S(1)}, u32[]{:S(2)}, u32[]{:S(2)}) collective-permute-start(f32[128,128]{1,0:T(8,128)S(1)} %shard_map.51.refs_0_), channel_id=1, source_target_pairs={{0,3},{1,2},{2,1},{3,0},{4,7},{5,6},{6,5},{7,4},{8,11},{9,10},{10,... | collective-permute-start | bytes 196616 | tf_op jit(solution)/shard_map/ppermute | solution.py:30
  43.4 4.8 %collective-permute-start.6 = (f32[128,128]{1,0:T(8,128)S(1)}, f32[128,128]{1,0:T(8,128)S(1)}, u32[]{:S(2)}, u32[]{:S(2)}) collective-permute-start(f32[128,128]{1,0:T(8,128)S(1)} %shard_map.51.refs_0_), channel_id=1, source_target_pairs={{0,2},{1,3},{2,0},{3,1},{4,6},{5,7},{6,4},{7,5},{8,10},{9,11},{10,... | collective-permute-start | bytes 196616 | tf_op jit(solution)/shard_map/ppermute | solution.py:30
  44.2 4.1 %collective-permute-start.5 = (f32[128,128]{1,0:T(8,128)S(1)}, f32[128,128]{1,0:T(8,128)S(1)}, u32[]{:S(2)}, u32[]{:S(2)}) collective-permute-start(f32[128,128]{1,0:T(8,128)S(1)} %shard_map.51.refs_0_), channel_id=1, source_target_pairs={{0,1},{1,0},{2,3},{3,2},{4,5},{5,4},{6,7},{7,6},{8,9},{9,8},{10,11... | collective-permute-start | bytes 196616 | tf_op jit(solution)/shard_map/ppermute | solution.py:30
  53.8 0.6 copy-start.1
  54.4 2.0 %copy-start.11 = (bf16[128,16384]{1,0:T(8,128)(2,1)}, bf16[128,16384]{1,0:T(8,128)(2,1)S(1)}, u32[]{:S(2)}) copy-start(bf16[128,16384]{1,0:T(8,128)(2,1)S(1)} %collective-permute-done.8.near) | copy-start | bytes 12582916
  56.4 5.2 %copy-start.2 = (bf16[64,256]{1,0:T(8,128)(2,1)S(1)}, bf16[64,256]{1,0:T(8,128)(2,1)}, u32[]{:S(2)}) copy-start(bf16[64,256]{1,0:T(8,128)(2,1)} %copy-done.1) | copy-start | bytes 98308
  60.1 15.0 %collective-permute-start.10 = (bf16[32,8192]{1,0:T(8,128)(2,1)}, bf16[32,8192]{1,0:T(8,128)(2,1)S(1)}, u32[]{:S(2)}, u32[]{:S(2)}) collective-permute-start(bf16[32,8192]{1,0:T(8,128)(2,1)} %get-tuple-element.57), channel_id=1, source_target_pairs={{0,2},{1,3},{2,0},{3,1},{4,6},{5,7},{6,4},{7,5},{8,10},{9,11},{10,... | collective-permute-start | bytes 1572872 | tf_op jit(solution)/shard_map/ppermute | solution.py:447
  61.6 0.7 copy-start.6
  62.3 12.9 %copy-start.3 = (bf16[32,8192]{1,0:T(8,128)(2,1)S(1)}, bf16[32,8192]{1,0:T(8,128)(2,1)}, u32[]{:S(2)}) copy-start(bf16[32,8192]{1,0:T(8,128)(2,1)} %get-tuple-element.56.refs_0_) | copy-start | bytes 1572868
  67.3 19.1 %collective-permute-start.12 = (bf16[32,8192]{1,0:T(8,128)(2,1)S(1)}, bf16[32,8192]{1,0:T(8,128)(2,1)S(1)}, u32[]{:S(2)}, u32[]{:S(2)}) collective-permute-start(bf16[32,8192]{1,0:T(8,128)(2,1)S(1)} %get-tuple-element.64), channel_id=1, source_target_pairs={{0,2},{1,3},{2,0},{3,1},{4,6},{5,7},{6,4},{7,5},{8,10},{9,11},{10,... | collective-permute-start | bytes 1572872 | tf_op jit(solution)/shard_map/ppermute | solution.py:447
  81.0 16.6 %collective-permute-start.11 = (bf16[32,8192]{1,0:T(8,128)(2,1)S(1)}, bf16[32,8192]{1,0:T(8,128)(2,1)S(1)}, u32[]{:S(2)}, u32[]{:S(2)}) collective-permute-start(bf16[32,8192]{1,0:T(8,128)(2,1)S(1)} %get-tuple-element.62), channel_id=1, source_target_pairs={{0,2},{1,3},{2,0},{3,1},{4,6},{5,7},{6,4},{7,5},{8,10},{9,11},{10,... | collective-permute-start | bytes 1572872 | tf_op jit(solution)/shard_map/ppermute | solution.py:447
  92.2 16.6 %collective-permute-start.14 = (bf16[32,8192]{1,0:T(8,128)(2,1)S(1)}, bf16[32,8192]{1,0:T(8,128)(2,1)S(1)}, u32[]{:S(2)}, u32[]{:S(2)}) collective-permute-start(bf16[32,8192]{1,0:T(8,128)(2,1)S(1)} %get-tuple-element.74), channel_id=1, source_target_pairs={{0,2},{1,3},{2,0},{3,1},{4,6},{5,7},{6,4},{7,5},{8,10},{9,11},{10,... | collective-permute-start | bytes 1572872 | tf_op jit(solution)/shard_map/ppermute | solution.py:447
  103.5 16.6 %collective-permute-start.13 = (bf16[32,8192]{1,0:T(8,128)(2,1)S(1)}, bf16[32,8192]{1,0:T(8,128)(2,1)S(1)}, u32[]{:S(2)}, u32[]{:S(2)}) collective-permute-start(bf16[32,8192]{1,0:T(8,128)(2,1)S(1)} %get-tuple-element.72), channel_id=1, source_target_pairs={{0,2},{1,3},{2,0},{3,1},{4,6},{5,7},{6,4},{7,5},{8,10},{9,11},{10,... | collective-permute-start | bytes 1572872 | tf_op jit(solution)/shard_map/ppermute | solution.py:447
  114.7 16.6 %collective-permute-start.16 = (bf16[32,8192]{1,0:T(8,128)(2,1)S(1)}, bf16[32,8192]{1,0:T(8,128)(2,1)S(1)}, u32[]{:S(2)}, u32[]{:S(2)}) collective-permute-start(bf16[32,8192]{1,0:T(8,128)(2,1)S(1)} %get-tuple-element.84), channel_id=1, source_target_pairs={{0,2},{1,3},{2,0},{3,1},{4,6},{5,7},{6,4},{7,5},{8,10},{9,11},{10,... | collective-permute-start | bytes 1572872 | tf_op jit(solution)/shard_map/ppermute | solution.py:447
  126.0 16.6 %collective-permute-start.15 = (bf16[32,8192]{1,0:T(8,128)(2,1)S(1)}, bf16[32,8192]{1,0:T(8,128)(2,1)S(1)}, u32[]{:S(2)}, u32[]{:S(2)}) collective-permute-start(bf16[32,8192]{1,0:T(8,128)(2,1)S(1)} %get-tuple-element.82), channel_id=1, source_target_pairs={{0,2},{1,3},{2,0},{3,1},{4,6},{5,7},{6,4},{7,5},{8,10},{9,11},{10,... | collective-permute-start | bytes 1572872 | tf_op jit(solution)/shard_map/ppermute | solution.py:447
  132.2 0.6 copy-start.8
  135.7 13.4 %collective-permute-start.18 = (bf16[32,4096]{1,0:T(8,128)(2,1)}, bf16[32,4096]{1,0:T(8,128)(2,1)S(1)}, u32[]{:S(2)}, u32[]{:S(2)}) collective-permute-start(bf16[32,4096]{1,0:T(8,128)(2,1)} %get-tuple-element.94), channel_id=1, source_target_pairs={{0,2},{1,3},{2,0},{3,1},{4,6},{5,7},{6,4},{7,5},{8,10},{9,11},{10,... | collective-permute-start | bytes 786440 | tf_op jit(solution)/shard_map/ppermute | solution.py:447
  142.6 0.7 copy-start.10
  144.1 0.6 copy-start.7
  144.7 4.3 %copy-start.4 = (bf16[32,4096]{1,0:T(8,128)(2,1)S(1)}, bf16[32,4096]{1,0:T(8,128)(2,1)}, u32[]{:S(2)}) copy-start(bf16[32,4096]{1,0:T(8,128)(2,1)} %get-tuple-element.93.refs_0_) | copy-start | bytes 786436
  147.6 6.6 %copy-start.5 = (bf16[32,4096]{1,0:T(8,128)(2,1)S(1)}, bf16[32,4096]{1,0:T(8,128)(2,1)}, u32[]{:S(2)}) copy-start(bf16[32,4096]{1,0:T(8,128)(2,1)} %get-tuple-element.91.refs_0_) | copy-start | bytes 786436
  147.6 6.6 %collective-permute-start.17 = (bf16[32,4096]{1,0:T(8,128)(2,1)}, bf16[32,4096]{1,0:T(8,128)(2,1)S(1)}, u32[]{:S(2)}, u32[]{:S(2)}) collective-permute-start(bf16[32,4096]{1,0:T(8,128)(2,1)} %get-tuple-element.92), channel_id=1, source_target_pairs={{0,2},{1,3},{2,0},{3,1},{4,6},{5,7},{6,4},{7,5},{8,10},{9,11},{10,... | collective-permute-start | bytes 786440 | tf_op jit(solution)/shard_map/ppermute | solution.py:447
  149.1 0.7 copy-start.9

commit v2 on v1

v2 whole, which is shorter than its diff:
```python
import functools
import math

import jax
import jax.numpy as jnp
from jax import lax
from jax.experimental import pallas as pl
from jax.experimental.pallas import tpu as pltpu
from jax.sharding import PartitionSpec as P

F32 = jnp.float32
BF16 = jnp.bfloat16
HIGHEST = lax.Precision.HIGHEST
TILE = 128
WIDTH = 256
REACH = 64
EDGE = 4096
VMEM = pl.BlockSpec(memory_space=pltpu.VMEM)


COST = pl.CostEstimate(flops=1, bytes_accessed=1, transcendentals=0)


def params(limit=56):
    return pltpu.CompilerParams(vmem_limit_bytes=limit * 2**20)


def partner(x, axis, shift):
    count = lax.axis_size(axis)
    return lax.ppermute(x, axis, [(i, i ^ shift) for i in range(count)])


def gather(x, axis):
    count = lax.axis_size(axis)
    if count & (count - 1):
        every = lax.all_gather(x, axis)
        return [every[k] for k in range(count)]
    return [x] + [partner(x, axis, shift) for shift in range(1, count)]


def spread(x, axis):
    count = lax.axis_size(axis)
    if count & (count - 1):
        return [lax.psum(x, axis)]
    shift = count // 2
    while shift >= 4:
        x = x + partner(x, axis, shift)
        shift //= 2
    return [x] + [partner(x, axis, s) for s in range(1, min(count, 4))]


def pairwise(parts):
    while len(parts) > 1:
        odd = [parts[-1]] if len(parts) % 2 else []
        parts = [a + b for a, b in zip(parts[::2], parts[1::2])] + odd
    return parts[0]


def band_of(taps):
    wide = jnp.broadcast_to(taps, (WIDTH, 2 * WIDTH))
    return pltpu.roll(wide, 0, 1, stride=1, stride_axis=0).T.astype(BF16)


def clean(before, block, after, band):
    ext = jnp.concatenate([before, block, after], axis=1)
    rows, bins = block.shape
    starts = range(0, bins, WIDTH)
    lhs = jnp.concatenate([ext[:, a : a + 2 * WIDTH] for a in starts], axis=0)
    base = jnp.dot(lhs, band, preferred_element_type=F32)
    mid = jnp.concatenate([block[:, a : a + WIDTH] for a in starts], axis=0)
    out = (mid.astype(F32) - base).astype(BF16)
    return jnp.concatenate([out[i * rows : (i + 1) * rows] for i in range(bins // WIDTH)], axis=1)


def sketch_kernel(steps, taps, block, prev, after, low, high, probes, sketch, band, edges):
    i = pl.program_id(0)

    @pl.when(i == 0)
    def _():
        band[...] = band_of(taps[...])
        sketch[...] = jnp.zeros_like(sketch)

    cleaned = clean(
        jnp.where(i == 0, low[...], prev[...]),
        block[...],
        jnp.where(i == steps - 1, high[...], after[...]),
        band[...],
    )
    sketch[...] += jnp.dot(cleaned, probes[...], preferred_element_type=F32)

    width = edges.shape[1] // 2

    @pl.when(i == 0)
    def _():
        edges[:, :width] = cleaned[:, :width]

    @pl.when(i == steps - 1)
    def _():
        edges[:, width:] = cleaned[:, -width:]


ANY = pl.BlockSpec(memory_space=pl.ANY)


def whole(shape):
    return pl.BlockSpec(shape, lambda i: (0, 0))


def block_specs(rows, size, first, last):
    per = size // TILE
    return [
        pl.BlockSpec((rows, size), lambda i: (0, first + i)),
        pl.BlockSpec((rows, TILE), lambda i: (0, jnp.maximum((first + i) * per - 1, 0))),
        pl.BlockSpec((rows, TILE), lambda i: (0, jnp.minimum((first + i + 1) * per, last))),
    ]


def sketch_of(taps, spectra, low, high, probes, edge):
    rows, bins = spectra.shape
    size = math.gcd(bins, 8192)
    steps = bins // size
    columns = probes.shape[1]
    return pl.pallas_call(
        functools.partial(sketch_kernel, steps),
        grid=(steps,),
        in_specs=[whole(taps.shape)]
        + block_specs(rows, size, 0, bins // TILE - 1)
        + [whole(low.shape), whole(high.shape)]
        + [pl.BlockSpec((size, columns), lambda i: (i, 0))],
        out_specs=[
            whole((rows, columns)),
            whole((2 * WIDTH, WIDTH)),
            whole((rows, 2 * edge)),
        ],
        out_shape=[
            jax.ShapeDtypeStruct((rows, columns), F32),
            jax.ShapeDtypeStruct((2 * WIDTH, WIDTH), BF16),
            jax.ShapeDtypeStruct((rows, 2 * edge), BF16),
        ],
        cost_estimate=COST,
        compiler_params=params(48),
    )(taps, spectra, spectra, spectra, low, high, probes)


def total_kernel(*refs):
    refs[-1][...] = pairwise([part[...] for part in refs[:-1]])


def total_of(parts):
    return pl.pallas_call(
        total_kernel,
        in_specs=[VMEM] * len(parts),
        out_specs=VMEM,
        out_shape=jax.ShapeDtypeStruct(parts[0].shape, F32),
        cost_estimate=COST,
        compiler_params=params(32),
    )(*parts)


def inverse_factor(gram):
    size = gram.shape[0]
    groups = range(size // 8)
    rows = [gram[8 * g : 8 * g + 8] for g in groups]
    lane = lax.broadcasted_iota(jnp.int32, (8, size), 1)
    sub = lax.broadcasted_iota(jnp.int32, (8, size), 0)

    def row_of(x, k):
        return jnp.broadcast_to(x[k : k + 1], (8, size))

    result = []
    for g in groups:
        inside = (lane >= 8 * g) & (lane < 8 * g + 8)
        below = groups[g:]
        cols = {
            h: [
                jnp.broadcast_to(rows[h][:, 8 * g + k : 8 * g + k + 1], (8, size))
                for k in range(8)
            ]
            for h in below
        }
        for h in below:
            unit = jnp.where(lane - 8 * g == sub, 1.0, 0.0) if h == g else 0.0
            rows[h] = jnp.where(inside, unit, rows[h])
        pivots = jnp.ones((8, size), F32)
        for k in range(8):
            pivot = row_of(cols[g][k], k)
            scale = 1.0 / pivot
            pivots = jnp.where(sub == k, pivot, pivots)
            line = row_of(rows[g], k) * scale
            heads = {m: row_of(cols[g][m], k) * scale for m in range(k + 1, 8)}
            for h in below:
                c = cols[h][k]
                if h == g:
                    c = jnp.where(sub > k, c, 0.0)
                rows[h] = rows[h] - c * line
                for m in range(k + 1, 8):
                    cols[h][m] = cols[h][m] - c * heads[m]
        result.append(jnp.where(lane < 8 * g + 8, rows[g] * lax.rsqrt(pivots), 0.0))
    return jnp.concatenate(result, axis=0)


def basis_kernel(chips, factor, count, *refs):
    own, near, basis, turned = refs[count : count + 4]
    outs, held, sems = refs[count + 4 : -2], refs[-2], refs[-1]
    rows, edge = held.shape[0] // 2, held.shape[1]
    copies = [
        pltpu.make_async_copy(
            one, held.at[pl.ds(n * rows, rows), :], sems.at[n]
        )
        for n, one in enumerate((own, near))
    ]
    for copy in copies:
        copy.start()
    sketches = [ref[...] for ref in refs[:count]]
    size = sketches[0].shape[1]
    grams = [
        lax.dot_general(
            one, one, (((0,), (0,)), ((), ())), precision=HIGHEST, preferred_element_type=F32
        )
        for one in sketches
    ]
    inverse = inverse_factor(pairwise(grams) / float(rows * len(sketches)))
    both = jnp.concatenate(sketches[:2], axis=0)
    across = lax.dot_general(
        inverse, both, (((1,), (1,)), ((), ())), precision=HIGHEST, preferred_element_type=F32
    )
    basis[...] = across[:, :rows].T.astype(BF16)
    share = size // (2 * chips)
    me = lax.axis_index("pix")
    shape = (size // 2, size)
    to = lax.broadcasted_iota(jnp.int32, shape, 0)
    source = lax.broadcasted_iota(jnp.int32, shape, 1)
    chip = lax.rem(to // share + me // 2, chips)
    wanted = (2 * chip + lax.rem(me, 2)) * share + lax.rem(to, share)
    pick = jnp.where(wanted == source, 1.0, 0.0).astype(BF16)
    turned[...] = jnp.dot(pick, across.astype(BF16), preferred_element_type=F32).astype(BF16)
    for copy in copies:
        copy.wait()
    for n in range(2):
        side = slice(n * edge // 2, (n + 1) * edge // 2)
        put_parts(turned, held[:, side], factor, outs[n * chips : (n + 1) * chips])


def basis_of(sketches, own, near, factor, chips):
    rows, size = sketches[0].shape
    edge = own.shape[1]
    share = size // (2 * chips)
    return pl.pallas_call(
        functools.partial(basis_kernel, chips, factor, len(sketches)),
        in_specs=[VMEM] * len(sketches) + [ANY] * 2,
        out_specs=[VMEM] * (2 + 2 * chips),
        out_shape=[
            jax.ShapeDtypeStruct((rows, size), BF16),
            jax.ShapeDtypeStruct((size // 2, 2 * rows), BF16),
        ]
        + [jax.ShapeDtypeStruct((share, edge // 2), BF16)] * (2 * chips),
        scratch_shapes=[
            pltpu.VMEM((2 * rows, edge), BF16),
            pltpu.SemaphoreType.DMA((2,)),
        ],
        cost_estimate=COST,
        compiler_params=params(32),
    )(*sketches, own, near)


def put_parts(turned, cleaned, factor, outs):
    used = cleaned.shape[0]
    part = jnp.dot(turned[:, :used], cleaned, preferred_element_type=F32) * factor
    share = outs[0].shape[0]
    for k, out in enumerate(outs):
        out[...] = part[k * share : (k + 1) * share].astype(BF16)


def project_kernel(factor, chips, turned, band, *refs):
    blocks, outs, done = refs[:6], refs[-1 - 2 * chips : -1], refs[-1]
    done[...] = jnp.zeros_like(done)
    cleaned = clean_all(blocks, band[...])

    @pl.when(pl.program_id(0) == 0)
    def _():
        put_parts(turned, cleaned, factor, outs[:chips])

    @pl.when(pl.program_id(0) == 1)
    def _():
        put_parts(turned, cleaned, factor, outs[chips:])


def clean_all(blocks, band):
    return jnp.concatenate(
        [
            clean(blocks[n + 1][...], blocks[n][...], blocks[n + 2][...], band)
            for n in range(0, len(blocks), 3)
        ],
        axis=0,
    )


def project(turned, band, spectra, near, start, size, factor, chips, wait):
    rows, bins = spectra.shape
    share = turned.shape[0] // chips
    return pl.pallas_call(
        functools.partial(project_kernel, factor, chips),
        grid=(2,),
        in_specs=[whole(turned.shape), whole(band.shape)]
        + block_specs(rows, size, start // size, bins // TILE - 1) * 2
        + [ANY] * len(wait),
        out_specs=[whole((share, size))] * (2 * chips) + [whole((8, TILE))],
        out_shape=[jax.ShapeDtypeStruct((share, size), BF16)] * (2 * chips)
        + [jax.ShapeDtypeStruct((8, TILE), F32)],
        cost_estimate=COST,
        compiler_params=params(50),
    )(turned, band, spectra, spectra, spectra, near, near, near, *wait)


def finish_kernel(blocks, count, *refs):
    out, done = refs[-2], refs[-1]
    done[...] = jnp.zeros_like(done)
    for n in range(blocks):

        @pl.when(pl.program_id(0) == n)
        def _():
            parts = refs[n * count : (n + 1) * count]
            out[...] = pairwise([part[...].astype(F32) for part in parts]).astype(BF16)


def finish(out, blocks, starts, bins, wait):
    parts = [part for block in blocks for part in block]
    share, size = parts[0].shape
    extra = [] if out is None else [out]
    return pl.pallas_call(
        functools.partial(finish_kernel, len(blocks), len(blocks[0])),
        grid=(len(blocks),),
        in_specs=[whole((share, size))] * len(parts) + [ANY] * (len(extra) + len(wait)),
        out_specs=[
            pl.BlockSpec(
                (share, size), lambda i: (0, jnp.where(i == 0, *[at // size for at in starts]))
            ),
            whole((8, TILE)),
        ],
        out_shape=[
            jax.ShapeDtypeStruct((share, bins), BF16),
            jax.ShapeDtypeStruct((8, TILE), F32),
        ],
        input_output_aliases={len(parts): 0} if extra else {},
        cost_estimate=COST,
        compiler_params=params(32),
    )(*parts, *extra, *wait)


def per_device(spectra, kernel, probes):
    rows, bins = spectra.shape
    pix = lax.axis_size("pix")
    depth = lax.axis_size("mz")
    chips = pix // 2
    factor = 1.0 / math.sqrt(float(rows * pix))

    up = [(i, i + 1) for i in range(depth - 1)]
    down = [(i + 1, i) for i in range(depth - 1)]
    low = lax.ppermute(spectra[:, bins - TILE :], "mz", up)
    high = lax.ppermute(spectra[:, :TILE], "mz", down)
    taps = jnp.pad(kernel.astype(F32), (REACH, 2 * WIDTH - REACH - kernel.shape[0]))[None]

    near = partner(spectra, "pix", 1)
    edge = math.gcd(bins // 2, EDGE)
    partial_sketch, band, edges = sketch_of(taps, spectra, low, high, probes, edge)
    near_edges = partner(edges, "pix", 1)
    sketch = total_of(spread(partial_sketch, "mz"))
    basis, turned, *mine = basis_of(
        gather(sketch, "pix"), edges, near_edges, factor, chips
    )

    routes = [
        [
            (2 * chip + core, 2 * ((chip + k) % chips) + core)
            for chip in range(chips)
            for core in range(2)
        ]
        for k in range(chips)
    ]

    def across(mine):
        return [mine[0]] + [lax.ppermute(mine[m], "pix", routes[m]) for m in range(1, chips)]

    def across(mine):
        return [mine[0]] + [lax.ppermute(mine[m], "pix", routes[m]) for m in range(1, chips)]

    out, recent = None, []
    before = ([across(mine[:chips]), across(mine[chips:])], (0, bins - edge))
    for start in range(edge, bins - edge, 2 * edge):
        *mine, done = project(turned, band, spectra, near, start, edge, factor, chips, recent)
        blocks = [across(mine[:chips]), across(mine[chips:])]
        out, done = finish(out, *before, bins, [done])
        recent = [done]
        before = (blocks, (start, start + edge))
    out, done = finish(out, *before, bins, recent)
    return (basis, out)


def solution(mesh):
    in_specs = (P(("groups", "pix"), "mz"), P(), P("mz", None))
    out_specs = (P(("groups", "pix"), None), P(("groups", "pix"), "mz"))
    return jax.shard_map(
        per_device, mesh=mesh, in_specs=in_specs, out_specs=out_specs, check_vma=False
    )
```

time: 155 us -> 146 us (0.942)
  local copies, waits for them, and re-layouts: 8.57 us -> 0.78 us
  starting transfers between devices: 26.8 us -> 31.1 us
  Pallas kernels: 72.3 us -> 68.7 us
  waiting for transfers between devices: 45.9 us -> 43.5 us
    unnamed x24 -> x0, local copies, waits for them, and re-layouts: 7.79 us -> none
    ppermute x9 -> x16, starting transfers between devices: 12.6 us -> 16.7 us  [across(): lax.ppermute(mine[m], 'pix', routes[m])]
    pallas_call x19 -> x16, Pallas kernels: 52.5 us -> 49.4 us  [the longest x7 36.2 us: project(): pl.pallas_call(functools.partial(project_kernel, factor, chips), grid=(2,...]
    ppermute x9 -> x16, waiting for transfers between devices: 35.7 us -> 33.5 us  [across(): lax.ppermute(mine[m], 'pix', routes[m])]
  transfers between devices with their start and end apart: 19 -> 26, of which waited for: 13 -> 14; matrix products, arithmetic and copies ran while one was open for 1% -> 1% of each run, Pallas kernels for 46% -> 47%
where the time goes in v2:
time: 146 us
  Pallas kernels  68.7 us (47%)
  waiting for transfers between devices  43.5 us (30%)
  starting transfers between devices  31.1 us (21%)
    pallas_call x7, Pallas kernels, project(): pl.pallas_call(functools.partial(project_kernel, factor, chips), grid=(2,...  36.2 us
    ppermute x16, waiting for transfers between devices, across(): lax.ppermute(mine[m], 'pix', routes[m])  33.5 us
    pallas_call x1, Pallas kernels, sketch_of(): pl.pallas_call(functools.partial(sketch_kernel, steps), grid=(steps,), in...  19.3 us
    ppermute x16, starting transfers between devices, across(): lax.ppermute(mine[m], 'pix', routes[m])  16.7 us
    ppermute x8, waiting for transfers between devices, partner(): return lax.ppermute(x, axis, [(i, i ^ shift) for i in range(count)])  9.19 us
    ppermute x8, starting transfers between devices, partner(): return lax.ppermute(x, axis, [(i, i ^ shift) for i in range(count)])  8 us
    pallas_call x8, Pallas kernels, finish(): pl.pallas_call(functools.partial(finish_kernel, len(blocks), len(blocks[0...  6.86 us
    pallas_call x1, Pallas kernels, basis_of(): pl.pallas_call(functools.partial(basis_kernel, chips, factor, len(sketche...  6.27 us
  transfers between devices with their start and end apart: 26, of which 14 were waited for; matrix products, arithmetic and copies ran while one was open for 1% of the time, Pallas kernels for 47%

profile of v2, /device:TPU:0, one launch (start us, length us, event | category | flops | bytes accessed | tf_op | source)
XLA Modules:
  0.0 145.6 jit_solution(6398295826081876559)
XLA Ops:
  0.6 0.5 collective-permute-start.9
  1.1 0.8 fusion
  1.9 1.3 collective-permute-start.1
  3.2 5.1 %collective-permute-start = (bf16[128,128]{1,0:T(8,128)(2,1)S(1)}, bf16[128,128]{1,0:T(8,128)(2,1)S(1)}, u32[]{:S(2)}, u32[]{:S(2)}) collective-permute-start(bf16[128,128]{1,0:T(8,128)(2,1)S(1)} %get-tuple-element.121), channel_id=1, source_target_pairs={{0,4},{4,8},{8,12},{1,5},{5,9},{9,13},{2,6},{6,10},{10,14},{3,7},{... | collective-permute-start | bytes 98312 | tf_op jit(solution)/shard_map/ppermute | solution.py:359
  8.3 0.7 pad_convert_fusion
  9.1 0.8 collective-permute-done.low
  9.9 19.3 %shard_map.50 = (f32[128,128]{1,0:T(8,128)S(1)}, bf16[512,256]{1,0:T(8,128)(2,1)S(1)}, bf16[128,8192]{1,0:T(8,128)(2,1)S(1)}) custom-call(f32[1,512]{1,0:T(1,128)S(1)} %bitcast.1, bf16[128,65536]{1,0:T(8,128)(2,1)} %refs_2_.13, bf16[128,65536]{1,0:T(8,128)(2,1)} %refs_2_.13, bf16[128,65536]{1,0:T(8,128)(2,1)} %refs_2_.13, ...), custom_call_target="tpu_custom_call" | custom-call | flops 1 | bytes 1 | tf_op jit(solution)/shard_map/pallas_call | solution.py:123
  29.3 0.1 collective-permute-start.8
  29.3 4.8 %collective-permute-start.4 = (f32[128,128]{1,0:T(8,128)S(1)}, f32[128,128]{1,0:T(8,128)S(1)}, u32[]{:S(2)}, u32[]{:S(2)}) collective-permute-start(f32[128,128]{1,0:T(8,128)S(1)} %get-tuple-element.61.refs_0_), channel_id=1, source_target_pairs={{0,12},{4,8},{8,4},{12,0},{1,13},{5,9},{9,5},{13,1},{2,14},{6,10},... | collective-permute-start | bytes 196616 | tf_op jit(solution)/shard_map/ppermute | solution.py:30
  34.2 0.0 collective-permute-start.3
  34.2 0.6 collective-permute-start.2
  34.8 2.2 %collective-permute-done.4.refs_3_ = f32[128,128]{1,0:T(8,128)S(1)} collective-permute-done((f32[128,128]{1,0:T(8,128)S(1)}, f32[128,128]{1,0:T(8,128)S(1)}, u32[]{:S(2)}, u32[]{:S(2)}) %collective-permute-start.4) | collective-permute-done | bytes 65568 | tf_op jit(solution)/shard_map/ppermute | solution.py:30
  37.0 3.0 %collective-permute-done.3.refs_2_ = f32[128,128]{1,0:T(8,128)S(1)} collective-permute-done((f32[128,128]{1,0:T(8,128)S(1)}, f32[128,128]{1,0:T(8,128)S(1)}, u32[]{:S(2)}, u32[]{:S(2)}) %collective-permute-start.3) | collective-permute-done | bytes 65568 | tf_op jit(solution)/shard_map/ppermute | solution.py:30
  40.1 0.0 collective-permute-done.2.refs_1_
  40.1 1.0 collective-permute-start.7
  41.1 0.8 collective-permute-start.6
  41.9 0.1 collective-permute-start.5
  42.0 2.3 %collective-permute-done.7.refs_3_ = f32[128,128]{1,0:T(8,128)S(1)} collective-permute-done((f32[128,128]{1,0:T(8,128)S(1)}, f32[128,128]{1,0:T(8,128)S(1)}, u32[]{:S(2)}, u32[]{:S(2)}) %collective-permute-start.7) | collective-permute-done | bytes 65568 | tf_op jit(solution)/shard_map/ppermute | solution.py:30
  44.3 1.6 %collective-permute-done.6.refs_2_ = f32[128,128]{1,0:T(8,128)S(1)} collective-permute-done((f32[128,128]{1,0:T(8,128)S(1)}, f32[128,128]{1,0:T(8,128)S(1)}, u32[]{:S(2)}, u32[]{:S(2)}) %collective-permute-start.6) | collective-permute-done | bytes 65568 | tf_op jit(solution)/shard_map/ppermute | solution.py:30
  45.9 0.0 collective-permute-done.5.refs_1_
  46.0 0.0 collective-permute-done.8.refs_5_
  46.0 6.3 %shard_map.52 = (bf16[128,128]{1,0:T(8,128)(2,1)}, bf16[64,256]{1,0:T(8,128)(2,1)S(1)}, bf16[32,4096]{1,0:T(8,128)(2,1)S(1)}, bf16[32,4096]{1,0:T(8,128)(2,1)S(1...) custom-call(f32[128,128]{1,0:T(8,128)S(1)} %shard_map.51.refs_0_, ...), custom_call_target="tpu_custom_call" | custom-call | flops 1 | bytes 1 | tf_op jit(solution)/shard_map/pallas_call | solution.py:248
  52.2 1.4 collective-permute-start.12
  53.6 0.7 collective-permute-start.13
  54.3 5.2 %shard_map.53 = (bf16[32,4096]{1,0:T(8,128)(2,1)S(1)}, bf16[32,4096]{1,0:T(8,128)(2,1)S(1)}, bf16[32,4096]{1,0:T(8,128)(2,1)S(1)}, bf16[32,4096]{1,0:T(8,128)(2,1)S(1)}, f32[8,128]{1,0:T(8,128)S(1)}) custom-call(bf16[64,256]{1,0:T(8,128)(2,1)S(1)} %get-tuple-element.64.turned, bf16[512,256]{1,0:T(8,128)(2,1)S(1)} %get-tuple-element.65.band, ...), custom_call_target="tpu_custom_call" | custom-call | flops 1 | bytes 1 | tf_op jit(solution)/shard_map/pallas_call | solution.py:301
  59.5 1.4 collective-permute-start.10
  60.9 0.7 collective-permute-start.11
  61.6 5.5 %collective-permute-done.13.refs_3_ = bf16[32,4096]{1,0:T(8,128)(2,1)S(1)} collective-permute-done((bf16[32,4096]{1,0:T(8,128)(2,1)S(1)}, bf16[32,4096]{1,0:T(8,128)(2,1)S(1)}, u32[]{:S(2)}, u32[]{:S(2)}) %collective-permute-start.13) | collective-permute-done | bytes 262176 | tf_op jit(solution)/shard_map/ppermute | solution.py:385
  67.1 0.9 shard_map.54
  67.9 5.2 %shard_map.55 = (bf16[32,4096]{1,0:T(8,128)(2,1)S(1)}, bf16[32,4096]{1,0:T(8,128)(2,1)S(1)}, bf16[32,4096]{1,0:T(8,128)(2,1)S(1)}, bf16[32,4096]{1,0:T(8,128)(2,1)S(1)}, f32[8,128]{1,0:T(8,128)S(1)}) custom-call(bf16[64,256]{1,0:T(8,128)(2,1)S(1)} %get-tuple-element.64.turned, bf16[512,256]{1,0:T(8,128)(2,1)S(1)} %get-tuple-element.65.band, ...), custom_call_target="tpu_custom_call" | custom-call | flops 1 | bytes 1 | tf_op jit(solution)/shard_map/pallas_call | solution.py:301
  73.1 1.4 collective-permute-start.16
  74.5 0.7 collective-permute-start.17
  75.2 3.1 %collective-permute-done.11.refs_3_ = bf16[32,4096]{1,0:T(8,128)(2,1)S(1)} collective-permute-done((bf16[32,4096]{1,0:T(8,128)(2,1)S(1)}, bf16[32,4096]{1,0:T(8,128)(2,1)S(1)}, u32[]{:S(2)}, u32[]{:S(2)}) %collective-permute-start.11) | collective-permute-done | bytes 262176 | tf_op jit(solution)/shard_map/ppermute | solution.py:385
  78.3 0.9 shard_map.56
  79.2 5.2 %shard_map.57 = (bf16[32,4096]{1,0:T(8,128)(2,1)S(1)}, bf16[32,4096]{1,0:T(8,128)(2,1)S(1)}, bf16[32,4096]{1,0:T(8,128)(2,1)S(1)}, bf16[32,4096]{1,0:T(8,128)(2,1)S(1)}, f32[8,128]{1,0:T(8,128)S(1)}) custom-call(bf16[64,256]{1,0:T(8,128)(2,1)S(1)} %get-tuple-element.64.turned, bf16[512,256]{1,0:T(8,128)(2,1)S(1)} %get-tuple-element.65.band, ...), custom_call_target="tpu_custom_call" | custom-call | flops 1 | bytes 1 | tf_op jit(solution)/shard_map/pallas_call | solution.py:301
  84.4 1.4 collective-permute-start.14
  85.8 0.7 collective-permute-start.15
  86.5 0.0 collective-permute-done.16.refs_1_
  86.5 3.1 %collective-permute-done.17.refs_3_ = bf16[32,4096]{1,0:T(8,128)(2,1)S(1)} collective-permute-done((bf16[32,4096]{1,0:T(8,128)(2,1)S(1)}, bf16[32,4096]{1,0:T(8,128)(2,1)S(1)}, u32[]{:S(2)}, u32[]{:S(2)}) %collective-permute-start.17) | collective-permute-done | bytes 262176 | tf_op jit(solution)/shard_map/ppermute | solution.py:385
  89.6 0.9 shard_map.58
  90.4 5.2 %shard_map.59 = (bf16[32,4096]{1,0:T(8,128)(2,1)S(1)}, bf16[32,4096]{1,0:T(8,128)(2,1)S(1)}, bf16[32,4096]{1,0:T(8,128)(2,1)S(1)}, bf16[32,4096]{1,0:T(8,128)(2,1)S(1)}, f32[8,128]{1,0:T(8,128)S(1)}) custom-call(bf16[64,256]{1,0:T(8,128)(2,1)S(1)} %get-tuple-element.64.turned, bf16[512,256]{1,0:T(8,128)(2,1)S(1)} %get-tuple-element.65.band, ...), custom_call_target="tpu_custom_call" | custom-call | flops 1 | bytes 1 | tf_op jit(solution)/shard_map/pallas_call | solution.py:301
  95.6 1.4 collective-permute-start.20
  97.0 0.7 collective-permute-start.21
  97.7 0.0 collective-permute-done.14.refs_1_
  97.7 3.1 %collective-permute-done.15.refs_3_ = bf16[32,4096]{1,0:T(8,128)(2,1)S(1)} collective-permute-done((bf16[32,4096]{1,0:T(8,128)(2,1)S(1)}, bf16[32,4096]{1,0:T(8,128)(2,1)S(1)}, u32[]{:S(2)}, u32[]{:S(2)}) %collective-permute-start.15) | collective-permute-done | bytes 262176 | tf_op jit(solution)/shard_map/ppermute | solution.py:385
  100.8 0.9 shard_map.60
  101.6 5.2 %shard_map.61 = (bf16[32,4096]{1,0:T(8,128)(2,1)S(1)}, bf16[32,4096]{1,0:T(8,128)(2,1)S(1)}, bf16[32,4096]{1,0:T(8,128)(2,1)S(1)}, bf16[32,4096]{1,0:T(8,128)(2,1)S(1)}, f32[8,128]{1,0:T(8,128)S(1)}) custom-call(bf16[64,256]{1,0:T(8,128)(2,1)S(1)} %get-tuple-element.64.turned, bf16[512,256]{1,0:T(8,128)(2,1)S(1)} %get-tuple-element.65.band, ...), custom_call_target="tpu_custom_call" | custom-call | flops 1 | bytes 1 | tf_op jit(solution)/shard_map/pallas_call | solution.py:301
  106.8 1.4 collective-permute-start.18
  108.2 0.7 collective-permute-start.19
  108.9 3.1 %collective-permute-done.21.refs_3_ = bf16[32,4096]{1,0:T(8,128)(2,1)S(1)} collective-permute-done((bf16[32,4096]{1,0:T(8,128)(2,1)S(1)}, bf16[32,4096]{1,0:T(8,128)(2,1)S(1)}, u32[]{:S(2)}, u32[]{:S(2)}) %collective-permute-start.21) | collective-permute-done | bytes 262176 | tf_op jit(solution)/shard_map/ppermute | solution.py:385
  112.0 0.9 shard_map.62
  112.9 5.2 %shard_map.63 = (bf16[32,4096]{1,0:T(8,128)(2,1)S(1)}, bf16[32,4096]{1,0:T(8,128)(2,1)S(1)}, bf16[32,4096]{1,0:T(8,128)(2,1)S(1)}, bf16[32,4096]{1,0:T(8,128)(2,1)S(1)}, f32[8,128]{1,0:T(8,128)S(1)}) custom-call(bf16[64,256]{1,0:T(8,128)(2,1)S(1)} %get-tuple-element.64.turned, bf16[512,256]{1,0:T(8,128)(2,1)S(1)} %get-tuple-element.65.band, ...), custom_call_target="tpu_custom_call" | custom-call | flops 1 | bytes 1 | tf_op jit(solution)/shard_map/pallas_call | solution.py:301
  118.1 1.4 collective-permute-start.24
  119.5 0.7 collective-permute-start.25
  120.2 3.1 %collective-permute-done.19.refs_3_ = bf16[32,4096]{1,0:T(8,128)(2,1)S(1)} collective-permute-done((bf16[32,4096]{1,0:T(8,128)(2,1)S(1)}, bf16[32,4096]{1,0:T(8,128)(2,1)S(1)}, u32[]{:S(2)}, u32[]{:S(2)}) %collective-permute-start.19) | collective-permute-done | bytes 262176 | tf_op jit(solution)/shard_map/ppermute | solution.py:385
  123.3 0.9 shard_map.64
  124.1 5.2 %shard_map.65 = (bf16[32,4096]{1,0:T(8,128)(2,1)S(1)}, bf16[32,4096]{1,0:T(8,128)(2,1)S(1)}, bf16[32,4096]{1,0:T(8,128)(2,1)S(1)}, bf16[32,4096]{1,0:T(8,128)(2,1)S(1)}, f32[8,128]{1,0:T(8,128)S(1)}) custom-call(bf16[64,256]{1,0:T(8,128)(2,1)S(1)} %get-tuple-element.64.turned, bf16[512,256]{1,0:T(8,128)(2,1)S(1)} %get-tuple-element.65.band, ...), custom_call_target="tpu_custom_call" | custom-call | flops 1 | bytes 1 | tf_op jit(solution)/shard_map/pallas_call | solution.py:301
  129.3 1.4 collective-permute-start.22
  130.7 0.7 collective-permute-start.23
  131.4 3.1 %collective-permute-done.25.refs_3_ = bf16[32,4096]{1,0:T(8,128)(2,1)S(1)} collective-permute-done((bf16[32,4096]{1,0:T(8,128)(2,1)S(1)}, bf16[32,4096]{1,0:T(8,128)(2,1)S(1)}, u32[]{:S(2)}, u32[]{:S(2)}) %collective-permute-start.25) | collective-permute-done | bytes 262176 | tf_op jit(solution)/shard_map/ppermute | solution.py:385
  134.5 0.9 shard_map.66
  135.4 4.8 %collective-permute-done.22.refs_1_ = bf16[32,4096]{1,0:T(8,128)(2,1)S(1)} collective-permute-done((bf16[32,4096]{1,0:T(8,128)(2,1)S(1)}, bf16[32,4096]{1,0:T(8,128)(2,1)S(1)}, u32[]{:S(2)}, u32[]{:S(2)}) %collective-permute-start.22) | collective-permute-done | bytes 262176 | tf_op jit(solution)/shard_map/ppermute | solution.py:385
  140.1 4.7 %collective-permute-done.23.refs_3_ = bf16[32,4096]{1,0:T(8,128)(2,1)S(1)} collective-permute-done((bf16[32,4096]{1,0:T(8,128)(2,1)S(1)}, bf16[32,4096]{1,0:T(8,128)(2,1)S(1)}, u32[]{:S(2)}, u32[]{:S(2)}) %collective-permute-start.23) | collective-permute-done | bytes 262176 | tf_op jit(solution)/shard_map/ppermute | solution.py:385
  144.8 0.9 shard_map.67
  (8 shorter events, 0.0 us)
Async XLA Ops:
  0.6 53.7 %collective-permute-start.9 = (bf16[128,65536]{1,0:T(8,128)(2,1)}, bf16[128,65536]{1,0:T(8,128)(2,1)}, u32[]{:S(2)}, u32[]{:S(2)}) collective-permute-start(bf16[128,65536]{1,0:T(8,128)(2,1)} %refs_2_.13), channel_id=1, source_target_pairs={{0,1},{1,0},{2,3},{3,2},{4,5},{5,4},{6,7},{7,6},{8,9},{9,8},{10,11... | collective-permute-start | bytes 50331656 | tf_op jit(solution)/shard_map/ppermute | solution.py:30
  1.9 7.2 %collective-permute-start.1 = (bf16[128,128]{1,0:T(8,128)(2,1)S(1)}, bf16[128,128]{1,0:T(8,128)(2,1)S(1)}, u32[]{:S(2)}, u32[]{:S(2)}) collective-permute-start(bf16[128,128]{1,0:T(8,128)(2,1)S(1)} %get-tuple-element.120), channel_id=1, source_target_pairs={{4,0},{8,4},{12,8},{5,1},{9,5},{13,9},{6,2},{10,6},{14,10},{7,3},{... | collective-permute-start | bytes 98312 | tf_op jit(solution)/shard_map/ppermute | solution.py:360
  3.2 6.7 %collective-permute-start = (bf16[128,128]{1,0:T(8,128)(2,1)S(1)}, bf16[128,128]{1,0:T(8,128)(2,1)S(1)}, u32[]{:S(2)}, u32[]{:S(2)}) collective-permute-start(bf16[128,128]{1,0:T(8,128)(2,1)S(1)} %get-tuple-element.121), channel_id=1, source_target_pairs={{0,4},{4,8},{8,12},{1,5},{5,9},{9,13},{2,6},{6,10},{10,14},{3,7},{... | collective-permute-start | bytes 98312 | tf_op jit(solution)/shard_map/ppermute | solution.py:359
  29.3 16.7 %collective-permute-start.8 = (bf16[128,8192]{1,0:T(8,128)(2,1)S(1)}, bf16[128,8192]{1,0:T(8,128)(2,1)S(1)}, u32[]{:S(2)}, u32[]{:S(2)}) collective-permute-start(bf16[128,8192]{1,0:T(8,128)(2,1)S(1)} %get-tuple-element.62.refs_4_), channel_id=1, source_target_pairs={{0,1},{1,0},{2,3},{3,2},{4,5},{5,4},{6,7},{7,6},{8,9},{9,8},{10,11... | collective-permute-start | bytes 6291464 | tf_op jit(solution)/shard_map/ppermute | solution.py:30
  29.3 7.7 %collective-permute-start.4 = (f32[128,128]{1,0:T(8,128)S(1)}, f32[128,128]{1,0:T(8,128)S(1)}, u32[]{:S(2)}, u32[]{:S(2)}) collective-permute-start(f32[128,128]{1,0:T(8,128)S(1)} %get-tuple-element.61.refs_0_), channel_id=1, source_target_pairs={{0,12},{4,8},{8,4},{12,0},{1,13},{5,9},{9,5},{13,1},{2,14},{6,10},... | collective-permute-start | bytes 196616 | tf_op jit(solution)/shard_map/ppermute | solution.py:30
  34.2 5.9 %collective-permute-start.3 = (f32[128,128]{1,0:T(8,128)S(1)}, f32[128,128]{1,0:T(8,128)S(1)}, u32[]{:S(2)}, u32[]{:S(2)}) collective-permute-start(f32[128,128]{1,0:T(8,128)S(1)} %get-tuple-element.61.refs_0_), channel_id=1, source_target_pairs={{0,8},{4,12},{8,0},{12,4},{1,9},{5,13},{9,1},{13,5},{2,10},{6,14},... | collective-permute-start | bytes 196616 | tf_op jit(solution)/shard_map/ppermute | solution.py:30
  34.2 5.9 %collective-permute-start.2 = (f32[128,128]{1,0:T(8,128)S(1)}, f32[128,128]{1,0:T(8,128)S(1)}, u32[]{:S(2)}, u32[]{:S(2)}) collective-permute-start(f32[128,128]{1,0:T(8,128)S(1)} %get-tuple-element.61.refs_0_), channel_id=1, source_target_pairs={{0,4},{4,0},{8,12},{12,8},{1,5},{5,1},{9,13},{13,9},{2,6},{6,2},{1... | collective-permute-start | bytes 196616 | tf_op jit(solution)/shard_map/ppermute | solution.py:30
  40.1 4.2 %collective-permute-start.7 = (f32[128,128]{1,0:T(8,128)S(1)}, f32[128,128]{1,0:T(8,128)S(1)}, u32[]{:S(2)}, u32[]{:S(2)}) collective-permute-start(f32[128,128]{1,0:T(8,128)S(1)} %shard_map.51.refs_0_), channel_id=1, source_target_pairs={{0,3},{1,2},{2,1},{3,0},{4,7},{5,6},{6,5},{7,4},{8,11},{9,10},{10,... | collective-permute-start | bytes 196616 | tf_op jit(solution)/shard_map/ppermute | solution.py:30
  41.1 4.9 %collective-permute-start.6 = (f32[128,128]{1,0:T(8,128)S(1)}, f32[128,128]{1,0:T(8,128)S(1)}, u32[]{:S(2)}, u32[]{:S(2)}) collective-permute-start(f32[128,128]{1,0:T(8,128)S(1)} %shard_map.51.refs_0_), channel_id=1, source_target_pairs={{0,2},{1,3},{2,0},{3,1},{4,6},{5,7},{6,4},{7,5},{8,10},{9,11},{10,... | collective-permute-start | bytes 196616 | tf_op jit(solution)/shard_map/ppermute | solution.py:30
  41.9 4.0 %collective-permute-start.5 = (f32[128,128]{1,0:T(8,128)S(1)}, f32[128,128]{1,0:T(8,128)S(1)}, u32[]{:S(2)}, u32[]{:S(2)}) collective-permute-start(f32[128,128]{1,0:T(8,128)S(1)} %shard_map.51.refs_0_), channel_id=1, source_target_pairs={{0,1},{1,0},{2,3},{3,2},{4,5},{5,4},{6,7},{7,6},{8,9},{9,8},{10,11... | collective-permute-start | bytes 196616 | tf_op jit(solution)/shard_map/ppermute | solution.py:30
  52.2 9.4 %collective-permute-start.12 = (bf16[32,4096]{1,0:T(8,128)(2,1)S(1)}, bf16[32,4096]{1,0:T(8,128)(2,1)S(1)}, u32[]{:S(2)}, u32[]{:S(2)}) collective-permute-start(bf16[32,4096]{1,0:T(8,128)(2,1)S(1)} %get-tuple-element.71), channel_id=1, source_target_pairs={{0,2},{1,3},{2,0},{3,1},{4,6},{5,7},{6,4},{7,5},{8,10},{9,11},{10,... | collective-permute-start | bytes 786440 | tf_op jit(solution)/shard_map/ppermute | solution.py:385
  53.6 13.4 %collective-permute-start.13 = (bf16[32,4096]{1,0:T(8,128)(2,1)S(1)}, bf16[32,4096]{1,0:T(8,128)(2,1)S(1)}, u32[]{:S(2)}, u32[]{:S(2)}) collective-permute-start(bf16[32,4096]{1,0:T(8,128)(2,1)S(1)} %get-tuple-element.73), channel_id=1, source_target_pairs={{0,2},{1,3},{2,0},{3,1},{4,6},{5,7},{6,4},{7,5},{8,10},{9,11},{10,... | collective-permute-start | bytes 786440 | tf_op jit(solution)/shard_map/ppermute | solution.py:385
  59.5 15.7 %collective-permute-start.10 = (bf16[32,4096]{1,0:T(8,128)(2,1)S(1)}, bf16[32,4096]{1,0:T(8,128)(2,1)S(1)}, u32[]{:S(2)}, u32[]{:S(2)}) collective-permute-start(bf16[32,4096]{1,0:T(8,128)(2,1)S(1)} %get-tuple-element.67), channel_id=1, source_target_pairs={{0,2},{1,3},{2,0},{3,1},{4,6},{5,7},{6,4},{7,5},{8,10},{9,11},{10,... | collective-permute-start | bytes 786440 | tf_op jit(solution)/shard_map/ppermute | solution.py:385
  60.9 17.4 %collective-permute-start.11 = (bf16[32,4096]{1,0:T(8,128)(2,1)S(1)}, bf16[32,4096]{1,0:T(8,128)(2,1)S(1)}, u32[]{:S(2)}, u32[]{:S(2)}) collective-permute-start(bf16[32,4096]{1,0:T(8,128)(2,1)S(1)} %get-tuple-element.69), channel_id=1, source_target_pairs={{0,2},{1,3},{2,0},{3,1},{4,6},{5,7},{6,4},{7,5},{8,10},{9,11},{10,... | collective-permute-start | bytes 786440 | tf_op jit(solution)/shard_map/ppermute | solution.py:385
  73.1 13.3 %collective-permute-start.16 = (bf16[32,4096]{1,0:T(8,128)(2,1)S(1)}, bf16[32,4096]{1,0:T(8,128)(2,1)S(1)}, u32[]{:S(2)}, u32[]{:S(2)}) collective-permute-start(bf16[32,4096]{1,0:T(8,128)(2,1)S(1)} %get-tuple-element.84), channel_id=1, source_target_pairs={{0,2},{1,3},{2,0},{3,1},{4,6},{5,7},{6,4},{7,5},{8,10},{9,11},{10,... | collective-permute-start | bytes 786440 | tf_op jit(solution)/shard_map/ppermute | solution.py:385
  74.5 15.0 %collective-permute-start.17 = (bf16[32,4096]{1,0:T(8,128)(2,1)S(1)}, bf16[32,4096]{1,0:T(8,128)(2,1)S(1)}, u32[]{:S(2)}, u32[]{:S(2)}) collective-permute-start(bf16[32,4096]{1,0:T(8,128)(2,1)S(1)} %get-tuple-element.86), channel_id=1, source_target_pairs={{0,2},{1,3},{2,0},{3,1},{4,6},{5,7},{6,4},{7,5},{8,10},{9,11},{10,... | collective-permute-start | bytes 786440 | tf_op jit(solution)/shard_map/ppermute | solution.py:385
  84.4 13.3 %collective-permute-start.14 = (bf16[32,4096]{1,0:T(8,128)(2,1)S(1)}, bf16[32,4096]{1,0:T(8,128)(2,1)S(1)}, u32[]{:S(2)}, u32[]{:S(2)}) collective-permute-start(bf16[32,4096]{1,0:T(8,128)(2,1)S(1)} %get-tuple-element.80), channel_id=1, source_target_pairs={{0,2},{1,3},{2,0},{3,1},{4,6},{5,7},{6,4},{7,5},{8,10},{9,11},{10,... | collective-permute-start | bytes 786440 | tf_op jit(solution)/shard_map/ppermute | solution.py:385
  85.8 15.0 %collective-permute-start.15 = (bf16[32,4096]{1,0:T(8,128)(2,1)S(1)}, bf16[32,4096]{1,0:T(8,128)(2,1)S(1)}, u32[]{:S(2)}, u32[]{:S(2)}) collective-permute-start(bf16[32,4096]{1,0:T(8,128)(2,1)S(1)} %get-tuple-element.82), channel_id=1, source_target_pairs={{0,2},{1,3},{2,0},{3,1},{4,6},{5,7},{6,4},{7,5},{8,10},{9,11},{10,... | collective-permute-start | bytes 786440 | tf_op jit(solution)/shard_map/ppermute | solution.py:385
  95.6 13.3 %collective-permute-start.20 = (bf16[32,4096]{1,0:T(8,128)(2,1)S(1)}, bf16[32,4096]{1,0:T(8,128)(2,1)S(1)}, u32[]{:S(2)}, u32[]{:S(2)}) collective-permute-start(bf16[32,4096]{1,0:T(8,128)(2,1)S(1)} %get-tuple-element.98), channel_id=1, source_target_pairs={{0,2},{1,3},{2,0},{3,1},{4,6},{5,7},{6,4},{7,5},{8,10},{9,11},{10,... | collective-permute-start | bytes 786440 | tf_op jit(solution)/shard_map/ppermute | solution.py:385
  97.0 15.0 %collective-permute-start.21 = (bf16[32,4096]{1,0:T(8,128)(2,1)S(1)}, bf16[32,4096]{1,0:T(8,128)(2,1)S(1)}, u32[]{:S(2)}, u32[]{:S(2)}) collective-permute-start(bf16[32,4096]{1,0:T(8,128)(2,1)S(1)} %get-tuple-element.100), channel_id=1, source_target_pairs={{0,2},{1,3},{2,0},{3,1},{4,6},{5,7},{6,4},{7,5},{8,10},{9,11},{10,... | collective-permute-start | bytes 786440 | tf_op jit(solution)/shard_map/ppermute | solution.py:385
  106.8 13.3 %collective-permute-start.18 = (bf16[32,4096]{1,0:T(8,128)(2,1)S(1)}, bf16[32,4096]{1,0:T(8,128)(2,1)S(1)}, u32[]{:S(2)}, u32[]{:S(2)}) collective-permute-start(bf16[32,4096]{1,0:T(8,128)(2,1)S(1)} %get-tuple-element.94), channel_id=1, source_target_pairs={{0,2},{1,3},{2,0},{3,1},{4,6},{5,7},{6,4},{7,5},{8,10},{9,11},{10,... | collective-permute-start | bytes 786440 | tf_op jit(solution)/shard_map/ppermute | solution.py:385
  108.2 15.0 %collective-permute-start.19 = (bf16[32,4096]{1,0:T(8,128)(2,1)S(1)}, bf16[32,4096]{1,0:T(8,128)(2,1)S(1)}, u32[]{:S(2)}, u32[]{:S(2)}) collective-permute-start(bf16[32,4096]{1,0:T(8,128)(2,1)S(1)} %get-tuple-element.96), channel_id=1, source_target_pairs={{0,2},{1,3},{2,0},{3,1},{4,6},{5,7},{6,4},{7,5},{8,10},{9,11},{10,... | collective-permute-start | bytes 786440 | tf_op jit(solution)/shard_map/ppermute | solution.py:385
  118.1 13.3 %collective-permute-start.24 = (bf16[32,4096]{1,0:T(8,128)(2,1)S(1)}, bf16[32,4096]{1,0:T(8,128)(2,1)S(1)}, u32[]{:S(2)}, u32[]{:S(2)}) collective-permute-start(bf16[32,4096]{1,0:T(8,128)(2,1)S(1)} %get-tuple-element.112), channel_id=1, source_target_pairs={{0,2},{1,3},{2,0},{3,1},{4,6},{5,7},{6,4},{7,5},{8,10},{9,11},{10,... | collective-permute-start | bytes 786440 | tf_op jit(solution)/shard_map/ppermute | solution.py:385
  119.5 15.0 %collective-permute-start.25 = (bf16[32,4096]{1,0:T(8,128)(2,1)S(1)}, bf16[32,4096]{1,0:T(8,128)(2,1)S(1)}, u32[]{:S(2)}, u32[]{:S(2)}) collective-permute-start(bf16[32,4096]{1,0:T(8,128)(2,1)S(1)} %get-tuple-element.114), channel_id=1, source_target_pairs={{0,2},{1,3},{2,0},{3,1},{4,6},{5,7},{6,4},{7,5},{8,10},{9,11},{10,... | collective-permute-start | bytes 786440 | tf_op jit(solution)/shard_map/ppermute | solution.py:385
  129.3 10.8 %collective-permute-start.22 = (bf16[32,4096]{1,0:T(8,128)(2,1)S(1)}, bf16[32,4096]{1,0:T(8,128)(2,1)S(1)}, u32[]{:S(2)}, u32[]{:S(2)}) collective-permute-start(bf16[32,4096]{1,0:T(8,128)(2,1)S(1)} %get-tuple-element.108), channel_id=1, source_target_pairs={{0,2},{1,3},{2,0},{3,1},{4,6},{5,7},{6,4},{7,5},{8,10},{9,11},{10,... | collective-permute-start | bytes 786440 | tf_op jit(solution)/shard_map/ppermute | solution.py:385
  130.7 14.1 %collective-permute-start.23 = (bf16[32,4096]{1,0:T(8,128)(2,1)S(1)}, bf16[32,4096]{1,0:T(8,128)(2,1)S(1)}, u32[]{:S(2)}, u32[]{:S(2)}) collective-permute-start(bf16[32,4096]{1,0:T(8,128)(2,1)S(1)} %get-tuple-element.110), channel_id=1, source_target_pairs={{0,2},{1,3},{2,0},{3,1},{4,6},{5,7},{6,4},{7,5},{8,10},{9,11},{10,... | collective-permute-start | bytes 786440 | tf_op jit(solution)/shard_map/ppermute | solution.py:385

commit v3 on v2

--- a/solution.py
+++ b/solution.py
@@ -46,7 +46,9 @@
     while shift >= 4:
         x = x + partner(x, axis, shift)
         shift //= 2
-    return [x] + [partner(x, axis, s) for s in range(1, min(count, 4))]
+    if count >= 4:
+        x = total_of([x, partner(x, axis, 1)], [])
+    return [x, partner(x, axis, 2)]
 
 
 def pairwise(parts):
@@ -72,7 +74,7 @@
     return jnp.concatenate([out[i * rows : (i + 1) * rows] for i in range(bins // WIDTH)], axis=1)
 
 
-def sketch_kernel(steps, taps, block, prev, after, low, high, probes, sketch, band, edges):
+def sketch_kernel(steps, taps, block, prev, after, low, high, probes, sketch, band, first, final):
     i = pl.program_id(0)
 
     @pl.when(i == 0)
@@ -88,15 +90,15 @@
     )
     sketch[...] += jnp.dot(cleaned, probes[...], preferred_element_type=F32)
 
-    width = edges.shape[1] // 2
+    width = first.shape[1]
 
     @pl.when(i == 0)
     def _():
-        edges[:, :width] = cleaned[:, :width]
+        first[...] = cleaned[:, :width]
 
     @pl.when(i == steps - 1)
     def _():
-        edges[:, width:] = cleaned[:, -width:]
+        final[...] = cleaned[:, -width:]
 
 
 ANY = pl.BlockSpec(memory_space=pl.ANY)
@@ -130,31 +132,33 @@
         out_specs=[
             whole((rows, columns)),
             whole((2 * WIDTH, WIDTH)),
-            whole((rows, 2 * edge)),
+            whole((rows, edge)),
+            whole((rows, edge)),
         ],
         out_shape=[
             jax.ShapeDtypeStruct((rows, columns), F32),
             jax.ShapeDtypeStruct((2 * WIDTH, WIDTH), BF16),
-            jax.ShapeDtypeStruct((rows, 2 * edge), BF16),
+            jax.ShapeDtypeStruct((rows, edge), BF16),
+            jax.ShapeDtypeStruct((rows, edge), BF16),
         ],
         cost_estimate=COST,
         compiler_params=params(48),
     )(taps, spectra, spectra, spectra, low, high, probes)
 
 
-def total_kernel(*refs):
-    refs[-1][...] = pairwise([part[...] for part in refs[:-1]])
-
-
-def total_of(parts):
-    return pl.pallas_call(
-        total_kernel,
-        in_specs=[VMEM] * len(parts),
+def total_kernel(count, *refs):
+    refs[-1][...] = pairwise([part[...] for part in refs[:count]])
+
+
+def total_of(parts, wait):
+    return pl.pallas_call(
+        functools.partial(total_kernel, len(parts)),
+        in_specs=[VMEM] * len(parts) + [ANY] * len(wait),
         out_specs=VMEM,
         out_shape=jax.ShapeDtypeStruct(parts[0].shape, F32),
         cost_estimate=COST,
         compiler_params=params(32),
-    )(*parts)
+    )(*parts, *wait)
 
 
 def inverse_factor(gram):
@@ -200,14 +204,14 @@
 
 
 def basis_kernel(chips, factor, count, *refs):
-    own, near, basis, turned = refs[count : count + 4]
-    outs, held, sems = refs[count + 4 : -2], refs[-2], refs[-1]
-    rows, edge = held.shape[0] // 2, held.shape[1]
+    ends, (basis, turned) = refs[count : count + 4], refs[count + 4 : count + 6]
+    outs, held, sems = refs[count + 6 : -2], refs[-2], refs[-1]
+    rows = held.shape[1] // 2
     copies = [
         pltpu.make_async_copy(
-            one, held.at[pl.ds(n * rows, rows), :], sems.at[n]
+            one, held.at[n // 2, pl.ds(n % 2 * rows, rows), :], sems.at[n]
         )
-        for n, one in enumerate((own, near))
+        for n, one in enumerate(ends)
     ]
     for copy in copies:
         copy.start()
@@ -220,7 +224,7 @@
         for one in sketches
     ]
     inverse = inverse_factor(pairwise(grams) / float(rows * len(sketches)))
-    both = jnp.concatenate(sketches[:2], axis=0)
+    both = jnp.concatenate(sketches[: turned.shape[1] // rows], axis=0)
     across = lax.dot_general(
         inverse, both, (((1,), (1,)), ((), ())), precision=HIGHEST, preferred_element_type=F32
     )
@@ -237,52 +241,47 @@
     for copy in copies:
         copy.wait()
     for n in range(2):
-        side = slice(n * edge // 2, (n + 1) * edge // 2)
-        put_parts(turned, held[:, side], factor, outs[n * chips : (n + 1) * chips])
-
-
-def basis_of(sketches, own, near, factor, chips):
+        put_parts(turned, held[n], factor, outs[n * chips : (n + 1) * chips])
+
+
+def basis_of(sketches, ends, factor, chips, used):
     rows, size = sketches[0].shape
-    edge = own.shape[1]
+    edge = ends[0].shape[1]
     share = size // (2 * chips)
     return pl.pallas_call(
         functools.partial(basis_kernel, chips, factor, len(sketches)),
-        in_specs=[VMEM] * len(sketches) + [ANY] * 2,
+        in_specs=[VMEM] * len(sketches) + [ANY] * 4,
         out_specs=[VMEM] * (2 + 2 * chips),
         out_shape=[
             jax.ShapeDtypeStruct((rows, size), BF16),
-            jax.ShapeDtypeStruct((size // 2, 2 * rows), BF16),
+            jax.ShapeDtypeStruct((size // 2, used * rows), BF16),
         ]
-        + [jax.ShapeDtypeStruct((share, edge // 2), BF16)] * (2 * chips),
+        + [jax.ShapeDtypeStruct((share, edge), BF16)] * (2 * chips),
         scratch_shapes=[
-            pltpu.VMEM((2 * rows, edge), BF16),
-            pltpu.SemaphoreType.DMA((2,)),
+            pltpu.VMEM((2, 2 * rows, edge), BF16),
+            pltpu.SemaphoreType.DMA((4,)),
         ],
         cost_estimate=COST,
         compiler_params=params(32),
-    )(*sketches, own, near)
+    )(*sketches, *ends)
 
 
 def put_parts(turned, cleaned, factor, outs):
-    used = cleaned.shape[0]
-    part = jnp.dot(turned[:, :used], cleaned, preferred_element_type=F32) * factor
+    part = jnp.dot(turned[:, : cleaned.shape[0]], cleaned, preferred_element_type=F32) * factor
     share = outs[0].shape[0]
     for k, out in enumerate(outs):
         out[...] = part[k * share : (k + 1) * share].astype(BF16)
 
 
-def project_kernel(factor, chips, turned, band, *refs):
-    blocks, outs, done = refs[:6], refs[-1 - 2 * chips : -1], refs[-1]
+def project_kernel(count, factor, chips, turned, band, *refs):
+    blocks, outs, done = refs[:6], refs[-1 - count * chips : -1], refs[-1]
     done[...] = jnp.zeros_like(done)
     cleaned = clean_all(blocks, band[...])
-
-    @pl.when(pl.program_id(0) == 0)
-    def _():
-        put_parts(turned, cleaned, factor, outs[:chips])
-
-    @pl.when(pl.program_id(0) == 1)
-    def _():
-        put_parts(turned, cleaned, factor, outs[chips:])
+    for n in range(count):
+
+        @pl.when(pl.program_id(0) == n)
+        def _():
+            put_parts(turned, cleaned, factor, outs[n * chips : (n + 1) * chips])
 
 
 def clean_all(blocks, band):
@@ -295,21 +294,58 @@
     )
 
 
-def project(turned, band, spectra, near, start, size, factor, chips, wait):
+def project(turned, band, spectra, near, start, size, count, factor, chips, wait):
     rows, bins = spectra.shape
     share = turned.shape[0] // chips
     return pl.pallas_call(
-        functools.partial(project_kernel, factor, chips),
-        grid=(2,),
+        functools.partial(project_kernel, count, factor, chips),
+        grid=(count,),
         in_specs=[whole(turned.shape), whole(band.shape)]
         + block_specs(rows, size, start // size, bins // TILE - 1) * 2
         + [ANY] * len(wait),
-        out_specs=[whole((share, size))] * (2 * chips) + [whole((8, TILE))],
-        out_shape=[jax.ShapeDtypeStruct((share, size), BF16)] * (2 * chips)
+        out_specs=[whole((share, size))] * (count * chips) + [whole((8, TILE))],
+        out_shape=[jax.ShapeDtypeStruct((share, size), BF16)] * (count * chips)
         + [jax.ShapeDtypeStruct((8, TILE), F32)],
         cost_estimate=COST,
         compiler_params=params(50),
     )(turned, band, spectra, spectra, spectra, near, near, near, *wait)
+
+
+def project_whole_kernel(factor, turned, band, own, own_low, own_high, near, *refs):
+    near_low, near_high, far, other = refs[:4]
+    out, done = refs[-2], refs[-1]
+    done[...] = jnp.zeros_like(done)
+    taps = band[...]
+    cleaned = [
+        clean(own_low[...], own[...], own_high[...], taps),
+        clean(near_low[...], near[...], near_high[...], taps),
+    ]
+    for one in (far, other):
+        last = one.shape[1] - TILE
+        cleaned.append(clean(one[:, :TILE], one[:, TILE:last], one[:, last:], taps))
+    put_parts(turned.at[: out.shape[0]], jnp.concatenate(cleaned, axis=0), factor, [out])
+
+
+def project_whole(out, turned, band, spectra, near, far, start, factor, wait):
+    rows, bins = spectra.shape
+    size = far[0].shape[1] - 2 * TILE
+    first = start // size
+    return pl.pallas_call(
+        functools.partial(project_whole_kernel, factor),
+        grid=(1,),
+        in_specs=[whole(turned.shape), whole(band.shape)]
+        + block_specs(rows, size, first, bins // TILE - 1) * 2
+        + [whole(one.shape) for one in far]
+        + [ANY] * (1 + len(wait)),
+        out_specs=[pl.BlockSpec((out.shape[0], size), lambda i: (0, first)), whole((8, TILE))],
+        out_shape=[
+            jax.ShapeDtypeStruct(out.shape, BF16),
+            jax.ShapeDtypeStruct((8, TILE), F32),
+        ],
+        input_output_aliases={10: 0},
+        cost_estimate=COST,
+        compiler_params=params(50),
+    )(turned, band, *[spectra] * 3, *[near] * 3, *far, out, *wait)
 
 
 def finish_kernel(blocks, count, *refs):
@@ -333,7 +369,8 @@
         in_specs=[whole((share, size))] * len(parts) + [ANY] * (len(extra) + len(wait)),
         out_specs=[
             pl.BlockSpec(
-                (share, size), lambda i: (0, jnp.where(i == 0, *[at // size for at in starts]))
+                (share, size),
+                lambda i: (0, jnp.where(i == 0, starts[0] // size, starts[-1] // size)),
             ),
             whole((8, TILE)),
         ],
@@ -362,11 +399,16 @@
 
     near = partner(spectra, "pix", 1)
     edge = math.gcd(bins // 2, EDGE)
-    partial_sketch, band, edges = sketch_of(taps, spectra, low, high, probes, edge)
-    near_edges = partner(edges, "pix", 1)
-    sketch = total_of(spread(partial_sketch, "mz"))
+    far = []
+    inner = edge
+    if chips == 2 and bins >= 6 * edge:
+        far = [partner(spectra[:, edge - TILE : 2 * edge + TILE], "pix", 2)]
+        inner = 2 * edge
+    partial_sketch, band, first, final = sketch_of(taps, spectra, low, high, probes, edge)
+    ends = [first, partner(first, "pix", 1), final, partner(final, "pix", 1)]
+    sketch = total_of(spread(partial_sketch, "mz"), far)
     basis, turned, *mine = basis_of(
-        gather(sketch, "pix"), edges, near_edges, factor, chips
+        gather(sketch, "pix"), ends, factor, chips, 2 + 2 * len(far)
     )
 
     routes = [
@@ -386,12 +428,22 @@
 
     out, recent = None, []
     before = ([across(mine[:chips]), across(mine[chips:])], (0, bins - edge))
-    for start in range(edge, bins - edge, 2 * edge):
-        *mine, done = project(turned, band, spectra, near, start, edge, factor, chips, recent)
-        blocks = [across(mine[:chips]), across(mine[chips:])]
-        out, done = finish(out, *before, bins, [done])
+    for start in range(inner, bins - edge, 2 * edge):
+        count = min(2, (bins - edge - start) // edge)
+        *mine, done = project(
+            turned, band, spectra, near, start, edge, count, factor, chips, recent
+        )
+        blocks = [across(mine[n * chips : (n + 1) * chips]) for n in range(count)]
         recent = [done]
-        before = (blocks, (start, start + edge))
+        if far and start + count * edge == bins - edge:
+            pair = [far[0], partner(far[0], "pix", 1)]
+            out, done = project_whole(
+                out, turned, band, spectra, near, pair, edge, factor, recent
+            )
+            recent = [done]
+        out, done = finish(out, *before, bins, recent)
+        recent = [done]
+        before = (blocks, tuple(start + n * edge for n in range(count)))
     out, done = finish(out, *before, bins, recent)
     return (basis, out)
 

time: 146 us -> 142 us (0.973)
  waiting for transfers between devices: 43.5 us -> 34.5 us
  Pallas kernels: 68.7 us -> 72.7 us
    ppermute x16 -> x15, waiting for transfers between devices: 33.5 us -> 25 us  [across(): lax.ppermute(mine[m], 'pix', routes[m])]
    pallas_call x8 -> x10, Pallas kernels: 36.3 us -> 40.2 us  [the longest x7 34.2 us: project(): pl.pallas_call(functools.partial(project_kernel, count, factor, chips), g...]
    ppermute x8 -> x10, starting transfers between devices: 8 us -> 9.52 us  [partner(): return lax.ppermute(x, axis, [(i, i ^ shift) for i in range(count)])]
    ppermute x16 -> x15, starting transfers between devices: 16.7 us -> 15.8 us  [across(): lax.ppermute(mine[m], 'pix', routes[m])]
    ppermute x8 -> x10, waiting for transfers between devices: 9.19 us -> 8.65 us  [partner(): return lax.ppermute(x, axis, [(i, i ^ shift) for i in range(count)])]
  transfers between devices with their start and end apart: 26 -> 27, of which waited for: 14 -> 12; matrix products, arithmetic and copies ran while one was open for 1% -> 2% of each run, Pallas kernels for 47% -> 51%
where the time goes in v3:
time: 142 us
  Pallas kernels  72.7 us (51%)
  waiting for transfers between devices  34.5 us (24%)
  starting transfers between devices  31 us (22%)
  local copies, waits for them, and re-layouts  2.1 us (1%)
    pallas_call x7, Pallas kernels, project(): pl.pallas_call(functools.partial(project_kernel, count, factor, chips), g...  34.2 us
    ppermute x15, waiting for transfers between devices, across(): lax.ppermute(mine[m], 'pix', routes[m])  25 us
    pallas_call x1, Pallas kernels, sketch_of(): pl.pallas_call(functools.partial(sketch_kernel, steps), grid=(steps,), in...  19.3 us
    ppermute x15, starting transfers between devices, across(): lax.ppermute(mine[m], 'pix', routes[m])  15.8 us
    ppermute x10, starting transfers between devices, partner(): return lax.ppermute(x, axis, [(i, i ^ shift) for i in range(count)])  9.52 us
    ppermute x10, waiting for transfers between devices, partner(): return lax.ppermute(x, axis, [(i, i ^ shift) for i in range(count)])  8.65 us
    pallas_call x8, Pallas kernels, finish(): pl.pallas_call(functools.partial(finish_kernel, len(blocks), len(blocks[0...  6.78 us
    pallas_call x1, Pallas kernels, basis_of(): pl.pallas_call(functools.partial(basis_kernel, chips, factor, len(sketche...  6.38 us
  transfers between devices with their start and end apart: 27, of which 12 were waited for; matrix products, arithmetic and copies ran while one was open for 2% of the time, Pallas kernels for 51%

profile of v3, /device:TPU:0, one launch (start us, length us, event | category | flops | bytes accessed | tf_op | source)
XLA Modules:
  0.0 141.9 jit_solution(4697731497854773394)
XLA Ops:
  0.6 0.5 collective-permute-start.10
  1.1 0.8 fusion
  1.9 4.5 %collective-permute-start = (bf16[128,128]{1,0:T(8,128)(2,1)S(1)}, bf16[128,128]{1,0:T(8,128)(2,1)S(1)}, u32[]{:S(2)}, u32[]{:S(2)}) collective-permute-start(bf16[128,128]{1,0:T(8,128)(2,1)S(1)} %get-tuple-element.123), channel_id=1, source_target_pairs={{0,4},{4,8},{8,12},{1,5},{5,9},{9,13},{2,6},{6,10},{10,14},{3,7},{... | collective-permute-start | bytes 98312 | tf_op jit(solution)/shard_map/ppermute | solution.py:396
  6.4 1.3 collective-permute-start.1
  7.7 1.3 slice.11
  9.0 1.6 %collective-permute-start.4 = (bf16[128,4352]{1,0:T(8,128)(2,1)S(1)}, bf16[128,4352]{1,0:T(8,128)(2,1)}, u32[]{:S(2)}, u32[]{:S(2)}) collective-permute-start(bf16[128,4352]{1,0:T(8,128)(2,1)S(1)} %slice.11), channel_id=1, source_target_pairs={{0,2},{1,3},{2,0},{3,1},{4,6},{5,7},{6,4},{7,5},{8,10},{9,11},{10,... | collective-permute-start | bytes 3342344 | tf_op jit(solution)/shard_map/ppermute | solution.py:30
  10.6 0.7 pad_convert_fusion
  11.3 0.0 collective-permute-done.low
  11.3 0.9 collective-permute-done.1.high
  12.2 19.3 %shard_map.50 = (f32[128,128]{1,0:T(8,128)S(1)}, bf16[512,256]{1,0:T(8,128)(2,1)S(1)}, bf16[128,4096]{1,0:T(8,128)(2,1)S(1)}, bf16[128,4096]{1,0:T(8,128)(2,1)S(1)}) custom-call(f32[1,512]{1,0:T(1,128)S(1)} %bitcast.1, bf16[128,65536]{1,0:T(8,128)(2,1)} %own_high.1, bf16[128,65536]{1,0:T(8,128)(2,1)} %own_high.1, bf16[128,65536]{1,0:T(8,128)(2,1)} %own_high.1, ...), custom_call_target="tpu_custom_call" | custom-call | flops 1 | bytes 1 | tf_op jit(solution)/shard_map/pallas_call | solution.py:125
  31.6 0.1 collective-permute-start.8
  31.6 0.5 collective-permute-start.9
  32.1 1.8 %collective-permute-start.2 = (f32[128,128]{1,0:T(8,128)S(1)}, f32[128,128]{1,0:T(8,128)S(1)}, u32[]{:S(2)}, u32[]{:S(2)}) collective-permute-start(f32[128,128]{1,0:T(8,128)S(1)} %get-tuple-element.62.refs_0_), channel_id=1, source_target_pairs={{0,4},{4,0},{8,12},{12,8},{1,5},{5,1},{9,13},{13,9},{2,6},{6,2},{1... | collective-permute-start | bytes 196616 | tf_op jit(solution)/shard_map/ppermute | solution.py:30
  33.9 2.5 %collective-permute-done.2.refs_1_ = f32[128,128]{1,0:T(8,128)S(1)} collective-permute-done((f32[128,128]{1,0:T(8,128)S(1)}, f32[128,128]{1,0:T(8,128)S(1)}, u32[]{:S(2)}, u32[]{:S(2)}) %collective-permute-start.2) | collective-permute-done | bytes 65568 | tf_op jit(solution)/shard_map/ppermute | solution.py:30
  36.4 2.8 %collective-permute-start.3 = (f32[128,128]{1,0:T(8,128)S(1)}, f32[128,128]{1,0:T(8,128)S(1)}, u32[]{:S(2)}, u32[]{:S(2)}) collective-permute-start(f32[128,128]{1,0:T(8,128)S(1)} %shard_map.51.refs_0_), channel_id=1, source_target_pairs={{0,8},{4,12},{8,0},{12,4},{1,9},{5,13},{9,1},{13,5},{2,10},{6,14},... | collective-permute-start | bytes 196616 | tf_op jit(solution)/shard_map/ppermute | solution.py:30
  39.3 2.6 %collective-permute-done.3.refs_1_ = f32[128,128]{1,0:T(8,128)S(1)} collective-permute-done((f32[128,128]{1,0:T(8,128)S(1)}, f32[128,128]{1,0:T(8,128)S(1)}, u32[]{:S(2)}, u32[]{:S(2)}) %collective-permute-start.3) | collective-permute-done | bytes 65568 | tf_op jit(solution)/shard_map/ppermute | solution.py:30
  41.9 0.1 collective-permute-start.5
  42.0 1.4 collective-permute-start.6
  43.4 0.5 collective-permute-start.7
  43.9 0.3 collective-permute-start.26
  44.2 0.0 collective-permute-done.5.refs_1_
  44.2 2.5 %collective-permute-done.6.refs_2_ = f32[128,128]{1,0:T(8,128)S(1)} collective-permute-done((f32[128,128]{1,0:T(8,128)S(1)}, f32[128,128]{1,0:T(8,128)S(1)}, u32[]{:S(2)}, u32[]{:S(2)}) %collective-permute-start.6) | collective-permute-done | bytes 65568 | tf_op jit(solution)/shard_map/ppermute | solution.py:30
  46.7 1.0 collective-permute-done.7.refs_3_
  47.7 6.4 %shard_map.53 = (bf16[128,128]{1,0:T(8,128)(2,1)}, bf16[64,512]{1,0:T(8,128)(2,1)S(1)}, bf16[32,4096]{1,0:T(8,128)(2,1)S(1)}, bf16[32,4096]{1,0:T(8,128)(2,1)S(1...) custom-call(f32[128,128]{1,0:T(8,128)S(1)} %shard_map.52.refs_0_, ...), custom_call_target="tpu_custom_call" | custom-call | flops 1 | bytes 1 | tf_op jit(solution)/shard_map/pallas_call | solution.py:251
  54.1 1.1 collective-permute-start.13
  55.2 1.0 collective-permute-start.14
  56.2 0.0 collective-permute-done.10.refs_3_.refs_4_.refs_5_.near.refs_0_.refs_1_
  56.2 5.2 %shard_map.54 = (bf16[32,4096]{1,0:T(8,128)(2,1)S(1)}, bf16[32,4096]{1,0:T(8,128)(2,1)S(1)}, bf16[32,4096]{1,0:T(8,128)(2,1)S(1)}, bf16[32,4096]{1,0:T(8,128)(2,1)S(1)}, f32[8,128]{1,0:T(8,128)S(1)}) custom-call(bf16[64,512]{1,0:T(8,128)(2,1)S(1)} %get-tuple-element.66.turned, bf16[512,256]{1,0:T(8,128)(2,1)S(1)} %get-tuple-element.67.band, ...), custom_call_target="tpu_custom_call" | custom-call | flops 1 | bytes 1 | tf_op jit(solution)/shard_map/pallas_call | solution.py:300
  61.4 1.1 collective-permute-start.11
  62.5 1.0 collective-permute-start.12
  63.5 5.5 %collective-permute-done.14.refs_3_ = bf16[32,4096]{1,0:T(8,128)(2,1)S(1)} collective-permute-done((bf16[32,4096]{1,0:T(8,128)(2,1)S(1)}, bf16[32,4096]{1,0:T(8,128)(2,1)S(1)}, u32[]{:S(2)}, u32[]{:S(2)}) %collective-permute-start.14) | collective-permute-done | bytes 262176 | tf_op jit(solution)/shard_map/ppermute | solution.py:427
  68.9 0.9 shard_map.55
  69.8 5.2 %shard_map.56 = (bf16[32,4096]{1,0:T(8,128)(2,1)S(1)}, bf16[32,4096]{1,0:T(8,128)(2,1)S(1)}, bf16[32,4096]{1,0:T(8,128)(2,1)S(1)}, bf16[32,4096]{1,0:T(8,128)(2,1)S(1)}, f32[8,128]{1,0:T(8,128)S(1)}) custom-call(bf16[64,512]{1,0:T(8,128)(2,1)S(1)} %get-tuple-element.66.turned, bf16[512,256]{1,0:T(8,128)(2,1)S(1)} %get-tuple-element.67.band, ...), custom_call_target="tpu_custom_call" | custom-call | flops 1 | bytes 1 | tf_op jit(solution)/shard_map/pallas_call | solution.py:300
  75.0 1.1 collective-permute-start.17
  76.1 1.0 collective-permute-start.18
  77.1 3.1 %collective-permute-done.12.refs_3_ = bf16[32,4096]{1,0:T(8,128)(2,1)S(1)} collective-permute-done((bf16[32,4096]{1,0:T(8,128)(2,1)S(1)}, bf16[32,4096]{1,0:T(8,128)(2,1)S(1)}, u32[]{:S(2)}, u32[]{:S(2)}) %collective-permute-start.12) | collective-permute-done | bytes 262176 | tf_op jit(solution)/shard_map/ppermute | solution.py:427
  80.2 0.9 shard_map.57
  81.0 5.2 %shard_map.58 = (bf16[32,4096]{1,0:T(8,128)(2,1)S(1)}, bf16[32,4096]{1,0:T(8,128)(2,1)S(1)}, bf16[32,4096]{1,0:T(8,128)(2,1)S(1)}, bf16[32,4096]{1,0:T(8,128)(2,1)S(1)}, f32[8,128]{1,0:T(8,128)S(1)}) custom-call(bf16[64,512]{1,0:T(8,128)(2,1)S(1)} %get-tuple-element.66.turned, bf16[512,256]{1,0:T(8,128)(2,1)S(1)} %get-tuple-element.67.band, ...), custom_call_target="tpu_custom_call" | custom-call | flops 1 | bytes 1 | tf_op jit(solution)/shard_map/pallas_call | solution.py:300
  86.2 1.1 collective-permute-start.15
  87.3 1.0 collective-permute-start.16
  88.3 3.1 %collective-permute-done.18.refs_3_ = bf16[32,4096]{1,0:T(8,128)(2,1)S(1)} collective-permute-done((bf16[32,4096]{1,0:T(8,128)(2,1)S(1)}, bf16[32,4096]{1,0:T(8,128)(2,1)S(1)}, u32[]{:S(2)}, u32[]{:S(2)}) %collective-permute-start.18) | collective-permute-done | bytes 262176 | tf_op jit(solution)/shard_map/ppermute | solution.py:427
  91.4 0.9 shard_map.59
  92.3 5.2 %shard_map.60 = (bf16[32,4096]{1,0:T(8,128)(2,1)S(1)}, bf16[32,4096]{1,0:T(8,128)(2,1)S(1)}, bf16[32,4096]{1,0:T(8,128)(2,1)S(1)}, bf16[32,4096]{1,0:T(8,128)(2,1)S(1)}, f32[8,128]{1,0:T(8,128)S(1)}) custom-call(bf16[64,512]{1,0:T(8,128)(2,1)S(1)} %get-tuple-element.66.turned, bf16[512,256]{1,0:T(8,128)(2,1)S(1)} %get-tuple-element.67.band, ...), custom_call_target="tpu_custom_call" | custom-call | flops 1 | bytes 1 | tf_op jit(solution)/shard_map/pallas_call | solution.py:300
  97.4 1.1 collective-permute-start.21
  98.5 1.0 collective-permute-start.22
  99.5 3.1 %collective-permute-done.16.refs_3_ = bf16[32,4096]{1,0:T(8,128)(2,1)S(1)} collective-permute-done((bf16[32,4096]{1,0:T(8,128)(2,1)S(1)}, bf16[32,4096]{1,0:T(8,128)(2,1)S(1)}, u32[]{:S(2)}, u32[]{:S(2)}) %collective-permute-start.16) | collective-permute-done | bytes 262176 | tf_op jit(solution)/shard_map/ppermute | solution.py:427
  102.6 0.9 shard_map.61
  103.5 5.2 %shard_map.62 = (bf16[32,4096]{1,0:T(8,128)(2,1)S(1)}, bf16[32,4096]{1,0:T(8,128)(2,1)S(1)}, bf16[32,4096]{1,0:T(8,128)(2,1)S(1)}, bf16[32,4096]{1,0:T(8,128)(2,1)S(1)}, f32[8,128]{1,0:T(8,128)S(1)}) custom-call(bf16[64,512]{1,0:T(8,128)(2,1)S(1)} %get-tuple-element.66.turned, bf16[512,256]{1,0:T(8,128)(2,1)S(1)} %get-tuple-element.67.band, ...), custom_call_target="tpu_custom_call" | custom-call | flops 1 | bytes 1 | tf_op jit(solution)/shard_map/pallas_call | solution.py:300
  108.7 1.1 collective-permute-start.19
  109.8 1.0 collective-permute-start.20
  110.8 3.1 %collective-permute-done.22.refs_3_ = bf16[32,4096]{1,0:T(8,128)(2,1)S(1)} collective-permute-done((bf16[32,4096]{1,0:T(8,128)(2,1)S(1)}, bf16[32,4096]{1,0:T(8,128)(2,1)S(1)}, u32[]{:S(2)}, u32[]{:S(2)}) %collective-permute-start.22) | collective-permute-done | bytes 262176 | tf_op jit(solution)/shard_map/ppermute | solution.py:427
  113.9 0.9 shard_map.63
  114.7 5.2 %shard_map.64 = (bf16[32,4096]{1,0:T(8,128)(2,1)S(1)}, bf16[32,4096]{1,0:T(8,128)(2,1)S(1)}, bf16[32,4096]{1,0:T(8,128)(2,1)S(1)}, bf16[32,4096]{1,0:T(8,128)(2,1)S(1)}, f32[8,128]{1,0:T(8,128)S(1)}) custom-call(bf16[64,512]{1,0:T(8,128)(2,1)S(1)} %get-tuple-element.66.turned, bf16[512,256]{1,0:T(8,128)(2,1)S(1)} %get-tuple-element.67.band, ...), custom_call_target="tpu_custom_call" | custom-call | flops 1 | bytes 1 | tf_op jit(solution)/shard_map/pallas_call | solution.py:300
  119.9 1.1 collective-permute-start.24
  121.0 1.0 collective-permute-start.25
  122.0 3.1 %collective-permute-done.20.refs_3_ = bf16[32,4096]{1,0:T(8,128)(2,1)S(1)} collective-permute-done((bf16[32,4096]{1,0:T(8,128)(2,1)S(1)}, bf16[32,4096]{1,0:T(8,128)(2,1)S(1)}, u32[]{:S(2)}, u32[]{:S(2)}) %collective-permute-start.20) | collective-permute-done | bytes 262176 | tf_op jit(solution)/shard_map/ppermute | solution.py:427
  125.1 0.9 shard_map.65
  126.0 3.2 %shard_map.66 = (bf16[32,4096]{1,0:T(8,128)(2,1)S(1)}, bf16[32,4096]{1,0:T(8,128)(2,1)S(1)}, f32[8,128]{1,0:T(8,128)S(1)}) custom-call(bf16[64,512]{1,0:T(8,128)(2,1)S(1)} %get-tuple-element.66.turned, bf16[512,256]{1,0:T(8,128)(2,1)S(1)} %get-tuple-element.67.band, bf16[128,65536]{1,0:T(8,128)(2,1)} %own_high.1, bf16[128,65536]{1,0:T(8,128)(2,1)} %own_high.1, ...), custom_call_target="tpu_custom_call" | custom-call | flops 1 | bytes 1 | tf_op jit(solution)/shard_map/pallas_call | solution.py:300
  129.1 1.1 collective-permute-start.23
  130.2 6.0 %shard_map.67 = (bf16[32,65536]{1,0:T(8,128)(2,1)}, f32[8,128]{1,0:T(8,128)S(1)}) custom-call(bf16[64,512]{1,0:T(8,128)(2,1)S(1)} %get-tuple-element.66.turned, bf16[512,256]{1,0:T(8,128)(2,1)S(1)} %get-tuple-element.67.band, bf16[128,65536]{1,0:T(8,128)(2,1)} %own_high.1, bf16[128,65536]{1,0:T(8,128)(2,1)} %own_high.1, ...), custom_call_target="tpu_custom_call", output_to_operand_aliasing={{0}: (10, {})} | custom-call | flops 1 | bytes 1 | tf_op jit(solution)/shard_map/pallas_call | solution.py:333
  136.3 0.0 collective-permute-done.25.refs_3_
  136.3 0.9 shard_map.68
  137.2 3.9 %collective-permute-done.23.refs_1_ = bf16[32,4096]{1,0:T(8,128)(2,1)S(1)} collective-permute-done((bf16[32,4096]{1,0:T(8,128)(2,1)S(1)}, bf16[32,4096]{1,0:T(8,128)(2,1)S(1)}, u32[]{:S(2)}, u32[]{:S(2)}) %collective-permute-start.23) | collective-permute-done | bytes 262176 | tf_op jit(solution)/shard_map/ppermute | solution.py:427
  141.1 0.8 shard_map.69
  (13 shorter events, 0.0 us)
Async XLA Ops:
  0.6 55.5 %collective-permute-start.10 = (bf16[128,65536]{1,0:T(8,128)(2,1)}, bf16[128,65536]{1,0:T(8,128)(2,1)}, u32[]{:S(2)}, u32[]{:S(2)}) collective-permute-start(bf16[128,65536]{1,0:T(8,128)(2,1)} %own_high.1), channel_id=1, source_target_pairs={{0,1},{1,0},{2,3},{3,2},{4,5},{5,4},{6,7},{7,6},{8,9},{9,8},{10,11... | collective-permute-start | bytes 50331656 | tf_op jit(solution)/shard_map/ppermute | solution.py:30
  1.9 9.4 %collective-permute-start = (bf16[128,128]{1,0:T(8,128)(2,1)S(1)}, bf16[128,128]{1,0:T(8,128)(2,1)S(1)}, u32[]{:S(2)}, u32[]{:S(2)}) collective-permute-start(bf16[128,128]{1,0:T(8,128)(2,1)S(1)} %get-tuple-element.123), channel_id=1, source_target_pairs={{0,4},{4,8},{8,12},{1,5},{5,9},{9,13},{2,6},{6,10},{10,14},{3,7},{... | collective-permute-start | bytes 98312 | tf_op jit(solution)/shard_map/ppermute | solution.py:396
  6.4 5.8 %collective-permute-start.1 = (bf16[128,128]{1,0:T(8,128)(2,1)S(1)}, bf16[128,128]{1,0:T(8,128)(2,1)S(1)}, u32[]{:S(2)}, u32[]{:S(2)}) collective-permute-start(bf16[128,128]{1,0:T(8,128)(2,1)S(1)} %get-tuple-element.122), channel_id=1, source_target_pairs={{4,0},{8,4},{12,8},{5,1},{9,5},{13,9},{6,2},{10,6},{14,10},{7,3},{... | collective-permute-start | bytes 98312 | tf_op jit(solution)/shard_map/ppermute | solution.py:397
  9.0 32.9 %collective-permute-start.4 = (bf16[128,4352]{1,0:T(8,128)(2,1)S(1)}, bf16[128,4352]{1,0:T(8,128)(2,1)}, u32[]{:S(2)}, u32[]{:S(2)}) collective-permute-start(bf16[128,4352]{1,0:T(8,128)(2,1)S(1)} %slice.11), channel_id=1, source_target_pairs={{0,2},{1,3},{2,0},{3,1},{4,6},{5,7},{6,4},{7,5},{8,10},{9,11},{10,... | collective-permute-start | bytes 3342344 | tf_op jit(solution)/shard_map/ppermute | solution.py:30
  31.6 11.8 %collective-permute-start.8 = (bf16[128,4096]{1,0:T(8,128)(2,1)S(1)}, bf16[128,4096]{1,0:T(8,128)(2,1)S(1)}, u32[]{:S(2)}, u32[]{:S(2)}) collective-permute-start(bf16[128,4096]{1,0:T(8,128)(2,1)S(1)} %get-tuple-element.63.refs_4_), channel_id=1, source_target_pairs={{0,1},{1,0},{2,3},{3,2},{4,5},{5,4},{6,7},{7,6},{8,9},{9,8},{10,11... | collective-permute-start | bytes 3145736 | tf_op jit(solution)/shard_map/ppermute | solution.py:30
  31.6 12.2 %collective-permute-start.9 = (bf16[128,4096]{1,0:T(8,128)(2,1)S(1)}, bf16[128,4096]{1,0:T(8,128)(2,1)S(1)}, u32[]{:S(2)}, u32[]{:S(2)}) collective-permute-start(bf16[128,4096]{1,0:T(8,128)(2,1)S(1)} %get-tuple-element.64.refs_6_), channel_id=1, source_target_pairs={{0,1},{1,0},{2,3},{3,2},{4,5},{5,4},{6,7},{7,6},{8,9},{9,8},{10,11... | collective-permute-start | bytes 3145736 | tf_op jit(solution)/shard_map/ppermute | solution.py:30
  32.1 4.3 %collective-permute-start.2 = (f32[128,128]{1,0:T(8,128)S(1)}, f32[128,128]{1,0:T(8,128)S(1)}, u32[]{:S(2)}, u32[]{:S(2)}) collective-permute-start(f32[128,128]{1,0:T(8,128)S(1)} %get-tuple-element.62.refs_0_), channel_id=1, source_target_pairs={{0,4},{4,0},{8,12},{12,8},{1,5},{5,1},{9,13},{13,9},{2,6},{6,2},{1... | collective-permute-start | bytes 196616 | tf_op jit(solution)/shard_map/ppermute | solution.py:30
  36.4 5.5 %collective-permute-start.3 = (f32[128,128]{1,0:T(8,128)S(1)}, f32[128,128]{1,0:T(8,128)S(1)}, u32[]{:S(2)}, u32[]{:S(2)}) collective-permute-start(f32[128,128]{1,0:T(8,128)S(1)} %shard_map.51.refs_0_), channel_id=1, source_target_pairs={{0,8},{4,12},{8,0},{12,4},{1,9},{5,13},{9,1},{13,5},{2,10},{6,14},... | collective-permute-start | bytes 196616 | tf_op jit(solution)/shard_map/ppermute | solution.py:30
  41.9 2.3 %collective-permute-start.5 = (f32[128,128]{1,0:T(8,128)S(1)}, f32[128,128]{1,0:T(8,128)S(1)}, u32[]{:S(2)}, u32[]{:S(2)}) collective-permute-start(f32[128,128]{1,0:T(8,128)S(1)} %shard_map.52.refs_0_), channel_id=1, source_target_pairs={{0,1},{1,0},{2,3},{3,2},{4,5},{5,4},{6,7},{7,6},{8,9},{9,8},{10,11... | collective-permute-start | bytes 196616 | tf_op jit(solution)/shard_map/ppermute | solution.py:30
  42.0 4.7 %collective-permute-start.6 = (f32[128,128]{1,0:T(8,128)S(1)}, f32[128,128]{1,0:T(8,128)S(1)}, u32[]{:S(2)}, u32[]{:S(2)}) collective-permute-start(f32[128,128]{1,0:T(8,128)S(1)} %shard_map.52.refs_0_), channel_id=1, source_target_pairs={{0,2},{1,3},{2,0},{3,1},{4,6},{5,7},{6,4},{7,5},{8,10},{9,11},{10,... | collective-permute-start | bytes 196616 | tf_op jit(solution)/shard_map/ppermute | solution.py:30
  43.4 4.3 %collective-permute-start.7 = (f32[128,128]{1,0:T(8,128)S(1)}, f32[128,128]{1,0:T(8,128)S(1)}, u32[]{:S(2)}, u32[]{:S(2)}) collective-permute-start(f32[128,128]{1,0:T(8,128)S(1)} %shard_map.52.refs_0_), channel_id=1, source_target_pairs={{0,3},{1,2},{2,1},{3,0},{4,7},{5,6},{6,5},{7,4},{8,11},{9,10},{10,... | collective-permute-start | bytes 196616 | tf_op jit(solution)/shard_map/ppermute | solution.py:30
  43.9 86.4 %collective-permute-start.26 = (bf16[128,4352]{1,0:T(8,128)(2,1)}, bf16[128,4352]{1,0:T(8,128)(2,1)}, u32[]{:S(2)}, u32[]{:S(2)}) collective-permute-start(bf16[128,4352]{1,0:T(8,128)(2,1)} %collective-permute-done.4.refs_2_), channel_id=1, source_target_pairs={{0,1},{1,0},{2,3},{3,2},{4,5},{5,4},{6,7},{7,6},{8,9},{9,8},{10,11... | collective-permute-start | bytes 3342344 | tf_op jit(solution)/shard_map/ppermute | solution.py:30
  54.1 9.4 %collective-permute-start.13 = (bf16[32,4096]{1,0:T(8,128)(2,1)S(1)}, bf16[32,4096]{1,0:T(8,128)(2,1)S(1)}, u32[]{:S(2)}, u32[]{:S(2)}) collective-permute-start(bf16[32,4096]{1,0:T(8,128)(2,1)S(1)} %get-tuple-element.73), channel_id=1, source_target_pairs={{0,2},{1,3},{2,0},{3,1},{4,6},{5,7},{6,4},{7,5},{8,10},{9,11},{10,... | collective-permute-start | bytes 786440 | tf_op jit(solution)/shard_map/ppermute | solution.py:427
  55.2 13.7 %collective-permute-start.14 = (bf16[32,4096]{1,0:T(8,128)(2,1)S(1)}, bf16[32,4096]{1,0:T(8,128)(2,1)S(1)}, u32[]{:S(2)}, u32[]{:S(2)}) collective-permute-start(bf16[32,4096]{1,0:T(8,128)(2,1)S(1)} %get-tuple-element.75), channel_id=1, source_target_pairs={{0,2},{1,3},{2,0},{3,1},{4,6},{5,7},{6,4},{7,5},{8,10},{9,11},{10,... | collective-permute-start | bytes 786440 | tf_op jit(solution)/shard_map/ppermute | solution.py:427
  61.4 15.7 %collective-permute-start.11 = (bf16[32,4096]{1,0:T(8,128)(2,1)S(1)}, bf16[32,4096]{1,0:T(8,128)(2,1)S(1)}, u32[]{:S(2)}, u32[]{:S(2)}) collective-permute-start(bf16[32,4096]{1,0:T(8,128)(2,1)S(1)} %get-tuple-element.69), channel_id=1, source_target_pairs={{0,2},{1,3},{2,0},{3,1},{4,6},{5,7},{6,4},{7,5},{8,10},{9,11},{10,... | collective-permute-start | bytes 786440 | tf_op jit(solution)/shard_map/ppermute | solution.py:427
  62.5 17.7 %collective-permute-start.12 = (bf16[32,4096]{1,0:T(8,128)(2,1)S(1)}, bf16[32,4096]{1,0:T(8,128)(2,1)S(1)}, u32[]{:S(2)}, u32[]{:S(2)}) collective-permute-start(bf16[32,4096]{1,0:T(8,128)(2,1)S(1)} %get-tuple-element.71), channel_id=1, source_target_pairs={{0,2},{1,3},{2,0},{3,1},{4,6},{5,7},{6,4},{7,5},{8,10},{9,11},{10,... | collective-permute-start | bytes 786440 | tf_op jit(solution)/shard_map/ppermute | solution.py:427
  75.0 13.3 %collective-permute-start.17 = (bf16[32,4096]{1,0:T(8,128)(2,1)S(1)}, bf16[32,4096]{1,0:T(8,128)(2,1)S(1)}, u32[]{:S(2)}, u32[]{:S(2)}) collective-permute-start(bf16[32,4096]{1,0:T(8,128)(2,1)S(1)} %get-tuple-element.86), channel_id=1, source_target_pairs={{0,2},{1,3},{2,0},{3,1},{4,6},{5,7},{6,4},{7,5},{8,10},{9,11},{10,... | collective-permute-start | bytes 786440 | tf_op jit(solution)/shard_map/ppermute | solution.py:427
  76.1 15.3 %collective-permute-start.18 = (bf16[32,4096]{1,0:T(8,128)(2,1)S(1)}, bf16[32,4096]{1,0:T(8,128)(2,1)S(1)}, u32[]{:S(2)}, u32[]{:S(2)}) collective-permute-start(bf16[32,4096]{1,0:T(8,128)(2,1)S(1)} %get-tuple-element.88), channel_id=1, source_target_pairs={{0,2},{1,3},{2,0},{3,1},{4,6},{5,7},{6,4},{7,5},{8,10},{9,11},{10,... | collective-permute-start | bytes 786440 | tf_op jit(solution)/shard_map/ppermute | solution.py:427
  86.2 13.3 %collective-permute-start.15 = (bf16[32,4096]{1,0:T(8,128)(2,1)S(1)}, bf16[32,4096]{1,0:T(8,128)(2,1)S(1)}, u32[]{:S(2)}, u32[]{:S(2)}) collective-permute-start(bf16[32,4096]{1,0:T(8,128)(2,1)S(1)} %get-tuple-element.82), channel_id=1, source_target_pairs={{0,2},{1,3},{2,0},{3,1},{4,6},{5,7},{6,4},{7,5},{8,10},{9,11},{10,... | collective-permute-start | bytes 786440 | tf_op jit(solution)/shard_map/ppermute | solution.py:427
  87.3 15.3 %collective-permute-start.16 = (bf16[32,4096]{1,0:T(8,128)(2,1)S(1)}, bf16[32,4096]{1,0:T(8,128)(2,1)S(1)}, u32[]{:S(2)}, u32[]{:S(2)}) collective-permute-start(bf16[32,4096]{1,0:T(8,128)(2,1)S(1)} %get-tuple-element.84), channel_id=1, source_target_pairs={{0,2},{1,3},{2,0},{3,1},{4,6},{5,7},{6,4},{7,5},{8,10},{9,11},{10,... | collective-permute-start | bytes 786440 | tf_op jit(solution)/shard_map/ppermute | solution.py:427
  97.4 13.3 %collective-permute-start.21 = (bf16[32,4096]{1,0:T(8,128)(2,1)S(1)}, bf16[32,4096]{1,0:T(8,128)(2,1)S(1)}, u32[]{:S(2)}, u32[]{:S(2)}) collective-permute-start(bf16[32,4096]{1,0:T(8,128)(2,1)S(1)} %get-tuple-element.100), channel_id=1, source_target_pairs={{0,2},{1,3},{2,0},{3,1},{4,6},{5,7},{6,4},{7,5},{8,10},{9,11},{10,... | collective-permute-start | bytes 786440 | tf_op jit(solution)/shard_map/ppermute | solution.py:427
  98.5 15.3 %collective-permute-start.22 = (bf16[32,4096]{1,0:T(8,128)(2,1)S(1)}, bf16[32,4096]{1,0:T(8,128)(2,1)S(1)}, u32[]{:S(2)}, u32[]{:S(2)}) collective-permute-start(bf16[32,4096]{1,0:T(8,128)(2,1)S(1)} %get-tuple-element.102), channel_id=1, source_target_pairs={{0,2},{1,3},{2,0},{3,1},{4,6},{5,7},{6,4},{7,5},{8,10},{9,11},{10,... | collective-permute-start | bytes 786440 | tf_op jit(solution)/shard_map/ppermute | solution.py:427
  108.7 13.3 %collective-permute-start.19 = (bf16[32,4096]{1,0:T(8,128)(2,1)S(1)}, bf16[32,4096]{1,0:T(8,128)(2,1)S(1)}, u32[]{:S(2)}, u32[]{:S(2)}) collective-permute-start(bf16[32,4096]{1,0:T(8,128)(2,1)S(1)} %get-tuple-element.96), channel_id=1, source_target_pairs={{0,2},{1,3},{2,0},{3,1},{4,6},{5,7},{6,4},{7,5},{8,10},{9,11},{10,... | collective-permute-start | bytes 786440 | tf_op jit(solution)/shard_map/ppermute | solution.py:427
  109.8 15.3 %collective-permute-start.20 = (bf16[32,4096]{1,0:T(8,128)(2,1)S(1)}, bf16[32,4096]{1,0:T(8,128)(2,1)S(1)}, u32[]{:S(2)}, u32[]{:S(2)}) collective-permute-start(bf16[32,4096]{1,0:T(8,128)(2,1)S(1)} %get-tuple-element.98), channel_id=1, source_target_pairs={{0,2},{1,3},{2,0},{3,1},{4,6},{5,7},{6,4},{7,5},{8,10},{9,11},{10,... | collective-permute-start | bytes 786440 | tf_op jit(solution)/shard_map/ppermute | solution.py:427
  119.9 16.4 %collective-permute-start.24 = (bf16[32,4096]{1,0:T(8,128)(2,1)S(1)}, bf16[32,4096]{1,0:T(8,128)(2,1)S(1)}, u32[]{:S(2)}, u32[]{:S(2)}) collective-permute-start(bf16[32,4096]{1,0:T(8,128)(2,1)S(1)} %get-tuple-element.112), channel_id=1, source_target_pairs={{0,2},{1,3},{2,0},{3,1},{4,6},{5,7},{6,4},{7,5},{8,10},{9,11},{10,... | collective-permute-start | bytes 786440 | tf_op jit(solution)/shard_map/ppermute | solution.py:427
  121.0 15.3 %collective-permute-start.25 = (bf16[32,4096]{1,0:T(8,128)(2,1)S(1)}, bf16[32,4096]{1,0:T(8,128)(2,1)S(1)}, u32[]{:S(2)}, u32[]{:S(2)}) collective-permute-start(bf16[32,4096]{1,0:T(8,128)(2,1)S(1)} %get-tuple-element.114), channel_id=1, source_target_pairs={{0,2},{1,3},{2,0},{3,1},{4,6},{5,7},{6,4},{7,5},{8,10},{9,11},{10,... | collective-permute-start | bytes 786440 | tf_op jit(solution)/shard_map/ppermute | solution.py:427
  129.1 12.0 %collective-permute-start.23 = (bf16[32,4096]{1,0:T(8,128)(2,1)S(1)}, bf16[32,4096]{1,0:T(8,128)(2,1)S(1)}, u32[]{:S(2)}, u32[]{:S(2)}) collective-permute-start(bf16[32,4096]{1,0:T(8,128)(2,1)S(1)} %get-tuple-element.110), channel_id=1, source_target_pairs={{0,2},{1,3},{2,0},{3,1},{4,6},{5,7},{6,4},{7,5},{8,10},{9,11},{10,... | collective-permute-start | bytes 786440 | tf_op jit(solution)/shard_map/ppermute | solution.py:427

commit v4 on v3

--- a/solution.py
+++ b/solution.py
@@ -15,6 +15,7 @@
 WIDTH = 256
 REACH = 64
 EDGE = 4096
+EARLY = 4096
 VMEM = pl.BlockSpec(memory_space=pltpu.VMEM)
 
 
@@ -74,8 +75,11 @@
     return jnp.concatenate([out[i * rows : (i + 1) * rows] for i in range(bins // WIDTH)], axis=1)
 
 
-def sketch_kernel(steps, taps, block, prev, after, low, high, probes, sketch, band, first, final):
+def sketch_kernel(steps, taps, block, prev, after, even, odd, probes, sketch, band, first, final):
     i = pl.program_id(0)
+    lower = lax.rem(lax.axis_index("mz"), 2) == 0
+    low = jnp.where(lower, odd[...], even[...])
+    high = jnp.where(lower, even[...], odd[...])
 
     @pl.when(i == 0)
     def _():
@@ -83,9 +87,9 @@
         sketch[...] = jnp.zeros_like(sketch)
 
     cleaned = clean(
-        jnp.where(i == 0, low[...], prev[...]),
+        jnp.where(i == 0, low, prev[...]),
         block[...],
-        jnp.where(i == steps - 1, high[...], after[...]),
+        jnp.where(i == steps - 1, high, after[...]),
         band[...],
     )
     sketch[...] += jnp.dot(cleaned, probes[...], preferred_element_type=F32)
@@ -106,6 +110,21 @@
 
 def whole(shape):
     return pl.BlockSpec(shape, lambda i: (0, 0))
+
+
+def at(shape, place):
+    return pl.BlockSpec(
+        tuple(pl.Element(n) for n in shape), lambda i: (0, place(i) * TILE)
+    )
+
+
+def inner_specs(rows, size, start):
+    first, per = start // TILE, size // TILE
+    return [
+        at((rows, size), lambda i: first + i * per),
+        at((rows, TILE), lambda i: first + i * per - 1),
+        at((rows, TILE), lambda i: first + i * per + per),
+    ]
 
 
 def block_specs(rows, size, first, last):
@@ -117,7 +136,7 @@
     ]
 
 
-def sketch_of(taps, spectra, low, high, probes, edge):
+def sketch_of(taps, spectra, even, odd, probes, edge):
     rows, bins = spectra.shape
     size = math.gcd(bins, 8192)
     steps = bins // size
@@ -127,7 +146,7 @@
         grid=(steps,),
         in_specs=[whole(taps.shape)]
         + block_specs(rows, size, 0, bins // TILE - 1)
-        + [whole(low.shape), whole(high.shape)]
+        + [whole(even.shape), whole(odd.shape)]
         + [pl.BlockSpec((size, columns), lambda i: (i, 0))],
         out_specs=[
             whole((rows, columns)),
@@ -143,7 +162,7 @@
         ],
         cost_estimate=COST,
         compiler_params=params(48),
-    )(taps, spectra, spectra, spectra, low, high, probes)
+    )(taps, spectra, spectra, spectra, even, odd, probes)
 
 
 def total_kernel(count, *refs):
@@ -217,16 +236,14 @@
         copy.start()
     sketches = [ref[...] for ref in refs[:count]]
     size = sketches[0].shape[1]
-    grams = [
-        lax.dot_general(
-            one, one, (((0,), (0,)), ((), ())), precision=HIGHEST, preferred_element_type=F32
-        )
-        for one in sketches
-    ]
-    inverse = inverse_factor(pairwise(grams) / float(rows * len(sketches)))
-    both = jnp.concatenate(sketches[: turned.shape[1] // rows], axis=0)
+    stacked = jnp.concatenate(sketches, axis=0)
+    gram = lax.dot_general(
+        stacked, stacked, (((0,), (0,)), ((), ())), precision=HIGHEST, preferred_element_type=F32
+    )
+    inverse = inverse_factor(gram / float(stacked.shape[0]))
+    used = stacked[: turned.shape[1]]
     across = lax.dot_general(
-        inverse, both, (((1,), (1,)), ((), ())), precision=HIGHEST, preferred_element_type=F32
+        inverse, used, (((1,), (1,)), ((), ())), precision=HIGHEST, preferred_element_type=F32
     )
     basis[...] = across[:, :rows].T.astype(BF16)
     share = size // (2 * chips)
@@ -295,13 +312,13 @@
 
 
 def project(turned, band, spectra, near, start, size, count, factor, chips, wait):
-    rows, bins = spectra.shape
+    rows = spectra.shape[0]
     share = turned.shape[0] // chips
     return pl.pallas_call(
         functools.partial(project_kernel, count, factor, chips),
         grid=(count,),
         in_specs=[whole(turned.shape), whole(band.shape)]
-        + block_specs(rows, size, start // size, bins // TILE - 1) * 2
+        + inner_specs(rows, size, start) * 2
         + [ANY] * len(wait),
         out_specs=[whole((share, size))] * (count * chips) + [whole((8, TILE))],
         out_shape=[jax.ShapeDtypeStruct((share, size), BF16)] * (count * chips)
@@ -327,17 +344,16 @@
 
 
 def project_whole(out, turned, band, spectra, near, far, start, factor, wait):
-    rows, bins = spectra.shape
+    rows = spectra.shape[0]
     size = far[0].shape[1] - 2 * TILE
-    first = start // size
     return pl.pallas_call(
         functools.partial(project_whole_kernel, factor),
         grid=(1,),
         in_specs=[whole(turned.shape), whole(band.shape)]
-        + block_specs(rows, size, first, bins // TILE - 1) * 2
+        + inner_specs(rows, size, start) * 2
         + [whole(one.shape) for one in far]
         + [ANY] * (1 + len(wait)),
-        out_specs=[pl.BlockSpec((out.shape[0], size), lambda i: (0, first)), whole((8, TILE))],
+        out_specs=[at((out.shape[0], size), lambda i: start // TILE), whole((8, TILE))],
         out_shape=[
             jax.ShapeDtypeStruct(out.shape, BF16),
             jax.ShapeDtypeStruct((8, TILE), F32),
@@ -368,9 +384,9 @@
         grid=(len(blocks),),
         in_specs=[whole((share, size))] * len(parts) + [ANY] * (len(extra) + len(wait)),
         out_specs=[
-            pl.BlockSpec(
+            at(
                 (share, size),
-                lambda i: (0, jnp.where(i == 0, starts[0] // size, starts[-1] // size)),
+                lambda i: jnp.where(i == 0, starts[0] // TILE, starts[-1] // TILE),
             ),
             whole((8, TILE)),
         ],
@@ -391,20 +407,24 @@
     chips = pix // 2
     factor = 1.0 / math.sqrt(float(rows * pix))
 
-    up = [(i, i + 1) for i in range(depth - 1)]
-    down = [(i + 1, i) for i in range(depth - 1)]
-    low = lax.ppermute(spectra[:, bins - TILE :], "mz", up)
-    high = lax.ppermute(spectra[:, :TILE], "mz", down)
+    def swap(first, tile):
+        pairs = [(i, i + 1) for i in range(first, depth - 1, 2)]
+        return lax.ppermute(tile, "mz", pairs + [(b, a) for a, b in pairs])
+
+    lower = lax.rem(lax.axis_index("mz"), 2) == 0
+    head, tail = spectra[:, :TILE], spectra[:, bins - TILE :]
+    even = swap(0, jnp.where(lower, tail, head))
+    odd = swap(1, jnp.where(lower, head, tail))
     taps = jnp.pad(kernel.astype(F32), (REACH, 2 * WIDTH - REACH - kernel.shape[0]))[None]
 
     near = partner(spectra, "pix", 1)
     edge = math.gcd(bins // 2, EDGE)
     far = []
     inner = edge
-    if chips == 2 and bins >= 6 * edge:
-        far = [partner(spectra[:, edge - TILE : 2 * edge + TILE], "pix", 2)]
-        inner = 2 * edge
-    partial_sketch, band, first, final = sketch_of(taps, spectra, low, high, probes, edge)
+    if chips == 2 and bins >= 8 * EARLY:
+        inner = edge + EARLY
+        far = [partner(spectra[:, edge - TILE : inner + TILE], "pix", 2)]
+    partial_sketch, band, first, final = sketch_of(taps, spectra, even, odd, probes, edge)
     ends = [first, partner(first, "pix", 1), final, partner(final, "pix", 1)]
     sketch = total_of(spread(partial_sketch, "mz"), far)
     basis, turned, *mine = basis_of(
@@ -428,14 +448,18 @@
 
     out, recent = None, []
     before = ([across(mine[:chips]), across(mine[chips:])], (0, bins - edge))
-    for start in range(inner, bins - edge, 2 * edge):
-        count = min(2, (bins - edge - start) // edge)
+    start, stop = inner, bins - edge
+    while start < stop:
+        size = min(edge, stop - start)
+        count = min(2, (stop - start) // size)
         *mine, done = project(
-            turned, band, spectra, near, start, edge, count, factor, chips, recent
+            turned, band, spectra, near, start, size, count, factor, chips, recent
         )
         blocks = [across(mine[n * chips : (n + 1) * chips]) for n in range(count)]
         recent = [done]
-        if far and start + count * edge == bins - edge:
+        places = tuple(start + n * size for n in range(count))
+        start += count * size
+        if far and start == stop:
             pair = [far[0], partner(far[0], "pix", 1)]
             out, done = project_whole(
                 out, turned, band, spectra, near, pair, edge, factor, recent
@@ -443,7 +467,7 @@
             recent = [done]
         out, done = finish(out, *before, bins, recent)
         recent = [done]
-        before = (blocks, tuple(start + n * edge for n in range(count)))
+        before = (blocks, places)
     out, done = finish(out, *before, bins, recent)
     return (basis, out)
 

time: 142 us -> 141 us (level)
    ppermute x2, starting transfers between devices: 5.78 us -> 3.3 us  [swap(): return lax.ppermute(tile, 'mz', pairs + [(b, a) for a, b in pairs])]
    ppermute x10, starting transfers between devices: 9.52 us -> 11 us  [partner(): return lax.ppermute(x, axis, [(i, i ^ shift) for i in range(count)])]
where the time goes in v4:
time: 141 us
  Pallas kernels  72.5 us (51%)
  waiting for transfers between devices  35 us (25%)
  starting transfers between devices  29.7 us (21%)
  other arithmetic  1.51 us (1%)
    pallas_call x7, Pallas kernels, project(): pl.pallas_call(functools.partial(project_kernel, count, factor, chips), g...  34.2 us
    ppermute x15, waiting for transfers between devices, across(): lax.ppermute(mine[m], 'pix', routes[m])  25.5 us
    pallas_call x1, Pallas kernels, sketch_of(): pl.pallas_call(functools.partial(sketch_kernel, steps), grid=(steps,), in...  19.4 us
    ppermute x15, starting transfers between devices, across(): lax.ppermute(mine[m], 'pix', routes[m])  15.4 us
    ppermute x10, starting transfers between devices, partner(): return lax.ppermute(x, axis, [(i, i ^ shift) for i in range(count)])  11 us
    ppermute x10, waiting for transfers between devices, partner(): return lax.ppermute(x, axis, [(i, i ^ shift) for i in range(count)])  9.55 us
    pallas_call x8, Pallas kernels, finish(): pl.pallas_call(functools.partial(finish_kernel, len(blocks), len(blocks[0...  6.79 us
    pallas_call x1, Pallas kernels, basis_of(): pl.pallas_call(functools.partial(basis_kernel, chips, factor, len(sketche...  6.07 us
  transfers between devices with their start and end apart: 27, of which 12 were waited for; matrix products, arithmetic and copies ran while one was open for 2% of the time, Pallas kernels for 51%

profile of v4, /device:TPU:0, one launch (start us, length us, event | category | flops | bytes accessed | tf_op | source)
XLA Modules:
  0.0 140.8 jit_solution(2359673748135362530)
XLA Ops:
  0.6 0.5 collective-permute-start.10
  1.1 0.8 broadcast_select_fusion
  1.9 2.7 %collective-permute-start = (bf16[128,128]{1,0:T(8,128)(2,1)S(1)}, bf16[128,128]{1,0:T(8,128)(2,1)S(1)}, u32[]{:S(2)}, u32[]{:S(2)}) collective-permute-start(bf16[128,128]{1,0:T(8,128)(2,1)S(1)} %get-tuple-element.123), channel_id=1, source_target_pairs={{0,4},{8,12},{4,0},{12,8},{1,5},{9,13},{5,1},{13,9},{2,6},{10,14},... | collective-permute-start | bytes 98312 | tf_op jit(solution)/shard_map/ppermute | solution.py:412
  4.6 0.7 collective-permute-start.1
  5.2 1.3 slice.11
  6.6 1.6 %collective-permute-start.4 = (bf16[128,4352]{1,0:T(8,128)(2,1)S(1)}, bf16[128,4352]{1,0:T(8,128)(2,1)}, u32[]{:S(2)}, u32[]{:S(2)}) collective-permute-start(bf16[128,4352]{1,0:T(8,128)(2,1)S(1)} %slice.11), channel_id=1, source_target_pairs={{0,2},{1,3},{2,0},{3,1},{4,6},{5,7},{6,4},{7,5},{8,10},{9,11},{10,... | collective-permute-start | bytes 3342344 | tf_op jit(solution)/shard_map/ppermute | solution.py:31
  8.1 0.7 pad_convert_fusion
  8.9 19.4 %shard_map.50 = (f32[128,128]{1,0:T(8,128)S(1)}, bf16[512,256]{1,0:T(8,128)(2,1)S(1)}, bf16[128,4096]{1,0:T(8,128)(2,1)S(1)}, bf16[128,4096]{1,0:T(8,128)(2,1)S(1)}) custom-call(f32[1,512]{1,0:T(1,128)S(1)} %bitcast.1, bf16[128,65536]{1,0:T(8,128)(2,1)} %own_high.1, bf16[128,65536]{1,0:T(8,128)(2,1)} %own_high.1, bf16[128,65536]{1,0:T(8,128)(2,1)} %own_high.1, ...), custom_call_target="tpu_custom_call" | custom-call | flops 1 | bytes 1 | tf_op jit(solution)/shard_map/pallas_call | solution.py:144
  28.2 0.1 collective-permute-start.8
  28.3 0.5 collective-permute-start.9
  28.8 4.4 %collective-permute-start.2 = (f32[128,128]{1,0:T(8,128)S(1)}, f32[128,128]{1,0:T(8,128)S(1)}, u32[]{:S(2)}, u32[]{:S(2)}) collective-permute-start(f32[128,128]{1,0:T(8,128)S(1)} %get-tuple-element.62.refs_0_), channel_id=1, source_target_pairs={{0,4},{4,0},{8,12},{12,8},{1,5},{5,1},{9,13},{13,9},{2,6},{6,2},{1... | collective-permute-start | bytes 196616 | tf_op jit(solution)/shard_map/ppermute | solution.py:31
  33.2 2.3 %collective-permute-done.2.refs_1_ = f32[128,128]{1,0:T(8,128)S(1)} collective-permute-done((f32[128,128]{1,0:T(8,128)S(1)}, f32[128,128]{1,0:T(8,128)S(1)}, u32[]{:S(2)}, u32[]{:S(2)}) %collective-permute-start.2) | collective-permute-done | bytes 65568 | tf_op jit(solution)/shard_map/ppermute | solution.py:31
  35.6 1.7 %collective-permute-start.3 = (f32[128,128]{1,0:T(8,128)S(1)}, f32[128,128]{1,0:T(8,128)S(1)}, u32[]{:S(2)}, u32[]{:S(2)}) collective-permute-start(f32[128,128]{1,0:T(8,128)S(1)} %shard_map.51.refs_0_), channel_id=1, source_target_pairs={{0,8},{4,12},{8,0},{12,4},{1,9},{5,13},{9,1},{13,5},{2,10},{6,14},... | collective-permute-start | bytes 196616 | tf_op jit(solution)/shard_map/ppermute | solution.py:31
  37.3 4.0 %collective-permute-done.3.refs_1_ = f32[128,128]{1,0:T(8,128)S(1)} collective-permute-done((f32[128,128]{1,0:T(8,128)S(1)}, f32[128,128]{1,0:T(8,128)S(1)}, u32[]{:S(2)}, u32[]{:S(2)}) %collective-permute-start.3) | collective-permute-done | bytes 65568 | tf_op jit(solution)/shard_map/ppermute | solution.py:31
  41.2 0.1 collective-permute-start.5
  41.3 0.6 collective-permute-start.6
  41.9 0.0 collective-permute-done.8.refs_5_
  41.9 1.3 collective-permute-start.7
  43.2 0.0 collective-permute-done.9.refs_7_
  43.2 0.3 collective-permute-start.26
  43.5 0.0 collective-permute-done.5.refs_1_
  43.5 2.7 %collective-permute-done.6.refs_2_ = f32[128,128]{1,0:T(8,128)S(1)} collective-permute-done((f32[128,128]{1,0:T(8,128)S(1)}, f32[128,128]{1,0:T(8,128)S(1)}, u32[]{:S(2)}, u32[]{:S(2)}) %collective-permute-start.6) | collective-permute-done | bytes 65568 | tf_op jit(solution)/shard_map/ppermute | solution.py:31
  46.3 0.5 collective-permute-done.7.refs_3_
  46.8 6.1 %shard_map.53 = (bf16[128,128]{1,0:T(8,128)(2,1)}, bf16[64,512]{1,0:T(8,128)(2,1)S(1)}, bf16[32,4096]{1,0:T(8,128)(2,1)S(1)}, bf16[32,4096]{1,0:T(8,128)(2,1)S(1...) custom-call(f32[128,128]{1,0:T(8,128)S(1)} %shard_map.52.refs_0_, ...), custom_call_target="tpu_custom_call" | custom-call | flops 1 | bytes 1 | tf_op jit(solution)/shard_map/pallas_call | solution.py:268
  52.9 0.8 collective-permute-start.13
  53.6 1.3 collective-permute-start.14
  54.9 0.0 collective-permute-done.10.refs_3_.refs_4_.refs_5_.near.refs_0_.refs_1_
  55.0 5.2 %shard_map.54 = (bf16[32,4096]{1,0:T(8,128)(2,1)S(1)}, bf16[32,4096]{1,0:T(8,128)(2,1)S(1)}, bf16[32,4096]{1,0:T(8,128)(2,1)S(1)}, bf16[32,4096]{1,0:T(8,128)(2,1)S(1)}, f32[8,128]{1,0:T(8,128)S(1)}) custom-call(bf16[64,512]{1,0:T(8,128)(2,1)S(1)} %get-tuple-element.66.turned, bf16[512,256]{1,0:T(8,128)(2,1)S(1)} %get-tuple-element.67.band, ...), custom_call_target="tpu_custom_call" | custom-call | flops 1 | bytes 1 | tf_op jit(solution)/shard_map/pallas_call | solution.py:317
  60.1 0.8 collective-permute-start.11
  60.9 1.3 collective-permute-start.12
  62.2 5.4 %collective-permute-done.14.refs_3_ = bf16[32,4096]{1,0:T(8,128)(2,1)S(1)} collective-permute-done((bf16[32,4096]{1,0:T(8,128)(2,1)S(1)}, bf16[32,4096]{1,0:T(8,128)(2,1)S(1)}, u32[]{:S(2)}, u32[]{:S(2)}) %collective-permute-start.14) | collective-permute-done | bytes 262176 | tf_op jit(solution)/shard_map/ppermute | solution.py:447
  67.7 0.9 shard_map.55
  68.5 5.2 %shard_map.56 = (bf16[32,4096]{1,0:T(8,128)(2,1)S(1)}, bf16[32,4096]{1,0:T(8,128)(2,1)S(1)}, bf16[32,4096]{1,0:T(8,128)(2,1)S(1)}, bf16[32,4096]{1,0:T(8,128)(2,1)S(1)}, f32[8,128]{1,0:T(8,128)S(1)}) custom-call(bf16[64,512]{1,0:T(8,128)(2,1)S(1)} %get-tuple-element.66.turned, bf16[512,256]{1,0:T(8,128)(2,1)S(1)} %get-tuple-element.67.band, ...), custom_call_target="tpu_custom_call" | custom-call | flops 1 | bytes 1 | tf_op jit(solution)/shard_map/pallas_call | solution.py:317
  73.7 0.8 collective-permute-start.17
  74.5 1.3 collective-permute-start.18
  75.8 3.1 %collective-permute-done.12.refs_3_ = bf16[32,4096]{1,0:T(8,128)(2,1)S(1)} collective-permute-done((bf16[32,4096]{1,0:T(8,128)(2,1)S(1)}, bf16[32,4096]{1,0:T(8,128)(2,1)S(1)}, u32[]{:S(2)}, u32[]{:S(2)}) %collective-permute-start.12) | collective-permute-done | bytes 262176 | tf_op jit(solution)/shard_map/ppermute | solution.py:447
  78.9 0.9 shard_map.57
  79.8 5.2 %shard_map.58 = (bf16[32,4096]{1,0:T(8,128)(2,1)S(1)}, bf16[32,4096]{1,0:T(8,128)(2,1)S(1)}, bf16[32,4096]{1,0:T(8,128)(2,1)S(1)}, bf16[32,4096]{1,0:T(8,128)(2,1)S(1)}, f32[8,128]{1,0:T(8,128)S(1)}) custom-call(bf16[64,512]{1,0:T(8,128)(2,1)S(1)} %get-tuple-element.66.turned, bf16[512,256]{1,0:T(8,128)(2,1)S(1)} %get-tuple-element.67.band, ...), custom_call_target="tpu_custom_call" | custom-call | flops 1 | bytes 1 | tf_op jit(solution)/shard_map/pallas_call | solution.py:317
  84.9 0.8 collective-permute-start.15
  85.7 1.3 collective-permute-start.16
  87.0 3.1 %collective-permute-done.18.refs_3_ = bf16[32,4096]{1,0:T(8,128)(2,1)S(1)} collective-permute-done((bf16[32,4096]{1,0:T(8,128)(2,1)S(1)}, bf16[32,4096]{1,0:T(8,128)(2,1)S(1)}, u32[]{:S(2)}, u32[]{:S(2)}) %collective-permute-start.18) | collective-permute-done | bytes 262176 | tf_op jit(solution)/shard_map/ppermute | solution.py:447
  90.1 0.9 shard_map.59
  91.0 5.2 %shard_map.60 = (bf16[32,4096]{1,0:T(8,128)(2,1)S(1)}, bf16[32,4096]{1,0:T(8,128)(2,1)S(1)}, bf16[32,4096]{1,0:T(8,128)(2,1)S(1)}, bf16[32,4096]{1,0:T(8,128)(2,1)S(1)}, f32[8,128]{1,0:T(8,128)S(1)}) custom-call(bf16[64,512]{1,0:T(8,128)(2,1)S(1)} %get-tuple-element.66.turned, bf16[512,256]{1,0:T(8,128)(2,1)S(1)} %get-tuple-element.67.band, ...), custom_call_target="tpu_custom_call" | custom-call | flops 1 | bytes 1 | tf_op jit(solution)/shard_map/pallas_call | solution.py:317
  96.2 0.8 collective-permute-start.21
  97.0 1.3 collective-permute-start.22
  98.3 3.1 %collective-permute-done.16.refs_3_ = bf16[32,4096]{1,0:T(8,128)(2,1)S(1)} collective-permute-done((bf16[32,4096]{1,0:T(8,128)(2,1)S(1)}, bf16[32,4096]{1,0:T(8,128)(2,1)S(1)}, u32[]{:S(2)}, u32[]{:S(2)}) %collective-permute-start.16) | collective-permute-done | bytes 262176 | tf_op jit(solution)/shard_map/ppermute | solution.py:447
  101.4 0.9 shard_map.61
  102.2 5.2 %shard_map.62 = (bf16[32,4096]{1,0:T(8,128)(2,1)S(1)}, bf16[32,4096]{1,0:T(8,128)(2,1)S(1)}, bf16[32,4096]{1,0:T(8,128)(2,1)S(1)}, bf16[32,4096]{1,0:T(8,128)(2,1)S(1)}, f32[8,128]{1,0:T(8,128)S(1)}) custom-call(bf16[64,512]{1,0:T(8,128)(2,1)S(1)} %get-tuple-element.66.turned, bf16[512,256]{1,0:T(8,128)(2,1)S(1)} %get-tuple-element.67.band, ...), custom_call_target="tpu_custom_call" | custom-call | flops 1 | bytes 1 | tf_op jit(solution)/shard_map/pallas_call | solution.py:317
  107.4 0.8 collective-permute-start.19
  108.2 1.3 collective-permute-start.20
  109.5 3.1 %collective-permute-done.22.refs_3_ = bf16[32,4096]{1,0:T(8,128)(2,1)S(1)} collective-permute-done((bf16[32,4096]{1,0:T(8,128)(2,1)S(1)}, bf16[32,4096]{1,0:T(8,128)(2,1)S(1)}, u32[]{:S(2)}, u32[]{:S(2)}) %collective-permute-start.22) | collective-permute-done | bytes 262176 | tf_op jit(solution)/shard_map/ppermute | solution.py:447
  112.6 0.9 shard_map.63
  113.5 5.2 %shard_map.64 = (bf16[32,4096]{1,0:T(8,128)(2,1)S(1)}, bf16[32,4096]{1,0:T(8,128)(2,1)S(1)}, bf16[32,4096]{1,0:T(8,128)(2,1)S(1)}, bf16[32,4096]{1,0:T(8,128)(2,1)S(1)}, f32[8,128]{1,0:T(8,128)S(1)}) custom-call(bf16[64,512]{1,0:T(8,128)(2,1)S(1)} %get-tuple-element.66.turned, bf16[512,256]{1,0:T(8,128)(2,1)S(1)} %get-tuple-element.67.band, ...), custom_call_target="tpu_custom_call" | custom-call | flops 1 | bytes 1 | tf_op jit(solution)/shard_map/pallas_call | solution.py:317
  118.6 0.8 collective-permute-start.24
  119.4 1.3 collective-permute-start.25
  120.7 3.1 %collective-permute-done.20.refs_3_ = bf16[32,4096]{1,0:T(8,128)(2,1)S(1)} collective-permute-done((bf16[32,4096]{1,0:T(8,128)(2,1)S(1)}, bf16[32,4096]{1,0:T(8,128)(2,1)S(1)}, u32[]{:S(2)}, u32[]{:S(2)}) %collective-permute-start.20) | collective-permute-done | bytes 262176 | tf_op jit(solution)/shard_map/ppermute | solution.py:447
  123.8 0.9 shard_map.65
  124.7 3.2 %shard_map.66 = (bf16[32,4096]{1,0:T(8,128)(2,1)S(1)}, bf16[32,4096]{1,0:T(8,128)(2,1)S(1)}, f32[8,128]{1,0:T(8,128)S(1)}) custom-call(bf16[64,512]{1,0:T(8,128)(2,1)S(1)} %get-tuple-element.66.turned, bf16[512,256]{1,0:T(8,128)(2,1)S(1)} %get-tuple-element.67.band, bf16[128,65536]{1,0:T(8,128)(2,1)} %own_high.1, bf16[128,65536]{1,0:T(8,128)(2,1)} %own_high.1, ...), custom_call_target="tpu_custom_call" | custom-call | flops 1 | bytes 1 | tf_op jit(solution)/shard_map/pallas_call | solution.py:317
  127.9 0.8 collective-permute-start.23
  128.7 6.0 %shard_map.67 = (bf16[32,65536]{1,0:T(8,128)(2,1)}, f32[8,128]{1,0:T(8,128)S(1)}) custom-call(bf16[64,512]{1,0:T(8,128)(2,1)S(1)} %get-tuple-element.66.turned, bf16[512,256]{1,0:T(8,128)(2,1)S(1)} %get-tuple-element.67.band, bf16[128,65536]{1,0:T(8,128)(2,1)} %own_high.1, bf16[128,65536]{1,0:T(8,128)(2,1)} %own_high.1, ...), custom_call_target="tpu_custom_call", output_to_operand_aliasing={{0}: (10, {})} | custom-call | flops 1 | bytes 1 | tf_op jit(solution)/shard_map/pallas_call | solution.py:349
  134.7 0.4 collective-permute-done.25.refs_3_
  135.1 0.9 shard_map.68
  135.9 4.1 %collective-permute-done.23.refs_1_ = bf16[32,4096]{1,0:T(8,128)(2,1)S(1)} collective-permute-done((bf16[32,4096]{1,0:T(8,128)(2,1)S(1)}, bf16[32,4096]{1,0:T(8,128)(2,1)S(1)}, u32[]{:S(2)}, u32[]{:S(2)}) %collective-permute-start.23) | collective-permute-done | bytes 262176 | tf_op jit(solution)/shard_map/ppermute | solution.py:447
  140.1 0.8 shard_map.69
  (13 shorter events, 0.0 us)
Async XLA Ops:
  0.6 54.3 %collective-permute-start.10 = (bf16[128,65536]{1,0:T(8,128)(2,1)}, bf16[128,65536]{1,0:T(8,128)(2,1)}, u32[]{:S(2)}, u32[]{:S(2)}) collective-permute-start(bf16[128,65536]{1,0:T(8,128)(2,1)} %own_high.1), channel_id=1, source_target_pairs={{0,1},{1,0},{2,3},{3,2},{4,5},{5,4},{6,7},{7,6},{8,9},{9,8},{10,11... | collective-permute-start | bytes 50331656 | tf_op jit(solution)/shard_map/ppermute | solution.py:31
  1.9 6.9 %collective-permute-start = (bf16[128,128]{1,0:T(8,128)(2,1)S(1)}, bf16[128,128]{1,0:T(8,128)(2,1)S(1)}, u32[]{:S(2)}, u32[]{:S(2)}) collective-permute-start(bf16[128,128]{1,0:T(8,128)(2,1)S(1)} %get-tuple-element.123), channel_id=1, source_target_pairs={{0,4},{8,12},{4,0},{12,8},{1,5},{9,13},{5,1},{13,9},{2,6},{10,14},... | collective-permute-start | bytes 98312 | tf_op jit(solution)/shard_map/ppermute | solution.py:412
  4.6 4.3 %collective-permute-start.1 = (bf16[128,128]{1,0:T(8,128)(2,1)S(1)}, bf16[128,128]{1,0:T(8,128)(2,1)S(1)}, u32[]{:S(2)}, u32[]{:S(2)}) collective-permute-start(bf16[128,128]{1,0:T(8,128)(2,1)S(1)} %get-tuple-element.122), channel_id=1, source_target_pairs={{4,8},{8,4},{5,9},{9,5},{6,10},{10,6},{7,11},{11,7},{20,24},{24,20... | collective-permute-start | bytes 98312 | tf_op jit(solution)/shard_map/ppermute | solution.py:412
  6.6 34.7 %collective-permute-start.4 = (bf16[128,4352]{1,0:T(8,128)(2,1)S(1)}, bf16[128,4352]{1,0:T(8,128)(2,1)}, u32[]{:S(2)}, u32[]{:S(2)}) collective-permute-start(bf16[128,4352]{1,0:T(8,128)(2,1)S(1)} %slice.11), channel_id=1, source_target_pairs={{0,2},{1,3},{2,0},{3,1},{4,6},{5,7},{6,4},{7,5},{8,10},{9,11},{10,... | collective-permute-start | bytes 3342344 | tf_op jit(solution)/shard_map/ppermute | solution.py:31
  28.2 13.7 %collective-permute-start.8 = (bf16[128,4096]{1,0:T(8,128)(2,1)S(1)}, bf16[128,4096]{1,0:T(8,128)(2,1)S(1)}, u32[]{:S(2)}, u32[]{:S(2)}) collective-permute-start(bf16[128,4096]{1,0:T(8,128)(2,1)S(1)} %get-tuple-element.63.refs_4_), channel_id=1, source_target_pairs={{0,1},{1,0},{2,3},{3,2},{4,5},{5,4},{6,7},{7,6},{8,9},{9,8},{10,11... | collective-permute-start | bytes 3145736 | tf_op jit(solution)/shard_map/ppermute | solution.py:31
  28.3 14.9 %collective-permute-start.9 = (bf16[128,4096]{1,0:T(8,128)(2,1)S(1)}, bf16[128,4096]{1,0:T(8,128)(2,1)S(1)}, u32[]{:S(2)}, u32[]{:S(2)}) collective-permute-start(bf16[128,4096]{1,0:T(8,128)(2,1)S(1)} %get-tuple-element.64.refs_6_), channel_id=1, source_target_pairs={{0,1},{1,0},{2,3},{3,2},{4,5},{5,4},{6,7},{7,6},{8,9},{9,8},{10,11... | collective-permute-start | bytes 3145736 | tf_op jit(solution)/shard_map/ppermute | solution.py:31
  28.8 6.7 %collective-permute-start.2 = (f32[128,128]{1,0:T(8,128)S(1)}, f32[128,128]{1,0:T(8,128)S(1)}, u32[]{:S(2)}, u32[]{:S(2)}) collective-permute-start(f32[128,128]{1,0:T(8,128)S(1)} %get-tuple-element.62.refs_0_), channel_id=1, source_target_pairs={{0,4},{4,0},{8,12},{12,8},{1,5},{5,1},{9,13},{13,9},{2,6},{6,2},{1... | collective-permute-start | bytes 196616 | tf_op jit(solution)/shard_map/ppermute | solution.py:31
  35.6 5.7 %collective-permute-start.3 = (f32[128,128]{1,0:T(8,128)S(1)}, f32[128,128]{1,0:T(8,128)S(1)}, u32[]{:S(2)}, u32[]{:S(2)}) collective-permute-start(f32[128,128]{1,0:T(8,128)S(1)} %shard_map.51.refs_0_), channel_id=1, source_target_pairs={{0,8},{4,12},{8,0},{12,4},{1,9},{5,13},{9,1},{13,5},{2,10},{6,14},... | collective-permute-start | bytes 196616 | tf_op jit(solution)/shard_map/ppermute | solution.py:31
  41.2 2.3 %collective-permute-start.5 = (f32[128,128]{1,0:T(8,128)S(1)}, f32[128,128]{1,0:T(8,128)S(1)}, u32[]{:S(2)}, u32[]{:S(2)}) collective-permute-start(f32[128,128]{1,0:T(8,128)S(1)} %shard_map.52.refs_0_), channel_id=1, source_target_pairs={{0,1},{1,0},{2,3},{3,2},{4,5},{5,4},{6,7},{7,6},{8,9},{9,8},{10,11... | collective-permute-start | bytes 196616 | tf_op jit(solution)/shard_map/ppermute | solution.py:31
  41.3 5.0 %collective-permute-start.6 = (f32[128,128]{1,0:T(8,128)S(1)}, f32[128,128]{1,0:T(8,128)S(1)}, u32[]{:S(2)}, u32[]{:S(2)}) collective-permute-start(f32[128,128]{1,0:T(8,128)S(1)} %shard_map.52.refs_0_), channel_id=1, source_target_pairs={{0,2},{1,3},{2,0},{3,1},{4,6},{5,7},{6,4},{7,5},{8,10},{9,11},{10,... | collective-permute-start | bytes 196616 | tf_op jit(solution)/shard_map/ppermute | solution.py:31
  41.9 4.9 %collective-permute-start.7 = (f32[128,128]{1,0:T(8,128)S(1)}, f32[128,128]{1,0:T(8,128)S(1)}, u32[]{:S(2)}, u32[]{:S(2)}) collective-permute-start(f32[128,128]{1,0:T(8,128)S(1)} %shard_map.52.refs_0_), channel_id=1, source_target_pairs={{0,3},{1,2},{2,1},{3,0},{4,7},{5,6},{6,5},{7,4},{8,11},{9,10},{10,... | collective-permute-start | bytes 196616 | tf_op jit(solution)/shard_map/ppermute | solution.py:31
  43.2 85.5 %collective-permute-start.26 = (bf16[128,4352]{1,0:T(8,128)(2,1)}, bf16[128,4352]{1,0:T(8,128)(2,1)}, u32[]{:S(2)}, u32[]{:S(2)}) collective-permute-start(bf16[128,4352]{1,0:T(8,128)(2,1)} %collective-permute-done.4.refs_2_), channel_id=1, source_target_pairs={{0,1},{1,0},{2,3},{3,2},{4,5},{5,4},{6,7},{7,6},{8,9},{9,8},{10,11... | collective-permute-start | bytes 3342344 | tf_op jit(solution)/shard_map/ppermute | solution.py:31
  52.9 9.4 %collective-permute-start.13 = (bf16[32,4096]{1,0:T(8,128)(2,1)S(1)}, bf16[32,4096]{1,0:T(8,128)(2,1)S(1)}, u32[]{:S(2)}, u32[]{:S(2)}) collective-permute-start(bf16[32,4096]{1,0:T(8,128)(2,1)S(1)} %get-tuple-element.73), channel_id=1, source_target_pairs={{0,2},{1,3},{2,0},{3,1},{4,6},{5,7},{6,4},{7,5},{8,10},{9,11},{10,... | collective-permute-start | bytes 786440 | tf_op jit(solution)/shard_map/ppermute | solution.py:447
  53.6 14.1 %collective-permute-start.14 = (bf16[32,4096]{1,0:T(8,128)(2,1)S(1)}, bf16[32,4096]{1,0:T(8,128)(2,1)S(1)}, u32[]{:S(2)}, u32[]{:S(2)}) collective-permute-start(bf16[32,4096]{1,0:T(8,128)(2,1)S(1)} %get-tuple-element.75), channel_id=1, source_target_pairs={{0,2},{1,3},{2,0},{3,1},{4,6},{5,7},{6,4},{7,5},{8,10},{9,11},{10,... | collective-permute-start | bytes 786440 | tf_op jit(solution)/shard_map/ppermute | solution.py:447
  60.1 15.7 %collective-permute-start.11 = (bf16[32,4096]{1,0:T(8,128)(2,1)S(1)}, bf16[32,4096]{1,0:T(8,128)(2,1)S(1)}, u32[]{:S(2)}, u32[]{:S(2)}) collective-permute-start(bf16[32,4096]{1,0:T(8,128)(2,1)S(1)} %get-tuple-element.69), channel_id=1, source_target_pairs={{0,2},{1,3},{2,0},{3,1},{4,6},{5,7},{6,4},{7,5},{8,10},{9,11},{10,... | collective-permute-start | bytes 786440 | tf_op jit(solution)/shard_map/ppermute | solution.py:447
  60.9 18.0 %collective-permute-start.12 = (bf16[32,4096]{1,0:T(8,128)(2,1)S(1)}, bf16[32,4096]{1,0:T(8,128)(2,1)S(1)}, u32[]{:S(2)}, u32[]{:S(2)}) collective-permute-start(bf16[32,4096]{1,0:T(8,128)(2,1)S(1)} %get-tuple-element.71), channel_id=1, source_target_pairs={{0,2},{1,3},{2,0},{3,1},{4,6},{5,7},{6,4},{7,5},{8,10},{9,11},{10,... | collective-permute-start | bytes 786440 | tf_op jit(solution)/shard_map/ppermute | solution.py:447
  73.7 13.3 %collective-permute-start.17 = (bf16[32,4096]{1,0:T(8,128)(2,1)S(1)}, bf16[32,4096]{1,0:T(8,128)(2,1)S(1)}, u32[]{:S(2)}, u32[]{:S(2)}) collective-permute-start(bf16[32,4096]{1,0:T(8,128)(2,1)S(1)} %get-tuple-element.86), channel_id=1, source_target_pairs={{0,2},{1,3},{2,0},{3,1},{4,6},{5,7},{6,4},{7,5},{8,10},{9,11},{10,... | collective-permute-start | bytes 786440 | tf_op jit(solution)/shard_map/ppermute | solution.py:447
  74.5 15.7 %collective-permute-start.18 = (bf16[32,4096]{1,0:T(8,128)(2,1)S(1)}, bf16[32,4096]{1,0:T(8,128)(2,1)S(1)}, u32[]{:S(2)}, u32[]{:S(2)}) collective-permute-start(bf16[32,4096]{1,0:T(8,128)(2,1)S(1)} %get-tuple-element.88), channel_id=1, source_target_pairs={{0,2},{1,3},{2,0},{3,1},{4,6},{5,7},{6,4},{7,5},{8,10},{9,11},{10,... | collective-permute-start | bytes 786440 | tf_op jit(solution)/shard_map/ppermute | solution.py:447
  84.9 13.3 %collective-permute-start.15 = (bf16[32,4096]{1,0:T(8,128)(2,1)S(1)}, bf16[32,4096]{1,0:T(8,128)(2,1)S(1)}, u32[]{:S(2)}, u32[]{:S(2)}) collective-permute-start(bf16[32,4096]{1,0:T(8,128)(2,1)S(1)} %get-tuple-element.82), channel_id=1, source_target_pairs={{0,2},{1,3},{2,0},{3,1},{4,6},{5,7},{6,4},{7,5},{8,10},{9,11},{10,... | collective-permute-start | bytes 786440 | tf_op jit(solution)/shard_map/ppermute | solution.py:447
  85.7 15.7 %collective-permute-start.16 = (bf16[32,4096]{1,0:T(8,128)(2,1)S(1)}, bf16[32,4096]{1,0:T(8,128)(2,1)S(1)}, u32[]{:S(2)}, u32[]{:S(2)}) collective-permute-start(bf16[32,4096]{1,0:T(8,128)(2,1)S(1)} %get-tuple-element.84), channel_id=1, source_target_pairs={{0,2},{1,3},{2,0},{3,1},{4,6},{5,7},{6,4},{7,5},{8,10},{9,11},{10,... | collective-permute-start | bytes 786440 | tf_op jit(solution)/shard_map/ppermute | solution.py:447
  96.2 13.3 %collective-permute-start.21 = (bf16[32,4096]{1,0:T(8,128)(2,1)S(1)}, bf16[32,4096]{1,0:T(8,128)(2,1)S(1)}, u32[]{:S(2)}, u32[]{:S(2)}) collective-permute-start(bf16[32,4096]{1,0:T(8,128)(2,1)S(1)} %get-tuple-element.100), channel_id=1, source_target_pairs={{0,2},{1,3},{2,0},{3,1},{4,6},{5,7},{6,4},{7,5},{8,10},{9,11},{10,... | collective-permute-start | bytes 786440 | tf_op jit(solution)/shard_map/ppermute | solution.py:447
  97.0 15.6 %collective-permute-start.22 = (bf16[32,4096]{1,0:T(8,128)(2,1)S(1)}, bf16[32,4096]{1,0:T(8,128)(2,1)S(1)}, u32[]{:S(2)}, u32[]{:S(2)}) collective-permute-start(bf16[32,4096]{1,0:T(8,128)(2,1)S(1)} %get-tuple-element.102), channel_id=1, source_target_pairs={{0,2},{1,3},{2,0},{3,1},{4,6},{5,7},{6,4},{7,5},{8,10},{9,11},{10,... | collective-permute-start | bytes 786440 | tf_op jit(solution)/shard_map/ppermute | solution.py:447
  107.4 13.3 %collective-permute-start.19 = (bf16[32,4096]{1,0:T(8,128)(2,1)S(1)}, bf16[32,4096]{1,0:T(8,128)(2,1)S(1)}, u32[]{:S(2)}, u32[]{:S(2)}) collective-permute-start(bf16[32,4096]{1,0:T(8,128)(2,1)S(1)} %get-tuple-element.96), channel_id=1, source_target_pairs={{0,2},{1,3},{2,0},{3,1},{4,6},{5,7},{6,4},{7,5},{8,10},{9,11},{10,... | collective-permute-start | bytes 786440 | tf_op jit(solution)/shard_map/ppermute | solution.py:447
  108.2 15.7 %collective-permute-start.20 = (bf16[32,4096]{1,0:T(8,128)(2,1)S(1)}, bf16[32,4096]{1,0:T(8,128)(2,1)S(1)}, u32[]{:S(2)}, u32[]{:S(2)}) collective-permute-start(bf16[32,4096]{1,0:T(8,128)(2,1)S(1)} %get-tuple-element.98), channel_id=1, source_target_pairs={{0,2},{1,3},{2,0},{3,1},{4,6},{5,7},{6,4},{7,5},{8,10},{9,11},{10,... | collective-permute-start | bytes 786440 | tf_op jit(solution)/shard_map/ppermute | solution.py:447
  118.6 16.0 %collective-permute-start.24 = (bf16[32,4096]{1,0:T(8,128)(2,1)S(1)}, bf16[32,4096]{1,0:T(8,128)(2,1)S(1)}, u32[]{:S(2)}, u32[]{:S(2)}) collective-permute-start(bf16[32,4096]{1,0:T(8,128)(2,1)S(1)} %get-tuple-element.112), channel_id=1, source_target_pairs={{0,2},{1,3},{2,0},{3,1},{4,6},{5,7},{6,4},{7,5},{8,10},{9,11},{10,... | collective-permute-start | bytes 786440 | tf_op jit(solution)/shard_map/ppermute | solution.py:447
  119.4 15.7 %collective-permute-start.25 = (bf16[32,4096]{1,0:T(8,128)(2,1)S(1)}, bf16[32,4096]{1,0:T(8,128)(2,1)S(1)}, u32[]{:S(2)}, u32[]{:S(2)}) collective-permute-start(bf16[32,4096]{1,0:T(8,128)(2,1)S(1)} %get-tuple-element.114), channel_id=1, source_target_pairs={{0,2},{1,3},{2,0},{3,1},{4,6},{5,7},{6,4},{7,5},{8,10},{9,11},{10,... | collective-permute-start | bytes 786440 | tf_op jit(solution)/shard_map/ppermute | solution.py:447
  127.9 12.2 %collective-permute-start.23 = (bf16[32,4096]{1,0:T(8,128)(2,1)S(1)}, bf16[32,4096]{1,0:T(8,128)(2,1)S(1)}, u32[]{:S(2)}, u32[]{:S(2)}) collective-permute-start(bf16[32,4096]{1,0:T(8,128)(2,1)S(1)} %get-tuple-element.110), channel_id=1, source_target_pairs={{0,2},{1,3},{2,0},{3,1},{4,6},{5,7},{6,4},{7,5},{8,10},{9,11},{10,... | collective-permute-start | bytes 786440 | tf_op jit(solution)/shard_map/ppermute | solution.py:447

commit v5 on v4

--- a/solution.py
+++ b/solution.py
@@ -75,34 +75,78 @@
     return jnp.concatenate([out[i * rows : (i + 1) * rows] for i in range(bins // WIDTH)], axis=1)
 
 
-def sketch_kernel(steps, taps, block, prev, after, even, odd, probes, sketch, band, first, final):
-    i = pl.program_id(0)
+def sketch_kernel(steps, taps, even, odd, spectra, probes, *refs):
+    sketch, band, first, final, ext, held, one, two, came, there = refs
+    size = one.shape[1]
+    bins = steps * size
+
+    def bins_copy(c):
+        start = pl.multiple_of(c * size, size)
+        return pltpu.make_async_copy(
+            spectra.at[:, pl.ds(start, size)], ext.at[:, pl.ds(start + TILE, size)], came.at[c]
+        )
+
+    def probes_copy(c):
+        start = pl.multiple_of(c * size, size)
+        return pltpu.make_async_copy(
+            probes.at[pl.ds(start, size), :], held.at[pl.ds(start, size), :], there.at[c]
+        )
+
+    for c in range(steps):
+        bins_copy(c).start()
+        if c > 0:
+            probes_copy(c - 1).start()
+    probes_copy(steps - 1).start()
     lower = lax.rem(lax.axis_index("mz"), 2) == 0
-    low = jnp.where(lower, odd[...], even[...])
-    high = jnp.where(lower, even[...], odd[...])
-
-    @pl.when(i == 0)
-    def _():
-        band[...] = band_of(taps[...])
-        sketch[...] = jnp.zeros_like(sketch)
-
-    cleaned = clean(
-        jnp.where(i == 0, low, prev[...]),
-        block[...],
-        jnp.where(i == steps - 1, high, after[...]),
-        band[...],
-    )
-    sketch[...] += jnp.dot(cleaned, probes[...], preferred_element_type=F32)
-
-    width = first.shape[1]
-
-    @pl.when(i == 0)
-    def _():
-        first[...] = cleaned[:, :width]
-
-    @pl.when(i == steps - 1)
-    def _():
-        final[...] = cleaned[:, -width:]
+    ext[:, :TILE] = jnp.where(lower, odd[...], even[...])
+    ext[:, bins + TILE :] = jnp.where(lower, even[...], odd[...])
+    band[...] = band_of(taps[...])
+    sketch[...] = jnp.zeros_like(sketch)
+
+    def filter_to(out, c):
+        start = pl.multiple_of(c * size, size)
+
+        def part(a, b):
+            return ext[:, pl.ds(pl.multiple_of(start + a, TILE), b - a)]
+
+        for a in range(0, size, WIDTH):
+            base = jnp.dot(part(a, a + 2 * WIDTH), band[...], preferred_element_type=F32)
+            block = part(a + TILE, a + TILE + WIDTH).astype(F32)
+            out[:, a : a + WIDTH] = (block - base).astype(BF16)
+
+    def add(cleaned, c):
+        rows = held[pl.ds(pl.multiple_of(c * size, size), size), :]
+        sketch[...] += jnp.dot(cleaned[...], rows, preferred_element_type=F32)
+
+    bins_copy(0).wait()
+    bins_copy(1).wait()
+    filter_to(one, 0)
+    first[...] = one[:, : first.shape[1]]
+    probes_copy(0).wait()
+
+    def pair(k, carry):
+        c = 2 * k + 1
+
+        @pl.when(c + 1 < steps)
+        def _():
+            bins_copy(c + 1).wait()
+
+        filter_to(two, c)
+        add(one, c - 1)
+        probes_copy(c).wait()
+
+        @pl.when(c + 1 < steps)
+        def _():
+            bins_copy(c + 2).wait()
+            filter_to(one, c + 1)
+            add(two, c)
+            probes_copy(c + 1).wait()
+
+        return carry
+
+    lax.fori_loop(0, steps // 2, pair, 0)
+    add(two, steps - 1)
+    final[...] = two[:, size - final.shape[1] :]
 
 
 ANY = pl.BlockSpec(memory_space=pl.ANY)
@@ -138,31 +182,30 @@
 
 def sketch_of(taps, spectra, even, odd, probes, edge):
     rows, bins = spectra.shape
-    size = math.gcd(bins, 8192)
+    size = math.gcd(bins // 2, 8192)
     steps = bins // size
     columns = probes.shape[1]
     return pl.pallas_call(
         functools.partial(sketch_kernel, steps),
-        grid=(steps,),
-        in_specs=[whole(taps.shape)]
-        + block_specs(rows, size, 0, bins // TILE - 1)
-        + [whole(even.shape), whole(odd.shape)]
-        + [pl.BlockSpec((size, columns), lambda i: (i, 0))],
-        out_specs=[
-            whole((rows, columns)),
-            whole((2 * WIDTH, WIDTH)),
-            whole((rows, edge)),
-            whole((rows, edge)),
-        ],
+        in_specs=[VMEM] * 3 + [ANY] * 2,
+        out_specs=[VMEM] * 4,
         out_shape=[
             jax.ShapeDtypeStruct((rows, columns), F32),
             jax.ShapeDtypeStruct((2 * WIDTH, WIDTH), BF16),
             jax.ShapeDtypeStruct((rows, edge), BF16),
             jax.ShapeDtypeStruct((rows, edge), BF16),
         ],
+        scratch_shapes=[
+            pltpu.VMEM((rows, bins + 2 * TILE), BF16),
+            pltpu.VMEM((bins, columns), BF16),
+            pltpu.VMEM((rows, size), BF16),
+            pltpu.VMEM((rows, size), BF16),
+            pltpu.SemaphoreType.DMA((steps,)),
+            pltpu.SemaphoreType.DMA((steps,)),
+        ],
         cost_estimate=COST,
-        compiler_params=params(48),
-    )(taps, spectra, spectra, spectra, even, odd, probes)
+        compiler_params=params(50),
+    )(taps, even, odd, spectra, probes)
 
 
 def total_kernel(count, *refs):

time: 141 us -> 140 us (level)
  no operation moved by 1% of the time
where the time goes in v5:
time: 140 us
  Pallas kernels  71.4 us (51%)
  waiting for transfers between devices  35 us (25%)
  starting transfers between devices  29.7 us (21%)
  other arithmetic  1.51 us (1%)
    pallas_call x7, Pallas kernels, project(): pl.pallas_call(functools.partial(project_kernel, count, factor, chips), g...  34.2 us
    ppermute x15, waiting for transfers between devices, across(): lax.ppermute(mine[m], 'pix', routes[m])  25.5 us
    pallas_call x1, Pallas kernels, sketch_of(): pl.pallas_call(functools.partial(sketch_kernel, steps), in_specs=[VMEM] *...  18.3 us
    ppermute x15, starting transfers between devices, across(): lax.ppermute(mine[m], 'pix', routes[m])  15.4 us
    ppermute x10, starting transfers between devices, partner(): return lax.ppermute(x, axis, [(i, i ^ shift) for i in range(count)])  11 us
    ppermute x10, waiting for transfers between devices, partner(): return lax.ppermute(x, axis, [(i, i ^ shift) for i in range(count)])  9.54 us
    pallas_call x8, Pallas kernels, finish(): pl.pallas_call(functools.partial(finish_kernel, len(blocks), len(blocks[0...  6.79 us
    pallas_call x1, Pallas kernels, basis_of(): pl.pallas_call(functools.partial(basis_kernel, chips, factor, len(sketche...  6.07 us
  transfers between devices with their start and end apart: 27, of which 12 were waited for; matrix products, arithmetic and copies ran while one was open for 2% of the time, Pallas kernels for 51%

profile of v5, /device:TPU:0, one launch (start us, length us, event | category | flops | bytes accessed | tf_op | source)
XLA Modules:
  0.0 139.8 jit_solution(17574907470947311084)
XLA Ops:
  0.6 0.5 collective-permute-start.10
  1.1 0.8 broadcast_select_fusion
  1.9 2.7 %collective-permute-start = (bf16[128,128]{1,0:T(8,128)(2,1)S(1)}, bf16[128,128]{1,0:T(8,128)(2,1)S(1)}, u32[]{:S(2)}, u32[]{:S(2)}) collective-permute-start(bf16[128,128]{1,0:T(8,128)(2,1)S(1)} %get-tuple-element.123), channel_id=1, source_target_pairs={{0,4},{8,12},{4,0},{12,8},{1,5},{9,13},{5,1},{13,9},{2,6},{10,14},... | collective-permute-start | bytes 98312 | tf_op jit(solution)/shard_map/ppermute | solution.py:455
  4.6 0.7 collective-permute-start.1
  5.2 1.3 slice.11
  6.6 1.6 %collective-permute-start.4 = (bf16[128,4352]{1,0:T(8,128)(2,1)S(1)}, bf16[128,4352]{1,0:T(8,128)(2,1)}, u32[]{:S(2)}, u32[]{:S(2)}) collective-permute-start(bf16[128,4352]{1,0:T(8,128)(2,1)S(1)} %slice.11), channel_id=1, source_target_pairs={{0,2},{1,3},{2,0},{3,1},{4,6},{5,7},{6,4},{7,5},{8,10},{9,11},{10,... | collective-permute-start | bytes 3342344 | tf_op jit(solution)/shard_map/ppermute | solution.py:31
  8.1 0.7 pad_convert_fusion
  8.9 0.0 collective-permute-done.even
  8.9 0.0 collective-permute-done.1.odd
  8.9 18.3 %shard_map.50 = (f32[128,128]{1,0:T(8,128)S(1)}, bf16[512,256]{1,0:T(8,128)(2,1)S(1)}, bf16[128,4096]{1,0:T(8,128)(2,1)S(1)}, bf16[128,4096]{1,0:T(8,128)(2,1)S(1)}) custom-call(f32[1,512]{1,0:T(1,128)S(1)} %bitcast.1, bf16[128,128]{1,0:T(8,128)(2,1)S(1)} %collective-permute-done.even, bf16[128,128]{1,0:T(8,128)(2,1)S(1)} %collective-permute-done.1.odd, ...), custom_call_target="tpu_custom_call" | custom-call | flops 1 | bytes 1 | tf_op jit(solution)/shard_map/pallas_call | solution.py:188
  27.2 0.1 collective-permute-start.8
  27.3 0.5 collective-permute-start.9
  27.8 4.4 %collective-permute-start.2 = (f32[128,128]{1,0:T(8,128)S(1)}, f32[128,128]{1,0:T(8,128)S(1)}, u32[]{:S(2)}, u32[]{:S(2)}) collective-permute-start(f32[128,128]{1,0:T(8,128)S(1)} %get-tuple-element.62.refs_0_), channel_id=1, source_target_pairs={{0,4},{4,0},{8,12},{12,8},{1,5},{5,1},{9,13},{13,9},{2,6},{6,2},{1... | collective-permute-start | bytes 196616 | tf_op jit(solution)/shard_map/ppermute | solution.py:31
  32.2 2.3 %collective-permute-done.2.refs_1_ = f32[128,128]{1,0:T(8,128)S(1)} collective-permute-done((f32[128,128]{1,0:T(8,128)S(1)}, f32[128,128]{1,0:T(8,128)S(1)}, u32[]{:S(2)}, u32[]{:S(2)}) %collective-permute-start.2) | collective-permute-done | bytes 65568 | tf_op jit(solution)/shard_map/ppermute | solution.py:31
  34.5 1.7 %collective-permute-start.3 = (f32[128,128]{1,0:T(8,128)S(1)}, f32[128,128]{1,0:T(8,128)S(1)}, u32[]{:S(2)}, u32[]{:S(2)}) collective-permute-start(f32[128,128]{1,0:T(8,128)S(1)} %shard_map.51.refs_0_), channel_id=1, source_target_pairs={{0,8},{4,12},{8,0},{12,4},{1,9},{5,13},{9,1},{13,5},{2,10},{6,14},... | collective-permute-start | bytes 196616 | tf_op jit(solution)/shard_map/ppermute | solution.py:31
  36.2 4.0 %collective-permute-done.3.refs_1_ = f32[128,128]{1,0:T(8,128)S(1)} collective-permute-done((f32[128,128]{1,0:T(8,128)S(1)}, f32[128,128]{1,0:T(8,128)S(1)}, u32[]{:S(2)}, u32[]{:S(2)}) %collective-permute-start.3) | collective-permute-done | bytes 65568 | tf_op jit(solution)/shard_map/ppermute | solution.py:31
  40.2 0.0 collective-permute-done.4.refs_2_
  40.2 0.1 collective-permute-start.5
  40.3 0.6 collective-permute-start.6
  40.9 1.3 collective-permute-start.7
  42.2 0.3 collective-permute-start.26
  42.5 2.7 %collective-permute-done.6.refs_2_ = f32[128,128]{1,0:T(8,128)S(1)} collective-permute-done((f32[128,128]{1,0:T(8,128)S(1)}, f32[128,128]{1,0:T(8,128)S(1)}, u32[]{:S(2)}, u32[]{:S(2)}) %collective-permute-start.6) | collective-permute-done | bytes 65568 | tf_op jit(solution)/shard_map/ppermute | solution.py:31
  45.2 0.5 collective-permute-done.7.refs_3_
  45.7 6.1 %shard_map.53 = (bf16[128,128]{1,0:T(8,128)(2,1)}, bf16[64,512]{1,0:T(8,128)(2,1)S(1)}, bf16[32,4096]{1,0:T(8,128)(2,1)S(1)}, bf16[32,4096]{1,0:T(8,128)(2,1)S(1...) custom-call(f32[128,128]{1,0:T(8,128)S(1)} %shard_map.52.refs_0_, ...), custom_call_target="tpu_custom_call" | custom-call | flops 1 | bytes 1 | tf_op jit(solution)/shard_map/pallas_call | solution.py:311
  51.8 0.7 collective-permute-start.13
  52.6 1.3 collective-permute-start.14
  53.9 0.0 collective-permute-done.10.refs_3_.refs_4_.refs_5_.near.refs_0_.refs_1_
  53.9 5.2 %shard_map.54 = (bf16[32,4096]{1,0:T(8,128)(2,1)S(1)}, bf16[32,4096]{1,0:T(8,128)(2,1)S(1)}, bf16[32,4096]{1,0:T(8,128)(2,1)S(1)}, bf16[32,4096]{1,0:T(8,128)(2,1)S(1)}, f32[8,128]{1,0:T(8,128)S(1)}) custom-call(bf16[64,512]{1,0:T(8,128)(2,1)S(1)} %get-tuple-element.66.turned, bf16[512,256]{1,0:T(8,128)(2,1)S(1)} %get-tuple-element.67.band, ...), custom_call_target="tpu_custom_call" | custom-call | flops 1 | bytes 1 | tf_op jit(solution)/shard_map/pallas_call | solution.py:360
  59.1 0.7 collective-permute-start.11
  59.9 1.3 collective-permute-start.12
  61.2 5.4 %collective-permute-done.14.refs_3_ = bf16[32,4096]{1,0:T(8,128)(2,1)S(1)} collective-permute-done((bf16[32,4096]{1,0:T(8,128)(2,1)S(1)}, bf16[32,4096]{1,0:T(8,128)(2,1)S(1)}, u32[]{:S(2)}, u32[]{:S(2)}) %collective-permute-start.14) | collective-permute-done | bytes 262176 | tf_op jit(solution)/shard_map/ppermute | solution.py:490
  66.6 0.9 shard_map.55
  67.5 5.2 %shard_map.56 = (bf16[32,4096]{1,0:T(8,128)(2,1)S(1)}, bf16[32,4096]{1,0:T(8,128)(2,1)S(1)}, bf16[32,4096]{1,0:T(8,128)(2,1)S(1)}, bf16[32,4096]{1,0:T(8,128)(2,1)S(1)}, f32[8,128]{1,0:T(8,128)S(1)}) custom-call(bf16[64,512]{1,0:T(8,128)(2,1)S(1)} %get-tuple-element.66.turned, bf16[512,256]{1,0:T(8,128)(2,1)S(1)} %get-tuple-element.67.band, ...), custom_call_target="tpu_custom_call" | custom-call | flops 1 | bytes 1 | tf_op jit(solution)/shard_map/pallas_call | solution.py:360
  72.7 0.8 collective-permute-start.17
  73.4 1.3 collective-permute-start.18
  74.8 3.1 %collective-permute-done.12.refs_3_ = bf16[32,4096]{1,0:T(8,128)(2,1)S(1)} collective-permute-done((bf16[32,4096]{1,0:T(8,128)(2,1)S(1)}, bf16[32,4096]{1,0:T(8,128)(2,1)S(1)}, u32[]{:S(2)}, u32[]{:S(2)}) %collective-permute-start.12) | collective-permute-done | bytes 262176 | tf_op jit(solution)/shard_map/ppermute | solution.py:490
  77.9 0.9 shard_map.57
  78.7 5.2 %shard_map.58 = (bf16[32,4096]{1,0:T(8,128)(2,1)S(1)}, bf16[32,4096]{1,0:T(8,128)(2,1)S(1)}, bf16[32,4096]{1,0:T(8,128)(2,1)S(1)}, bf16[32,4096]{1,0:T(8,128)(2,1)S(1)}, f32[8,128]{1,0:T(8,128)S(1)}) custom-call(bf16[64,512]{1,0:T(8,128)(2,1)S(1)} %get-tuple-element.66.turned, bf16[512,256]{1,0:T(8,128)(2,1)S(1)} %get-tuple-element.67.band, ...), custom_call_target="tpu_custom_call" | custom-call | flops 1 | bytes 1 | tf_op jit(solution)/shard_map/pallas_call | solution.py:360
  83.9 0.8 collective-permute-start.15
  84.7 1.3 collective-permute-start.16
  86.0 3.1 %collective-permute-done.18.refs_3_ = bf16[32,4096]{1,0:T(8,128)(2,1)S(1)} collective-permute-done((bf16[32,4096]{1,0:T(8,128)(2,1)S(1)}, bf16[32,4096]{1,0:T(8,128)(2,1)S(1)}, u32[]{:S(2)}, u32[]{:S(2)}) %collective-permute-start.18) | collective-permute-done | bytes 262176 | tf_op jit(solution)/shard_map/ppermute | solution.py:490
  89.1 0.9 shard_map.59
  90.0 5.2 %shard_map.60 = (bf16[32,4096]{1,0:T(8,128)(2,1)S(1)}, bf16[32,4096]{1,0:T(8,128)(2,1)S(1)}, bf16[32,4096]{1,0:T(8,128)(2,1)S(1)}, bf16[32,4096]{1,0:T(8,128)(2,1)S(1)}, f32[8,128]{1,0:T(8,128)S(1)}) custom-call(bf16[64,512]{1,0:T(8,128)(2,1)S(1)} %get-tuple-element.66.turned, bf16[512,256]{1,0:T(8,128)(2,1)S(1)} %get-tuple-element.67.band, ...), custom_call_target="tpu_custom_call" | custom-call | flops 1 | bytes 1 | tf_op jit(solution)/shard_map/pallas_call | solution.py:360
  95.2 0.8 collective-permute-start.21
  95.9 1.3 collective-permute-start.22
  97.3 3.1 %collective-permute-done.16.refs_3_ = bf16[32,4096]{1,0:T(8,128)(2,1)S(1)} collective-permute-done((bf16[32,4096]{1,0:T(8,128)(2,1)S(1)}, bf16[32,4096]{1,0:T(8,128)(2,1)S(1)}, u32[]{:S(2)}, u32[]{:S(2)}) %collective-permute-start.16) | collective-permute-done | bytes 262176 | tf_op jit(solution)/shard_map/ppermute | solution.py:490
  100.3 0.9 shard_map.61
  101.2 5.2 %shard_map.62 = (bf16[32,4096]{1,0:T(8,128)(2,1)S(1)}, bf16[32,4096]{1,0:T(8,128)(2,1)S(1)}, bf16[32,4096]{1,0:T(8,128)(2,1)S(1)}, bf16[32,4096]{1,0:T(8,128)(2,1)S(1)}, f32[8,128]{1,0:T(8,128)S(1)}) custom-call(bf16[64,512]{1,0:T(8,128)(2,1)S(1)} %get-tuple-element.66.turned, bf16[512,256]{1,0:T(8,128)(2,1)S(1)} %get-tuple-element.67.band, ...), custom_call_target="tpu_custom_call" | custom-call | flops 1 | bytes 1 | tf_op jit(solution)/shard_map/pallas_call | solution.py:360
  106.4 0.8 collective-permute-start.19
  107.2 1.3 collective-permute-start.20
  108.5 3.1 %collective-permute-done.22.refs_3_ = bf16[32,4096]{1,0:T(8,128)(2,1)S(1)} collective-permute-done((bf16[32,4096]{1,0:T(8,128)(2,1)S(1)}, bf16[32,4096]{1,0:T(8,128)(2,1)S(1)}, u32[]{:S(2)}, u32[]{:S(2)}) %collective-permute-start.22) | collective-permute-done | bytes 262176 | tf_op jit(solution)/shard_map/ppermute | solution.py:490
  111.6 0.9 shard_map.63
  112.4 5.2 %shard_map.64 = (bf16[32,4096]{1,0:T(8,128)(2,1)S(1)}, bf16[32,4096]{1,0:T(8,128)(2,1)S(1)}, bf16[32,4096]{1,0:T(8,128)(2,1)S(1)}, bf16[32,4096]{1,0:T(8,128)(2,1)S(1)}, f32[8,128]{1,0:T(8,128)S(1)}) custom-call(bf16[64,512]{1,0:T(8,128)(2,1)S(1)} %get-tuple-element.66.turned, bf16[512,256]{1,0:T(8,128)(2,1)S(1)} %get-tuple-element.67.band, ...), custom_call_target="tpu_custom_call" | custom-call | flops 1 | bytes 1 | tf_op jit(solution)/shard_map/pallas_call | solution.py:360
  117.6 0.8 collective-permute-start.24
  118.4 1.3 collective-permute-start.25
  119.7 3.1 %collective-permute-done.20.refs_3_ = bf16[32,4096]{1,0:T(8,128)(2,1)S(1)} collective-permute-done((bf16[32,4096]{1,0:T(8,128)(2,1)S(1)}, bf16[32,4096]{1,0:T(8,128)(2,1)S(1)}, u32[]{:S(2)}, u32[]{:S(2)}) %collective-permute-start.20) | collective-permute-done | bytes 262176 | tf_op jit(solution)/shard_map/ppermute | solution.py:490
  122.8 0.9 shard_map.65
  123.7 3.2 %shard_map.66 = (bf16[32,4096]{1,0:T(8,128)(2,1)S(1)}, bf16[32,4096]{1,0:T(8,128)(2,1)S(1)}, f32[8,128]{1,0:T(8,128)S(1)}) custom-call(bf16[64,512]{1,0:T(8,128)(2,1)S(1)} %get-tuple-element.66.turned, bf16[512,256]{1,0:T(8,128)(2,1)S(1)} %get-tuple-element.67.band, bf16[128,65536]{1,0:T(8,128)(2,1)} %own_high.1, bf16[128,65536]{1,0:T(8,128)(2,1)} %own_high.1, ...), custom_call_target="tpu_custom_call" | custom-call | flops 1 | bytes 1 | tf_op jit(solution)/shard_map/pallas_call | solution.py:360
  126.8 0.8 collective-permute-start.23
  127.6 6.0 %shard_map.67 = (bf16[32,65536]{1,0:T(8,128)(2,1)}, f32[8,128]{1,0:T(8,128)S(1)}) custom-call(bf16[64,512]{1,0:T(8,128)(2,1)S(1)} %get-tuple-element.66.turned, bf16[512,256]{1,0:T(8,128)(2,1)S(1)} %get-tuple-element.67.band, bf16[128,65536]{1,0:T(8,128)(2,1)} %own_high.1, bf16[128,65536]{1,0:T(8,128)(2,1)} %own_high.1, ...), custom_call_target="tpu_custom_call", output_to_operand_aliasing={{0}: (10, {})} | custom-call | flops 1 | bytes 1 | tf_op jit(solution)/shard_map/pallas_call | solution.py:392
  133.6 0.4 collective-permute-done.25.refs_3_
  134.1 0.9 shard_map.68
  134.9 4.1 %collective-permute-done.23.refs_1_ = bf16[32,4096]{1,0:T(8,128)(2,1)S(1)} collective-permute-done((bf16[32,4096]{1,0:T(8,128)(2,1)S(1)}, bf16[32,4096]{1,0:T(8,128)(2,1)S(1)}, u32[]{:S(2)}, u32[]{:S(2)}) %collective-permute-start.23) | collective-permute-done | bytes 262176 | tf_op jit(solution)/shard_map/ppermute | solution.py:490
  139.0 0.8 shard_map.69
  (13 shorter events, 0.0 us)
Async XLA Ops:
  0.6 53.3 %collective-permute-start.10 = (bf16[128,65536]{1,0:T(8,128)(2,1)}, bf16[128,65536]{1,0:T(8,128)(2,1)}, u32[]{:S(2)}, u32[]{:S(2)}) collective-permute-start(bf16[128,65536]{1,0:T(8,128)(2,1)} %own_high.1), channel_id=1, source_target_pairs={{0,1},{1,0},{2,3},{3,2},{4,5},{5,4},{6,7},{7,6},{8,9},{9,8},{10,11... | collective-permute-start | bytes 50331656 | tf_op jit(solution)/shard_map/ppermute | solution.py:31
  1.9 6.9 %collective-permute-start = (bf16[128,128]{1,0:T(8,128)(2,1)S(1)}, bf16[128,128]{1,0:T(8,128)(2,1)S(1)}, u32[]{:S(2)}, u32[]{:S(2)}) collective-permute-start(bf16[128,128]{1,0:T(8,128)(2,1)S(1)} %get-tuple-element.123), channel_id=1, source_target_pairs={{0,4},{8,12},{4,0},{12,8},{1,5},{9,13},{5,1},{13,9},{2,6},{10,14},... | collective-permute-start | bytes 98312 | tf_op jit(solution)/shard_map/ppermute | solution.py:455
  4.6 4.3 %collective-permute-start.1 = (bf16[128,128]{1,0:T(8,128)(2,1)S(1)}, bf16[128,128]{1,0:T(8,128)(2,1)S(1)}, u32[]{:S(2)}, u32[]{:S(2)}) collective-permute-start(bf16[128,128]{1,0:T(8,128)(2,1)S(1)} %get-tuple-element.122), channel_id=1, source_target_pairs={{4,8},{8,4},{5,9},{9,5},{6,10},{10,6},{7,11},{11,7},{20,24},{24,20... | collective-permute-start | bytes 98312 | tf_op jit(solution)/shard_map/ppermute | solution.py:455
  6.6 33.6 %collective-permute-start.4 = (bf16[128,4352]{1,0:T(8,128)(2,1)S(1)}, bf16[128,4352]{1,0:T(8,128)(2,1)}, u32[]{:S(2)}, u32[]{:S(2)}) collective-permute-start(bf16[128,4352]{1,0:T(8,128)(2,1)S(1)} %slice.11), channel_id=1, source_target_pairs={{0,2},{1,3},{2,0},{3,1},{4,6},{5,7},{6,4},{7,5},{8,10},{9,11},{10,... | collective-permute-start | bytes 3342344 | tf_op jit(solution)/shard_map/ppermute | solution.py:31
  27.2 13.7 %collective-permute-start.8 = (bf16[128,4096]{1,0:T(8,128)(2,1)S(1)}, bf16[128,4096]{1,0:T(8,128)(2,1)S(1)}, u32[]{:S(2)}, u32[]{:S(2)}) collective-permute-start(bf16[128,4096]{1,0:T(8,128)(2,1)S(1)} %get-tuple-element.63.refs_4_), channel_id=1, source_target_pairs={{0,1},{1,0},{2,3},{3,2},{4,5},{5,4},{6,7},{7,6},{8,9},{9,8},{10,11... | collective-permute-start | bytes 3145736 | tf_op jit(solution)/shard_map/ppermute | solution.py:31
  27.3 14.9 %collective-permute-start.9 = (bf16[128,4096]{1,0:T(8,128)(2,1)S(1)}, bf16[128,4096]{1,0:T(8,128)(2,1)S(1)}, u32[]{:S(2)}, u32[]{:S(2)}) collective-permute-start(bf16[128,4096]{1,0:T(8,128)(2,1)S(1)} %get-tuple-element.64.refs_6_), channel_id=1, source_target_pairs={{0,1},{1,0},{2,3},{3,2},{4,5},{5,4},{6,7},{7,6},{8,9},{9,8},{10,11... | collective-permute-start | bytes 3145736 | tf_op jit(solution)/shard_map/ppermute | solution.py:31
  27.8 6.7 %collective-permute-start.2 = (f32[128,128]{1,0:T(8,128)S(1)}, f32[128,128]{1,0:T(8,128)S(1)}, u32[]{:S(2)}, u32[]{:S(2)}) collective-permute-start(f32[128,128]{1,0:T(8,128)S(1)} %get-tuple-element.62.refs_0_), channel_id=1, source_target_pairs={{0,4},{4,0},{8,12},{12,8},{1,5},{5,1},{9,13},{13,9},{2,6},{6,2},{1... | collective-permute-start | bytes 196616 | tf_op jit(solution)/shard_map/ppermute | solution.py:31
  34.5 5.7 %collective-permute-start.3 = (f32[128,128]{1,0:T(8,128)S(1)}, f32[128,128]{1,0:T(8,128)S(1)}, u32[]{:S(2)}, u32[]{:S(2)}) collective-permute-start(f32[128,128]{1,0:T(8,128)S(1)} %shard_map.51.refs_0_), channel_id=1, source_target_pairs={{0,8},{4,12},{8,0},{12,4},{1,9},{5,13},{9,1},{13,5},{2,10},{6,14},... | collective-permute-start | bytes 196616 | tf_op jit(solution)/shard_map/ppermute | solution.py:31
  40.2 2.3 %collective-permute-start.5 = (f32[128,128]{1,0:T(8,128)S(1)}, f32[128,128]{1,0:T(8,128)S(1)}, u32[]{:S(2)}, u32[]{:S(2)}) collective-permute-start(f32[128,128]{1,0:T(8,128)S(1)} %shard_map.52.refs_0_), channel_id=1, source_target_pairs={{0,1},{1,0},{2,3},{3,2},{4,5},{5,4},{6,7},{7,6},{8,9},{9,8},{10,11... | collective-permute-start | bytes 196616 | tf_op jit(solution)/shard_map/ppermute | solution.py:31
  40.3 5.0 %collective-permute-start.6 = (f32[128,128]{1,0:T(8,128)S(1)}, f32[128,128]{1,0:T(8,128)S(1)}, u32[]{:S(2)}, u32[]{:S(2)}) collective-permute-start(f32[128,128]{1,0:T(8,128)S(1)} %shard_map.52.refs_0_), channel_id=1, source_target_pairs={{0,2},{1,3},{2,0},{3,1},{4,6},{5,7},{6,4},{7,5},{8,10},{9,11},{10,... | collective-permute-start | bytes 196616 | tf_op jit(solution)/shard_map/ppermute | solution.py:31
  40.9 4.9 %collective-permute-start.7 = (f32[128,128]{1,0:T(8,128)S(1)}, f32[128,128]{1,0:T(8,128)S(1)}, u32[]{:S(2)}, u32[]{:S(2)}) collective-permute-start(f32[128,128]{1,0:T(8,128)S(1)} %shard_map.52.refs_0_), channel_id=1, source_target_pairs={{0,3},{1,2},{2,1},{3,0},{4,7},{5,6},{6,5},{7,4},{8,11},{9,10},{10,... | collective-permute-start | bytes 196616 | tf_op jit(solution)/shard_map/ppermute | solution.py:31
  42.2 85.4 %collective-permute-start.26 = (bf16[128,4352]{1,0:T(8,128)(2,1)}, bf16[128,4352]{1,0:T(8,128)(2,1)}, u32[]{:S(2)}, u32[]{:S(2)}) collective-permute-start(bf16[128,4352]{1,0:T(8,128)(2,1)} %collective-permute-done.4.refs_2_), channel_id=1, source_target_pairs={{0,1},{1,0},{2,3},{3,2},{4,5},{5,4},{6,7},{7,6},{8,9},{9,8},{10,11... | collective-permute-start | bytes 3342344 | tf_op jit(solution)/shard_map/ppermute | solution.py:31
  51.8 9.4 %collective-permute-start.13 = (bf16[32,4096]{1,0:T(8,128)(2,1)S(1)}, bf16[32,4096]{1,0:T(8,128)(2,1)S(1)}, u32[]{:S(2)}, u32[]{:S(2)}) collective-permute-start(bf16[32,4096]{1,0:T(8,128)(2,1)S(1)} %get-tuple-element.73), channel_id=1, source_target_pairs={{0,2},{1,3},{2,0},{3,1},{4,6},{5,7},{6,4},{7,5},{8,10},{9,11},{10,... | collective-permute-start | bytes 786440 | tf_op jit(solution)/shard_map/ppermute | solution.py:490
  52.6 14.1 %collective-permute-start.14 = (bf16[32,4096]{1,0:T(8,128)(2,1)S(1)}, bf16[32,4096]{1,0:T(8,128)(2,1)S(1)}, u32[]{:S(2)}, u32[]{:S(2)}) collective-permute-start(bf16[32,4096]{1,0:T(8,128)(2,1)S(1)} %get-tuple-element.75), channel_id=1, source_target_pairs={{0,2},{1,3},{2,0},{3,1},{4,6},{5,7},{6,4},{7,5},{8,10},{9,11},{10,... | collective-permute-start | bytes 786440 | tf_op jit(solution)/shard_map/ppermute | solution.py:490
  59.1 15.7 %collective-permute-start.11 = (bf16[32,4096]{1,0:T(8,128)(2,1)S(1)}, bf16[32,4096]{1,0:T(8,128)(2,1)S(1)}, u32[]{:S(2)}, u32[]{:S(2)}) collective-permute-start(bf16[32,4096]{1,0:T(8,128)(2,1)S(1)} %get-tuple-element.69), channel_id=1, source_target_pairs={{0,2},{1,3},{2,0},{3,1},{4,6},{5,7},{6,4},{7,5},{8,10},{9,11},{10,... | collective-permute-start | bytes 786440 | tf_op jit(solution)/shard_map/ppermute | solution.py:490
  59.9 18.0 %collective-permute-start.12 = (bf16[32,4096]{1,0:T(8,128)(2,1)S(1)}, bf16[32,4096]{1,0:T(8,128)(2,1)S(1)}, u32[]{:S(2)}, u32[]{:S(2)}) collective-permute-start(bf16[32,4096]{1,0:T(8,128)(2,1)S(1)} %get-tuple-element.71), channel_id=1, source_target_pairs={{0,2},{1,3},{2,0},{3,1},{4,6},{5,7},{6,4},{7,5},{8,10},{9,11},{10,... | collective-permute-start | bytes 786440 | tf_op jit(solution)/shard_map/ppermute | solution.py:490
  72.7 13.3 %collective-permute-start.17 = (bf16[32,4096]{1,0:T(8,128)(2,1)S(1)}, bf16[32,4096]{1,0:T(8,128)(2,1)S(1)}, u32[]{:S(2)}, u32[]{:S(2)}) collective-permute-start(bf16[32,4096]{1,0:T(8,128)(2,1)S(1)} %get-tuple-element.86), channel_id=1, source_target_pairs={{0,2},{1,3},{2,0},{3,1},{4,6},{5,7},{6,4},{7,5},{8,10},{9,11},{10,... | collective-permute-start | bytes 786440 | tf_op jit(solution)/shard_map/ppermute | solution.py:490
  73.4 15.7 %collective-permute-start.18 = (bf16[32,4096]{1,0:T(8,128)(2,1)S(1)}, bf16[32,4096]{1,0:T(8,128)(2,1)S(1)}, u32[]{:S(2)}, u32[]{:S(2)}) collective-permute-start(bf16[32,4096]{1,0:T(8,128)(2,1)S(1)} %get-tuple-element.88), channel_id=1, source_target_pairs={{0,2},{1,3},{2,0},{3,1},{4,6},{5,7},{6,4},{7,5},{8,10},{9,11},{10,... | collective-permute-start | bytes 786440 | tf_op jit(solution)/shard_map/ppermute | solution.py:490
  83.9 13.3 %collective-permute-start.15 = (bf16[32,4096]{1,0:T(8,128)(2,1)S(1)}, bf16[32,4096]{1,0:T(8,128)(2,1)S(1)}, u32[]{:S(2)}, u32[]{:S(2)}) collective-permute-start(bf16[32,4096]{1,0:T(8,128)(2,1)S(1)} %get-tuple-element.82), channel_id=1, source_target_pairs={{0,2},{1,3},{2,0},{3,1},{4,6},{5,7},{6,4},{7,5},{8,10},{9,11},{10,... | collective-permute-start | bytes 786440 | tf_op jit(solution)/shard_map/ppermute | solution.py:490
  84.7 15.7 %collective-permute-start.16 = (bf16[32,4096]{1,0:T(8,128)(2,1)S(1)}, bf16[32,4096]{1,0:T(8,128)(2,1)S(1)}, u32[]{:S(2)}, u32[]{:S(2)}) collective-permute-start(bf16[32,4096]{1,0:T(8,128)(2,1)S(1)} %get-tuple-element.84), channel_id=1, source_target_pairs={{0,2},{1,3},{2,0},{3,1},{4,6},{5,7},{6,4},{7,5},{8,10},{9,11},{10,... | collective-permute-start | bytes 786440 | tf_op jit(solution)/shard_map/ppermute | solution.py:490
  95.2 13.3 %collective-permute-start.21 = (bf16[32,4096]{1,0:T(8,128)(2,1)S(1)}, bf16[32,4096]{1,0:T(8,128)(2,1)S(1)}, u32[]{:S(2)}, u32[]{:S(2)}) collective-permute-start(bf16[32,4096]{1,0:T(8,128)(2,1)S(1)} %get-tuple-element.100), channel_id=1, source_target_pairs={{0,2},{1,3},{2,0},{3,1},{4,6},{5,7},{6,4},{7,5},{8,10},{9,11},{10,... | collective-permute-start | bytes 786440 | tf_op jit(solution)/shard_map/ppermute | solution.py:490
  95.9 15.7 %collective-permute-start.22 = (bf16[32,4096]{1,0:T(8,128)(2,1)S(1)}, bf16[32,4096]{1,0:T(8,128)(2,1)S(1)}, u32[]{:S(2)}, u32[]{:S(2)}) collective-permute-start(bf16[32,4096]{1,0:T(8,128)(2,1)S(1)} %get-tuple-element.102), channel_id=1, source_target_pairs={{0,2},{1,3},{2,0},{3,1},{4,6},{5,7},{6,4},{7,5},{8,10},{9,11},{10,... | collective-permute-start | bytes 786440 | tf_op jit(solution)/shard_map/ppermute | solution.py:490
  106.4 13.3 %collective-permute-start.19 = (bf16[32,4096]{1,0:T(8,128)(2,1)S(1)}, bf16[32,4096]{1,0:T(8,128)(2,1)S(1)}, u32[]{:S(2)}, u32[]{:S(2)}) collective-permute-start(bf16[32,4096]{1,0:T(8,128)(2,1)S(1)} %get-tuple-element.96), channel_id=1, source_target_pairs={{0,2},{1,3},{2,0},{3,1},{4,6},{5,7},{6,4},{7,5},{8,10},{9,11},{10,... | collective-permute-start | bytes 786440 | tf_op jit(solution)/shard_map/ppermute | solution.py:490
  107.2 15.7 %collective-permute-start.20 = (bf16[32,4096]{1,0:T(8,128)(2,1)S(1)}, bf16[32,4096]{1,0:T(8,128)(2,1)S(1)}, u32[]{:S(2)}, u32[]{:S(2)}) collective-permute-start(bf16[32,4096]{1,0:T(8,128)(2,1)S(1)} %get-tuple-element.98), channel_id=1, source_target_pairs={{0,2},{1,3},{2,0},{3,1},{4,6},{5,7},{6,4},{7,5},{8,10},{9,11},{10,... | collective-permute-start | bytes 786440 | tf_op jit(solution)/shard_map/ppermute | solution.py:490
  117.6 16.0 %collective-permute-start.24 = (bf16[32,4096]{1,0:T(8,128)(2,1)S(1)}, bf16[32,4096]{1,0:T(8,128)(2,1)S(1)}, u32[]{:S(2)}, u32[]{:S(2)}) collective-permute-start(bf16[32,4096]{1,0:T(8,128)(2,1)S(1)} %get-tuple-element.112), channel_id=1, source_target_pairs={{0,2},{1,3},{2,0},{3,1},{4,6},{5,7},{6,4},{7,5},{8,10},{9,11},{10,... | collective-permute-start | bytes 786440 | tf_op jit(solution)/shard_map/ppermute | solution.py:490
  118.4 15.7 %collective-permute-start.25 = (bf16[32,4096]{1,0:T(8,128)(2,1)S(1)}, bf16[32,4096]{1,0:T(8,128)(2,1)S(1)}, u32[]{:S(2)}, u32[]{:S(2)}) collective-permute-start(bf16[32,4096]{1,0:T(8,128)(2,1)S(1)} %get-tuple-element.114), channel_id=1, source_target_pairs={{0,2},{1,3},{2,0},{3,1},{4,6},{5,7},{6,4},{7,5},{8,10},{9,11},{10,... | collective-permute-start | bytes 786440 | tf_op jit(solution)/shard_map/ppermute | solution.py:490
  126.8 12.2 %collective-permute-start.23 = (bf16[32,4096]{1,0:T(8,128)(2,1)S(1)}, bf16[32,4096]{1,0:T(8,128)(2,1)S(1)}, u32[]{:S(2)}, u32[]{:S(2)}) collective-permute-start(bf16[32,4096]{1,0:T(8,128)(2,1)S(1)} %get-tuple-element.110), channel_id=1, source_target_pairs={{0,2},{1,3},{2,0},{3,1},{4,6},{5,7},{6,4},{7,5},{8,10},{9,11},{10,... | collective-permute-start | bytes 786440 | tf_op jit(solution)/shard_map/ppermute | solution.py:490

commit v6 on v5

--- a/solution.py
+++ b/solution.py
@@ -80,10 +80,12 @@
     size = one.shape[1]
     bins = steps * size
 
-    def bins_copy(c):
-        start = pl.multiple_of(c * size, size)
+    def bins_copy(c, last=False):
+        skip = TILE if not isinstance(c, int) or c > 0 else 0
+        width = size + TILE - skip - (TILE if last else 0)
+        start = pl.multiple_of(c * size + skip, TILE)
         return pltpu.make_async_copy(
-            spectra.at[:, pl.ds(start, size)], ext.at[:, pl.ds(start + TILE, size)], came.at[c]
+            spectra.at[:, pl.ds(start, width)], ext.at[:, pl.ds(start + TILE, width)], came.at[c]
         )
 
     def probes_copy(c):
@@ -93,7 +95,7 @@
         )
 
     for c in range(steps):
-        bins_copy(c).start()
+        bins_copy(c, c == steps - 1).start()
         if c > 0:
             probes_copy(c - 1).start()
     probes_copy(steps - 1).start()
@@ -119,7 +121,6 @@
         sketch[...] += jnp.dot(cleaned[...], rows, preferred_element_type=F32)
 
     bins_copy(0).wait()
-    bins_copy(1).wait()
     filter_to(one, 0)
     first[...] = one[:, : first.shape[1]]
     probes_copy(0).wait()
@@ -129,7 +130,11 @@
 
         @pl.when(c + 1 < steps)
         def _():
-            bins_copy(c + 1).wait()
+            bins_copy(c).wait()
+
+        @pl.when(c + 1 == steps)
+        def _():
+            bins_copy(c, True).wait()
 
         filter_to(two, c)
         add(one, c - 1)
@@ -137,7 +142,7 @@
 
         @pl.when(c + 1 < steps)
         def _():
-            bins_copy(c + 2).wait()
+            bins_copy(c + 1).wait()
             filter_to(one, c + 1)
             add(two, c)
             probes_copy(c + 1).wait()

time: 140 us -> 139 us (level)
  transfers between devices with their start and end apart: 27 -> 27, of which waited for: 12 -> 12; matrix products, arithmetic and copies ran while one was open for 2% -> 2% of each run, Pallas kernels for 51% -> 50%
where the time goes in v6:
time: 139 us
  Pallas kernels  70.8 us (51%)
  waiting for transfers between devices  35 us (25%)
  starting transfers between devices  29.7 us (21%)
  other arithmetic  1.51 us (1%)
    pallas_call x7, Pallas kernels, project(): pl.pallas_call(functools.partial(project_kernel, count, factor, chips), g...  34.2 us
    ppermute x15, waiting for transfers between devices, across(): lax.ppermute(mine[m], 'pix', routes[m])  25.5 us
    pallas_call x1, Pallas kernels, sketch_of(): pl.pallas_call(functools.partial(sketch_kernel, steps), in_specs=[VMEM] *...  17.7 us
    ppermute x15, starting transfers between devices, across(): lax.ppermute(mine[m], 'pix', routes[m])  15.4 us
    ppermute x10, starting transfers between devices, partner(): return lax.ppermute(x, axis, [(i, i ^ shift) for i in range(count)])  11 us
    ppermute x10, waiting for transfers between devices, partner(): return lax.ppermute(x, axis, [(i, i ^ shift) for i in range(count)])  9.54 us
    pallas_call x8, Pallas kernels, finish(): pl.pallas_call(functools.partial(finish_kernel, len(blocks), len(blocks[0...  6.79 us
    pallas_call x1, Pallas kernels, basis_of(): pl.pallas_call(functools.partial(basis_kernel, chips, factor, len(sketche...  6.08 us
  transfers between devices with their start and end apart: 27, of which 12 were waited for; matrix products, arithmetic and copies ran while one was open for 2% of the time, Pallas kernels for 50%

profile of v6, /device:TPU:0, one launch (start us, length us, event | category | flops | bytes accessed | tf_op | source)
XLA Modules:
  0.0 139.2 jit_solution(7260443394552551886)
XLA Ops:
  0.6 0.5 collective-permute-start.10
  1.1 0.8 broadcast_select_fusion
  1.9 2.7 %collective-permute-start = (bf16[128,128]{1,0:T(8,128)(2,1)S(1)}, bf16[128,128]{1,0:T(8,128)(2,1)S(1)}, u32[]{:S(2)}, u32[]{:S(2)}) collective-permute-start(bf16[128,128]{1,0:T(8,128)(2,1)S(1)} %get-tuple-element.123), channel_id=1, source_target_pairs={{0,4},{8,12},{4,0},{12,8},{1,5},{9,13},{5,1},{13,9},{2,6},{10,14},... | collective-permute-start | bytes 98312 | tf_op jit(solution)/shard_map/ppermute | solution.py:460
  4.6 0.7 collective-permute-start.1
  5.2 1.3 slice.11
  6.6 1.6 %collective-permute-start.4 = (bf16[128,4352]{1,0:T(8,128)(2,1)S(1)}, bf16[128,4352]{1,0:T(8,128)(2,1)}, u32[]{:S(2)}, u32[]{:S(2)}) collective-permute-start(bf16[128,4352]{1,0:T(8,128)(2,1)S(1)} %slice.11), channel_id=1, source_target_pairs={{0,2},{1,3},{2,0},{3,1},{4,6},{5,7},{6,4},{7,5},{8,10},{9,11},{10,... | collective-permute-start | bytes 3342344 | tf_op jit(solution)/shard_map/ppermute | solution.py:31
  8.1 0.7 pad_convert_fusion
  8.9 0.0 collective-permute-done.1.odd
  8.9 17.7 %shard_map.50 = (f32[128,128]{1,0:T(8,128)S(1)}, bf16[512,256]{1,0:T(8,128)(2,1)S(1)}, bf16[128,4096]{1,0:T(8,128)(2,1)S(1)}, bf16[128,4096]{1,0:T(8,128)(2,1)S(1)}) custom-call(f32[1,512]{1,0:T(1,128)S(1)} %bitcast.1, bf16[128,128]{1,0:T(8,128)(2,1)S(1)} %collective-permute-done.even, bf16[128,128]{1,0:T(8,128)(2,1)S(1)} %collective-permute-done.1.odd, ...), custom_call_target="tpu_custom_call" | custom-call | flops 1 | bytes 1 | tf_op jit(solution)/shard_map/pallas_call | solution.py:193
  26.6 0.1 collective-permute-start.8
  26.7 0.5 collective-permute-start.9
  27.2 4.4 %collective-permute-start.2 = (f32[128,128]{1,0:T(8,128)S(1)}, f32[128,128]{1,0:T(8,128)S(1)}, u32[]{:S(2)}, u32[]{:S(2)}) collective-permute-start(f32[128,128]{1,0:T(8,128)S(1)} %get-tuple-element.62.refs_0_), channel_id=1, source_target_pairs={{0,4},{4,0},{8,12},{12,8},{1,5},{5,1},{9,13},{13,9},{2,6},{6,2},{1... | collective-permute-start | bytes 196616 | tf_op jit(solution)/shard_map/ppermute | solution.py:31
  31.6 2.3 %collective-permute-done.2.refs_1_ = f32[128,128]{1,0:T(8,128)S(1)} collective-permute-done((f32[128,128]{1,0:T(8,128)S(1)}, f32[128,128]{1,0:T(8,128)S(1)}, u32[]{:S(2)}, u32[]{:S(2)}) %collective-permute-start.2) | collective-permute-done | bytes 65568 | tf_op jit(solution)/shard_map/ppermute | solution.py:31
  33.9 1.7 %collective-permute-start.3 = (f32[128,128]{1,0:T(8,128)S(1)}, f32[128,128]{1,0:T(8,128)S(1)}, u32[]{:S(2)}, u32[]{:S(2)}) collective-permute-start(f32[128,128]{1,0:T(8,128)S(1)} %shard_map.51.refs_0_), channel_id=1, source_target_pairs={{0,8},{4,12},{8,0},{12,4},{1,9},{5,13},{9,1},{13,5},{2,10},{6,14},... | collective-permute-start | bytes 196616 | tf_op jit(solution)/shard_map/ppermute | solution.py:31
  35.6 4.0 %collective-permute-done.3.refs_1_ = f32[128,128]{1,0:T(8,128)S(1)} collective-permute-done((f32[128,128]{1,0:T(8,128)S(1)}, f32[128,128]{1,0:T(8,128)S(1)}, u32[]{:S(2)}, u32[]{:S(2)}) %collective-permute-start.3) | collective-permute-done | bytes 65568 | tf_op jit(solution)/shard_map/ppermute | solution.py:31
  39.6 0.1 collective-permute-start.5
  39.7 0.6 collective-permute-start.6
  40.3 1.3 collective-permute-start.7
  41.5 0.0 collective-permute-done.9.refs_7_
  41.5 0.3 collective-permute-start.26
  41.9 0.0 collective-permute-done.5.refs_1_
  41.9 2.7 %collective-permute-done.6.refs_2_ = f32[128,128]{1,0:T(8,128)S(1)} collective-permute-done((f32[128,128]{1,0:T(8,128)S(1)}, f32[128,128]{1,0:T(8,128)S(1)}, u32[]{:S(2)}, u32[]{:S(2)}) %collective-permute-start.6) | collective-permute-done | bytes 65568 | tf_op jit(solution)/shard_map/ppermute | solution.py:31
  44.6 0.5 collective-permute-done.7.refs_3_
  45.1 6.1 %shard_map.53 = (bf16[128,128]{1,0:T(8,128)(2,1)}, bf16[64,512]{1,0:T(8,128)(2,1)S(1)}, bf16[32,4096]{1,0:T(8,128)(2,1)S(1)}, bf16[32,4096]{1,0:T(8,128)(2,1)S(1...) custom-call(f32[128,128]{1,0:T(8,128)S(1)} %shard_map.52.refs_0_, ...), custom_call_target="tpu_custom_call" | custom-call | flops 1 | bytes 1 | tf_op jit(solution)/shard_map/pallas_call | solution.py:316
  51.2 0.7 collective-permute-start.13
  52.0 1.4 collective-permute-start.14
  53.3 5.2 %shard_map.54 = (bf16[32,4096]{1,0:T(8,128)(2,1)S(1)}, bf16[32,4096]{1,0:T(8,128)(2,1)S(1)}, bf16[32,4096]{1,0:T(8,128)(2,1)S(1)}, bf16[32,4096]{1,0:T(8,128)(2,1)S(1)}, f32[8,128]{1,0:T(8,128)S(1)}) custom-call(bf16[64,512]{1,0:T(8,128)(2,1)S(1)} %get-tuple-element.66.turned, bf16[512,256]{1,0:T(8,128)(2,1)S(1)} %get-tuple-element.67.band, ...), custom_call_target="tpu_custom_call" | custom-call | flops 1 | bytes 1 | tf_op jit(solution)/shard_map/pallas_call | solution.py:365
  58.5 0.7 collective-permute-start.11
  59.2 1.3 collective-permute-start.12
  60.6 0.0 collective-permute-done.13.refs_1_
  60.6 5.4 %collective-permute-done.14.refs_3_ = bf16[32,4096]{1,0:T(8,128)(2,1)S(1)} collective-permute-done((bf16[32,4096]{1,0:T(8,128)(2,1)S(1)}, bf16[32,4096]{1,0:T(8,128)(2,1)S(1)}, u32[]{:S(2)}, u32[]{:S(2)}) %collective-permute-start.14) | collective-permute-done | bytes 262176 | tf_op jit(solution)/shard_map/ppermute | solution.py:495
  66.0 0.9 shard_map.55
  66.9 5.2 %shard_map.56 = (bf16[32,4096]{1,0:T(8,128)(2,1)S(1)}, bf16[32,4096]{1,0:T(8,128)(2,1)S(1)}, bf16[32,4096]{1,0:T(8,128)(2,1)S(1)}, bf16[32,4096]{1,0:T(8,128)(2,1)S(1)}, f32[8,128]{1,0:T(8,128)S(1)}) custom-call(bf16[64,512]{1,0:T(8,128)(2,1)S(1)} %get-tuple-element.66.turned, bf16[512,256]{1,0:T(8,128)(2,1)S(1)} %get-tuple-element.67.band, ...), custom_call_target="tpu_custom_call" | custom-call | flops 1 | bytes 1 | tf_op jit(solution)/shard_map/pallas_call | solution.py:365
  72.1 0.8 collective-permute-start.17
  72.8 1.3 collective-permute-start.18
  74.2 3.1 %collective-permute-done.12.refs_3_ = bf16[32,4096]{1,0:T(8,128)(2,1)S(1)} collective-permute-done((bf16[32,4096]{1,0:T(8,128)(2,1)S(1)}, bf16[32,4096]{1,0:T(8,128)(2,1)S(1)}, u32[]{:S(2)}, u32[]{:S(2)}) %collective-permute-start.12) | collective-permute-done | bytes 262176 | tf_op jit(solution)/shard_map/ppermute | solution.py:495
  77.3 0.9 shard_map.57
  78.1 5.2 %shard_map.58 = (bf16[32,4096]{1,0:T(8,128)(2,1)S(1)}, bf16[32,4096]{1,0:T(8,128)(2,1)S(1)}, bf16[32,4096]{1,0:T(8,128)(2,1)S(1)}, bf16[32,4096]{1,0:T(8,128)(2,1)S(1)}, f32[8,128]{1,0:T(8,128)S(1)}) custom-call(bf16[64,512]{1,0:T(8,128)(2,1)S(1)} %get-tuple-element.66.turned, bf16[512,256]{1,0:T(8,128)(2,1)S(1)} %get-tuple-element.67.band, ...), custom_call_target="tpu_custom_call" | custom-call | flops 1 | bytes 1 | tf_op jit(solution)/shard_map/pallas_call | solution.py:365
  83.3 0.8 collective-permute-start.15
  84.1 1.3 collective-permute-start.16
  85.4 3.1 %collective-permute-done.18.refs_3_ = bf16[32,4096]{1,0:T(8,128)(2,1)S(1)} collective-permute-done((bf16[32,4096]{1,0:T(8,128)(2,1)S(1)}, bf16[32,4096]{1,0:T(8,128)(2,1)S(1)}, u32[]{:S(2)}, u32[]{:S(2)}) %collective-permute-start.18) | collective-permute-done | bytes 262176 | tf_op jit(solution)/shard_map/ppermute | solution.py:495
  88.5 0.9 shard_map.59
  89.4 5.2 %shard_map.60 = (bf16[32,4096]{1,0:T(8,128)(2,1)S(1)}, bf16[32,4096]{1,0:T(8,128)(2,1)S(1)}, bf16[32,4096]{1,0:T(8,128)(2,1)S(1)}, bf16[32,4096]{1,0:T(8,128)(2,1)S(1)}, f32[8,128]{1,0:T(8,128)S(1)}) custom-call(bf16[64,512]{1,0:T(8,128)(2,1)S(1)} %get-tuple-element.66.turned, bf16[512,256]{1,0:T(8,128)(2,1)S(1)} %get-tuple-element.67.band, ...), custom_call_target="tpu_custom_call" | custom-call | flops 1 | bytes 1 | tf_op jit(solution)/shard_map/pallas_call | solution.py:365
  94.5 0.8 collective-permute-start.21
  95.3 1.3 collective-permute-start.22
  96.6 3.1 %collective-permute-done.16.refs_3_ = bf16[32,4096]{1,0:T(8,128)(2,1)S(1)} collective-permute-done((bf16[32,4096]{1,0:T(8,128)(2,1)S(1)}, bf16[32,4096]{1,0:T(8,128)(2,1)S(1)}, u32[]{:S(2)}, u32[]{:S(2)}) %collective-permute-start.16) | collective-permute-done | bytes 262176 | tf_op jit(solution)/shard_map/ppermute | solution.py:495
  99.7 0.9 shard_map.61
  100.6 5.2 %shard_map.62 = (bf16[32,4096]{1,0:T(8,128)(2,1)S(1)}, bf16[32,4096]{1,0:T(8,128)(2,1)S(1)}, bf16[32,4096]{1,0:T(8,128)(2,1)S(1)}, bf16[32,4096]{1,0:T(8,128)(2,1)S(1)}, f32[8,128]{1,0:T(8,128)S(1)}) custom-call(bf16[64,512]{1,0:T(8,128)(2,1)S(1)} %get-tuple-element.66.turned, bf16[512,256]{1,0:T(8,128)(2,1)S(1)} %get-tuple-element.67.band, ...), custom_call_target="tpu_custom_call" | custom-call | flops 1 | bytes 1 | tf_op jit(solution)/shard_map/pallas_call | solution.py:365
  105.8 0.8 collective-permute-start.19
  106.5 1.3 collective-permute-start.20
  107.9 3.1 %collective-permute-done.22.refs_3_ = bf16[32,4096]{1,0:T(8,128)(2,1)S(1)} collective-permute-done((bf16[32,4096]{1,0:T(8,128)(2,1)S(1)}, bf16[32,4096]{1,0:T(8,128)(2,1)S(1)}, u32[]{:S(2)}, u32[]{:S(2)}) %collective-permute-start.22) | collective-permute-done | bytes 262176 | tf_op jit(solution)/shard_map/ppermute | solution.py:495
  111.0 0.9 shard_map.63
  111.8 5.2 %shard_map.64 = (bf16[32,4096]{1,0:T(8,128)(2,1)S(1)}, bf16[32,4096]{1,0:T(8,128)(2,1)S(1)}, bf16[32,4096]{1,0:T(8,128)(2,1)S(1)}, bf16[32,4096]{1,0:T(8,128)(2,1)S(1)}, f32[8,128]{1,0:T(8,128)S(1)}) custom-call(bf16[64,512]{1,0:T(8,128)(2,1)S(1)} %get-tuple-element.66.turned, bf16[512,256]{1,0:T(8,128)(2,1)S(1)} %get-tuple-element.67.band, ...), custom_call_target="tpu_custom_call" | custom-call | flops 1 | bytes 1 | tf_op jit(solution)/shard_map/pallas_call | solution.py:365
  117.0 0.8 collective-permute-start.24
  117.8 1.3 collective-permute-start.25
  119.1 3.1 %collective-permute-done.20.refs_3_ = bf16[32,4096]{1,0:T(8,128)(2,1)S(1)} collective-permute-done((bf16[32,4096]{1,0:T(8,128)(2,1)S(1)}, bf16[32,4096]{1,0:T(8,128)(2,1)S(1)}, u32[]{:S(2)}, u32[]{:S(2)}) %collective-permute-start.20) | collective-permute-done | bytes 262176 | tf_op jit(solution)/shard_map/ppermute | solution.py:495
  122.2 0.9 shard_map.65
  123.1 3.2 %shard_map.66 = (bf16[32,4096]{1,0:T(8,128)(2,1)S(1)}, bf16[32,4096]{1,0:T(8,128)(2,1)S(1)}, f32[8,128]{1,0:T(8,128)S(1)}) custom-call(bf16[64,512]{1,0:T(8,128)(2,1)S(1)} %get-tuple-element.66.turned, bf16[512,256]{1,0:T(8,128)(2,1)S(1)} %get-tuple-element.67.band, bf16[128,65536]{1,0:T(8,128)(2,1)} %own_high.1, bf16[128,65536]{1,0:T(8,128)(2,1)} %own_high.1, ...), custom_call_target="tpu_custom_call" | custom-call | flops 1 | bytes 1 | tf_op jit(solution)/shard_map/pallas_call | solution.py:365
  126.2 0.8 collective-permute-start.23
  127.0 6.0 %shard_map.67 = (bf16[32,65536]{1,0:T(8,128)(2,1)}, f32[8,128]{1,0:T(8,128)S(1)}) custom-call(bf16[64,512]{1,0:T(8,128)(2,1)S(1)} %get-tuple-element.66.turned, bf16[512,256]{1,0:T(8,128)(2,1)S(1)} %get-tuple-element.67.band, bf16[128,65536]{1,0:T(8,128)(2,1)} %own_high.1, bf16[128,65536]{1,0:T(8,128)(2,1)} %own_high.1, ...), custom_call_target="tpu_custom_call", output_to_operand_aliasing={{0}: (10, {})} | custom-call | flops 1 | bytes 1 | tf_op jit(solution)/shard_map/pallas_call | solution.py:397
  133.0 0.4 collective-permute-done.25.refs_3_
  133.4 0.9 shard_map.68
  134.3 4.1 %collective-permute-done.23.refs_1_ = bf16[32,4096]{1,0:T(8,128)(2,1)S(1)} collective-permute-done((bf16[32,4096]{1,0:T(8,128)(2,1)S(1)}, bf16[32,4096]{1,0:T(8,128)(2,1)S(1)}, u32[]{:S(2)}, u32[]{:S(2)}) %collective-permute-start.23) | collective-permute-done | bytes 262176 | tf_op jit(solution)/shard_map/ppermute | solution.py:495
  138.4 0.8 shard_map.69
  (13 shorter events, 0.0 us)
Async XLA Ops:
  0.6 52.7 %collective-permute-start.10 = (bf16[128,65536]{1,0:T(8,128)(2,1)}, bf16[128,65536]{1,0:T(8,128)(2,1)}, u32[]{:S(2)}, u32[]{:S(2)}) collective-permute-start(bf16[128,65536]{1,0:T(8,128)(2,1)} %own_high.1), channel_id=1, source_target_pairs={{0,1},{1,0},{2,3},{3,2},{4,5},{5,4},{6,7},{7,6},{8,9},{9,8},{10,11... | collective-permute-start | bytes 50331656 | tf_op jit(solution)/shard_map/ppermute | solution.py:31
  1.9 6.9 %collective-permute-start = (bf16[128,128]{1,0:T(8,128)(2,1)S(1)}, bf16[128,128]{1,0:T(8,128)(2,1)S(1)}, u32[]{:S(2)}, u32[]{:S(2)}) collective-permute-start(bf16[128,128]{1,0:T(8,128)(2,1)S(1)} %get-tuple-element.123), channel_id=1, source_target_pairs={{0,4},{8,12},{4,0},{12,8},{1,5},{9,13},{5,1},{13,9},{2,6},{10,14},... | collective-permute-start | bytes 98312 | tf_op jit(solution)/shard_map/ppermute | solution.py:460
  4.6 4.3 %collective-permute-start.1 = (bf16[128,128]{1,0:T(8,128)(2,1)S(1)}, bf16[128,128]{1,0:T(8,128)(2,1)S(1)}, u32[]{:S(2)}, u32[]{:S(2)}) collective-permute-start(bf16[128,128]{1,0:T(8,128)(2,1)S(1)} %get-tuple-element.122), channel_id=1, source_target_pairs={{4,8},{8,4},{5,9},{9,5},{6,10},{10,6},{7,11},{11,7},{20,24},{24,20... | collective-permute-start | bytes 98312 | tf_op jit(solution)/shard_map/ppermute | solution.py:460
  6.6 33.0 %collective-permute-start.4 = (bf16[128,4352]{1,0:T(8,128)(2,1)S(1)}, bf16[128,4352]{1,0:T(8,128)(2,1)}, u32[]{:S(2)}, u32[]{:S(2)}) collective-permute-start(bf16[128,4352]{1,0:T(8,128)(2,1)S(1)} %slice.11), channel_id=1, source_target_pairs={{0,2},{1,3},{2,0},{3,1},{4,6},{5,7},{6,4},{7,5},{8,10},{9,11},{10,... | collective-permute-start | bytes 3342344 | tf_op jit(solution)/shard_map/ppermute | solution.py:31
  26.6 13.7 %collective-permute-start.8 = (bf16[128,4096]{1,0:T(8,128)(2,1)S(1)}, bf16[128,4096]{1,0:T(8,128)(2,1)S(1)}, u32[]{:S(2)}, u32[]{:S(2)}) collective-permute-start(bf16[128,4096]{1,0:T(8,128)(2,1)S(1)} %get-tuple-element.63.refs_4_), channel_id=1, source_target_pairs={{0,1},{1,0},{2,3},{3,2},{4,5},{5,4},{6,7},{7,6},{8,9},{9,8},{10,11... | collective-permute-start | bytes 3145736 | tf_op jit(solution)/shard_map/ppermute | solution.py:31
  26.7 14.9 %collective-permute-start.9 = (bf16[128,4096]{1,0:T(8,128)(2,1)S(1)}, bf16[128,4096]{1,0:T(8,128)(2,1)S(1)}, u32[]{:S(2)}, u32[]{:S(2)}) collective-permute-start(bf16[128,4096]{1,0:T(8,128)(2,1)S(1)} %get-tuple-element.64.refs_6_), channel_id=1, source_target_pairs={{0,1},{1,0},{2,3},{3,2},{4,5},{5,4},{6,7},{7,6},{8,9},{9,8},{10,11... | collective-permute-start | bytes 3145736 | tf_op jit(solution)/shard_map/ppermute | solution.py:31
  27.2 6.7 %collective-permute-start.2 = (f32[128,128]{1,0:T(8,128)S(1)}, f32[128,128]{1,0:T(8,128)S(1)}, u32[]{:S(2)}, u32[]{:S(2)}) collective-permute-start(f32[128,128]{1,0:T(8,128)S(1)} %get-tuple-element.62.refs_0_), channel_id=1, source_target_pairs={{0,4},{4,0},{8,12},{12,8},{1,5},{5,1},{9,13},{13,9},{2,6},{6,2},{1... | collective-permute-start | bytes 196616 | tf_op jit(solution)/shard_map/ppermute | solution.py:31
  33.9 5.7 %collective-permute-start.3 = (f32[128,128]{1,0:T(8,128)S(1)}, f32[128,128]{1,0:T(8,128)S(1)}, u32[]{:S(2)}, u32[]{:S(2)}) collective-permute-start(f32[128,128]{1,0:T(8,128)S(1)} %shard_map.51.refs_0_), channel_id=1, source_target_pairs={{0,8},{4,12},{8,0},{12,4},{1,9},{5,13},{9,1},{13,5},{2,10},{6,14},... | collective-permute-start | bytes 196616 | tf_op jit(solution)/shard_map/ppermute | solution.py:31
  39.6 2.3 %collective-permute-start.5 = (f32[128,128]{1,0:T(8,128)S(1)}, f32[128,128]{1,0:T(8,128)S(1)}, u32[]{:S(2)}, u32[]{:S(2)}) collective-permute-start(f32[128,128]{1,0:T(8,128)S(1)} %shard_map.52.refs_0_), channel_id=1, source_target_pairs={{0,1},{1,0},{2,3},{3,2},{4,5},{5,4},{6,7},{7,6},{8,9},{9,8},{10,11... | collective-permute-start | bytes 196616 | tf_op jit(solution)/shard_map/ppermute | solution.py:31
  39.7 5.0 %collective-permute-start.6 = (f32[128,128]{1,0:T(8,128)S(1)}, f32[128,128]{1,0:T(8,128)S(1)}, u32[]{:S(2)}, u32[]{:S(2)}) collective-permute-start(f32[128,128]{1,0:T(8,128)S(1)} %shard_map.52.refs_0_), channel_id=1, source_target_pairs={{0,2},{1,3},{2,0},{3,1},{4,6},{5,7},{6,4},{7,5},{8,10},{9,11},{10,... | collective-permute-start | bytes 196616 | tf_op jit(solution)/shard_map/ppermute | solution.py:31
  40.3 4.9 %collective-permute-start.7 = (f32[128,128]{1,0:T(8,128)S(1)}, f32[128,128]{1,0:T(8,128)S(1)}, u32[]{:S(2)}, u32[]{:S(2)}) collective-permute-start(f32[128,128]{1,0:T(8,128)S(1)} %shard_map.52.refs_0_), channel_id=1, source_target_pairs={{0,3},{1,2},{2,1},{3,0},{4,7},{5,6},{6,5},{7,4},{8,11},{9,10},{10,... | collective-permute-start | bytes 196616 | tf_op jit(solution)/shard_map/ppermute | solution.py:31
  41.5 85.5 %collective-permute-start.26 = (bf16[128,4352]{1,0:T(8,128)(2,1)}, bf16[128,4352]{1,0:T(8,128)(2,1)}, u32[]{:S(2)}, u32[]{:S(2)}) collective-permute-start(bf16[128,4352]{1,0:T(8,128)(2,1)} %collective-permute-done.4.refs_2_), channel_id=1, source_target_pairs={{0,1},{1,0},{2,3},{3,2},{4,5},{5,4},{6,7},{7,6},{8,9},{9,8},{10,11... | collective-permute-start | bytes 3342344 | tf_op jit(solution)/shard_map/ppermute | solution.py:31
  51.2 9.4 %collective-permute-start.13 = (bf16[32,4096]{1,0:T(8,128)(2,1)S(1)}, bf16[32,4096]{1,0:T(8,128)(2,1)S(1)}, u32[]{:S(2)}, u32[]{:S(2)}) collective-permute-start(bf16[32,4096]{1,0:T(8,128)(2,1)S(1)} %get-tuple-element.73), channel_id=1, source_target_pairs={{0,2},{1,3},{2,0},{3,1},{4,6},{5,7},{6,4},{7,5},{8,10},{9,11},{10,... | collective-permute-start | bytes 786440 | tf_op jit(solution)/shard_map/ppermute | solution.py:495
  52.0 14.1 %collective-permute-start.14 = (bf16[32,4096]{1,0:T(8,128)(2,1)S(1)}, bf16[32,4096]{1,0:T(8,128)(2,1)S(1)}, u32[]{:S(2)}, u32[]{:S(2)}) collective-permute-start(bf16[32,4096]{1,0:T(8,128)(2,1)S(1)} %get-tuple-element.75), channel_id=1, source_target_pairs={{0,2},{1,3},{2,0},{3,1},{4,6},{5,7},{6,4},{7,5},{8,10},{9,11},{10,... | collective-permute-start | bytes 786440 | tf_op jit(solution)/shard_map/ppermute | solution.py:495
  58.5 15.7 %collective-permute-start.11 = (bf16[32,4096]{1,0:T(8,128)(2,1)S(1)}, bf16[32,4096]{1,0:T(8,128)(2,1)S(1)}, u32[]{:S(2)}, u32[]{:S(2)}) collective-permute-start(bf16[32,4096]{1,0:T(8,128)(2,1)S(1)} %get-tuple-element.69), channel_id=1, source_target_pairs={{0,2},{1,3},{2,0},{3,1},{4,6},{5,7},{6,4},{7,5},{8,10},{9,11},{10,... | collective-permute-start | bytes 786440 | tf_op jit(solution)/shard_map/ppermute | solution.py:495
  59.2 18.0 %collective-permute-start.12 = (bf16[32,4096]{1,0:T(8,128)(2,1)S(1)}, bf16[32,4096]{1,0:T(8,128)(2,1)S(1)}, u32[]{:S(2)}, u32[]{:S(2)}) collective-permute-start(bf16[32,4096]{1,0:T(8,128)(2,1)S(1)} %get-tuple-element.71), channel_id=1, source_target_pairs={{0,2},{1,3},{2,0},{3,1},{4,6},{5,7},{6,4},{7,5},{8,10},{9,11},{10,... | collective-permute-start | bytes 786440 | tf_op jit(solution)/shard_map/ppermute | solution.py:495
  72.1 13.3 %collective-permute-start.17 = (bf16[32,4096]{1,0:T(8,128)(2,1)S(1)}, bf16[32,4096]{1,0:T(8,128)(2,1)S(1)}, u32[]{:S(2)}, u32[]{:S(2)}) collective-permute-start(bf16[32,4096]{1,0:T(8,128)(2,1)S(1)} %get-tuple-element.86), channel_id=1, source_target_pairs={{0,2},{1,3},{2,0},{3,1},{4,6},{5,7},{6,4},{7,5},{8,10},{9,11},{10,... | collective-permute-start | bytes 786440 | tf_op jit(solution)/shard_map/ppermute | solution.py:495
  72.8 15.7 %collective-permute-start.18 = (bf16[32,4096]{1,0:T(8,128)(2,1)S(1)}, bf16[32,4096]{1,0:T(8,128)(2,1)S(1)}, u32[]{:S(2)}, u32[]{:S(2)}) collective-permute-start(bf16[32,4096]{1,0:T(8,128)(2,1)S(1)} %get-tuple-element.88), channel_id=1, source_target_pairs={{0,2},{1,3},{2,0},{3,1},{4,6},{5,7},{6,4},{7,5},{8,10},{9,11},{10,... | collective-permute-start | bytes 786440 | tf_op jit(solution)/shard_map/ppermute | solution.py:495
  83.3 13.3 %collective-permute-start.15 = (bf16[32,4096]{1,0:T(8,128)(2,1)S(1)}, bf16[32,4096]{1,0:T(8,128)(2,1)S(1)}, u32[]{:S(2)}, u32[]{:S(2)}) collective-permute-start(bf16[32,4096]{1,0:T(8,128)(2,1)S(1)} %get-tuple-element.82), channel_id=1, source_target_pairs={{0,2},{1,3},{2,0},{3,1},{4,6},{5,7},{6,4},{7,5},{8,10},{9,11},{10,... | collective-permute-start | bytes 786440 | tf_op jit(solution)/shard_map/ppermute | solution.py:495
  84.1 15.7 %collective-permute-start.16 = (bf16[32,4096]{1,0:T(8,128)(2,1)S(1)}, bf16[32,4096]{1,0:T(8,128)(2,1)S(1)}, u32[]{:S(2)}, u32[]{:S(2)}) collective-permute-start(bf16[32,4096]{1,0:T(8,128)(2,1)S(1)} %get-tuple-element.84), channel_id=1, source_target_pairs={{0,2},{1,3},{2,0},{3,1},{4,6},{5,7},{6,4},{7,5},{8,10},{9,11},{10,... | collective-permute-start | bytes 786440 | tf_op jit(solution)/shard_map/ppermute | solution.py:495
  94.5 13.3 %collective-permute-start.21 = (bf16[32,4096]{1,0:T(8,128)(2,1)S(1)}, bf16[32,4096]{1,0:T(8,128)(2,1)S(1)}, u32[]{:S(2)}, u32[]{:S(2)}) collective-permute-start(bf16[32,4096]{1,0:T(8,128)(2,1)S(1)} %get-tuple-element.100), channel_id=1, source_target_pairs={{0,2},{1,3},{2,0},{3,1},{4,6},{5,7},{6,4},{7,5},{8,10},{9,11},{10,... | collective-permute-start | bytes 786440 | tf_op jit(solution)/shard_map/ppermute | solution.py:495
  95.3 15.7 %collective-permute-start.22 = (bf16[32,4096]{1,0:T(8,128)(2,1)S(1)}, bf16[32,4096]{1,0:T(8,128)(2,1)S(1)}, u32[]{:S(2)}, u32[]{:S(2)}) collective-permute-start(bf16[32,4096]{1,0:T(8,128)(2,1)S(1)} %get-tuple-element.102), channel_id=1, source_target_pairs={{0,2},{1,3},{2,0},{3,1},{4,6},{5,7},{6,4},{7,5},{8,10},{9,11},{10,... | collective-permute-start | bytes 786440 | tf_op jit(solution)/shard_map/ppermute | solution.py:495
  105.8 13.3 %collective-permute-start.19 = (bf16[32,4096]{1,0:T(8,128)(2,1)S(1)}, bf16[32,4096]{1,0:T(8,128)(2,1)S(1)}, u32[]{:S(2)}, u32[]{:S(2)}) collective-permute-start(bf16[32,4096]{1,0:T(8,128)(2,1)S(1)} %get-tuple-element.96), channel_id=1, source_target_pairs={{0,2},{1,3},{2,0},{3,1},{4,6},{5,7},{6,4},{7,5},{8,10},{9,11},{10,... | collective-permute-start | bytes 786440 | tf_op jit(solution)/shard_map/ppermute | solution.py:495
  106.5 15.7 %collective-permute-start.20 = (bf16[32,4096]{1,0:T(8,128)(2,1)S(1)}, bf16[32,4096]{1,0:T(8,128)(2,1)S(1)}, u32[]{:S(2)}, u32[]{:S(2)}) collective-permute-start(bf16[32,4096]{1,0:T(8,128)(2,1)S(1)} %get-tuple-element.98), channel_id=1, source_target_pairs={{0,2},{1,3},{2,0},{3,1},{4,6},{5,7},{6,4},{7,5},{8,10},{9,11},{10,... | collective-permute-start | bytes 786440 | tf_op jit(solution)/shard_map/ppermute | solution.py:495
  117.0 16.0 %collective-permute-start.24 = (bf16[32,4096]{1,0:T(8,128)(2,1)S(1)}, bf16[32,4096]{1,0:T(8,128)(2,1)S(1)}, u32[]{:S(2)}, u32[]{:S(2)}) collective-permute-start(bf16[32,4096]{1,0:T(8,128)(2,1)S(1)} %get-tuple-element.112), channel_id=1, source_target_pairs={{0,2},{1,3},{2,0},{3,1},{4,6},{5,7},{6,4},{7,5},{8,10},{9,11},{10,... | collective-permute-start | bytes 786440 | tf_op jit(solution)/shard_map/ppermute | solution.py:495
  117.8 15.7 %collective-permute-start.25 = (bf16[32,4096]{1,0:T(8,128)(2,1)S(1)}, bf16[32,4096]{1,0:T(8,128)(2,1)S(1)}, u32[]{:S(2)}, u32[]{:S(2)}) collective-permute-start(bf16[32,4096]{1,0:T(8,128)(2,1)S(1)} %get-tuple-element.114), channel_id=1, source_target_pairs={{0,2},{1,3},{2,0},{3,1},{4,6},{5,7},{6,4},{7,5},{8,10},{9,11},{10,... | collective-permute-start | bytes 786440 | tf_op jit(solution)/shard_map/ppermute | solution.py:495
  126.2 12.2 %collective-permute-start.23 = (bf16[32,4096]{1,0:T(8,128)(2,1)S(1)}, bf16[32,4096]{1,0:T(8,128)(2,1)S(1)}, u32[]{:S(2)}, u32[]{:S(2)}) collective-permute-start(bf16[32,4096]{1,0:T(8,128)(2,1)S(1)} %get-tuple-element.110), channel_id=1, source_target_pairs={{0,2},{1,3},{2,0},{3,1},{4,6},{5,7},{6,4},{7,5},{8,10},{9,11},{10,... | collective-permute-start | bytes 786440 | tf_op jit(solution)/shard_map/ppermute | solution.py:495
